TPU v7x, 128 devices: a whole 4x4x4 slice. The times are simulated.
128 devices in a mesh: gy: 16 (over y_lo, z, core), gx: 8 (over x, y_hi).
Axes of the slice: x: 4, y: 4 (y_hi: 2, y_lo: 2; y = y_hi * 2 + y_lo), z: 4, core: 2. Of those that a mesh axis runs over, the one named last changes fastest.
Arguments:
- tokens: bfloat16 [512, 1024, 256], P('gy', 'gx'), may hold values from -40 to 40
- cotangent: bfloat16 [512, 1024, 256], P('gy', 'gx'), may hold values from -6 to 6
- norm1_gain: float32 [256], replicated, may hold values from 0.25 to 1.75
- w_qkv: bfloat16 [256, 768], replicated, may hold values from -0.375 to 0.375
- w_out: bfloat16 [256, 256], replicated, may hold values from -0.375 to 0.375
- pos_bias: float32 [8, 64, 64], replicated, may hold values from -3.5 to 302
- norm2_gain: float32 [256], replicated, may hold values from 0.25 to 1.75
- w_up: bfloat16 [256, 1024], replicated, may hold values from -0.375 to 0.375
- w_down: bfloat16 [1024, 256], replicated, may hold values from -0.1875 to 0.1875
Outputs:
- mixed: bfloat16 [512, 1024, 256], P('gy', 'gx')
- grad_tokens: bfloat16 [512, 1024, 256], P('gy', 'gx')
- grad_qkv: float32 [256, 768], replicated
- grad_out: float32 [256, 256], replicated
All inputs are finite; a program needn't handle non-finite values.
Results may differ from a plain program's by a relative error of at most 0.009.
Values may be sent and summed in bfloat16 or wider, within the bound.
No kernel may reach another device: no remote copies, remote signals or barrier semaphores. Data moves between devices by JAX's collectives and lax.ppermute only.
A program may use at most 192 MiB of HBM per device.

v0:
```python
import math

import jax
import jax.numpy as jnp
from jax import lax
from jax.sharding import PartitionSpec as P

GRID = 8


EPSILON = 1e-05


def normalize(values, gain):
    wide = values.astype(jnp.float32)
    centre = jnp.mean(wide, axis=-1, keepdims=True)
    shifted = wide - centre
    variance = jnp.mean(shifted * shifted, axis=-1, keepdims=True)
    inverse = lax.rsqrt(variance + EPSILON)
    unit = shifted * inverse
    return (unit * gain, unit, inverse)


def geometry(tile_rows, tile_cols, row_devices, column_devices):
    row_part = tile_rows // row_devices
    row_extra = row_devices // GRID
    local_members = GRID // column_devices
    strip_part = tile_cols // local_members // column_devices
    return (row_devices, row_part, row_extra, local_members, column_devices, strip_part)


def outbound(stacked, layout):
    row_devices, row_part, row_extra, local_members, column_devices, strip_part = layout
    return stacked.reshape(
        stacked.shape[0],
        row_devices,
        row_part,
        local_members,
        column_devices,
        strip_part,
        stacked.shape[-1],
    )


def inbound(received, layout):
    row_devices, row_part, row_extra, local_members, column_devices, strip_part = layout
    arranged = received.reshape(
        received.shape[0],
        GRID,
        row_extra,
        row_part,
        local_members,
        column_devices,
        strip_part,
        received.shape[-1],
    )
    arranged = arranged.transpose(0, 2, 3, 6, 1, 5, 4, 7)
    return arranged.reshape(received.shape[0], -1, received.shape[-1])


def homeward(flat, layout):
    row_devices, row_part, row_extra, local_members, column_devices, strip_part = layout
    arranged = flat.reshape(
        flat.shape[0],
        row_extra,
        row_part,
        strip_part,
        GRID,
        column_devices,
        local_members,
        flat.shape[-1],
    )
    arranged = arranged.transpose(0, 4, 1, 2, 6, 5, 3, 7)
    return arranged.reshape(
        flat.shape[0],
        row_devices,
        row_part,
        local_members,
        column_devices,
        strip_part,
        flat.shape[-1],
    )


def feed_forward(attended, norm2_gain, w_up, w_down):
    normed_wide, unit, inverse = normalize(attended, norm2_gain)
    normed2 = normed_wide.astype(jnp.bfloat16)
    hidden = jax.nn.gelu(jnp.dot(normed2, w_up, preferred_element_type=jnp.float32)).astype(
        jnp.bfloat16
    )
    return (
        attended.astype(jnp.float32) + jnp.dot(hidden, w_down, preferred_element_type=jnp.float32)
    ).astype(jnp.bfloat16)


def attention_forward(x_rows, norm1_gain, w_qkv, w_out, pos_bias):
    channels = x_rows.shape[-1]
    heads = pos_bias.shape[0]
    members = pos_bias.shape[1]
    width = channels // heads
    groups = x_rows.shape[0] // members
    scale_factor = 1.0 / math.sqrt(width)
    normed_wide, unit, inverse = normalize(x_rows, norm1_gain)
    normed = normed_wide.astype(jnp.bfloat16)
    qkv = jnp.dot(normed, w_qkv, preferred_element_type=jnp.float32).astype(jnp.bfloat16)
    split_qkv = qkv.reshape(groups, members, 3, heads, width)
    query = split_qkv[:, :, 0]
    keys = split_qkv[:, :, 1]
    values = split_qkv[:, :, 2]
    scores = (
        jnp.einsum("nmhd,nkhd->nhmk", query, keys, preferred_element_type=jnp.float32)
        * scale_factor
        + pos_bias[None]
    )
    soft = jax.nn.softmax(scores, axis=-1)
    soft_low = soft.astype(jnp.bfloat16)
    context = jnp.einsum("nhmk,nkhd->nmhd", soft_low, values, preferred_element_type=jnp.float32)
    context = context.astype(jnp.bfloat16).reshape(groups * members, channels)
    attended = (
        x_rows.astype(jnp.float32) + jnp.dot(context, w_out, preferred_element_type=jnp.float32)
    ).astype(jnp.bfloat16)
    saved = (normed, unit, inverse, query, keys, values, soft, soft_low, context)
    return (attended, saved)


def attention_backward(saved, g_rows, norm1_gain, w_qkv, w_out):
    normed, unit, inverse, query, keys, values, soft, soft_low, context = saved
    groups, members, heads, width = query.shape
    channels = heads * width
    scale_factor = 1.0 / math.sqrt(width)
    d_context = jnp.dot(g_rows, w_out.T, preferred_element_type=jnp.float32).astype(jnp.bfloat16)
    d_wout = lax.dot_general(
        context, g_rows, (((0,), (0,)), ((), ())), preferred_element_type=jnp.float32
    )
    d_ctx = d_context.reshape(groups, members, heads, width)
    d_soft = jnp.einsum("nmhd,nkhd->nhmk", d_ctx, values, preferred_element_type=jnp.float32)
    d_scores = soft * (d_soft - jnp.sum(soft * d_soft, axis=-1, keepdims=True))
    d_scaled = (d_scores * scale_factor).astype(jnp.bfloat16)
    d_query = jnp.einsum("nhmk,nkhd->nmhd", d_scaled, keys, preferred_element_type=jnp.float32)
    d_keys = jnp.einsum("nhmk,nmhd->nkhd", d_scaled, query, preferred_element_type=jnp.float32)
    d_values = jnp.einsum("nhmk,nmhd->nkhd", soft_low, d_ctx, preferred_element_type=jnp.float32)
    d_qkv = (
        jnp.stack([d_query, d_keys, d_values], axis=2)
        .astype(jnp.bfloat16)
        .reshape(groups * members, 3 * channels)
    )
    d_wqkv = lax.dot_general(
        normed, d_qkv, (((0,), (0,)), ((), ())), preferred_element_type=jnp.float32
    )
    d_normed = jnp.dot(d_qkv, w_qkv.T, preferred_element_type=jnp.float32)
    d_unit = d_normed * norm1_gain
    d_x = inverse * (
        d_unit
        - jnp.mean(d_unit, axis=-1, keepdims=True)
        - unit * jnp.mean(d_unit * unit, axis=-1, keepdims=True)
    )
    grad_rows = (g_rows.astype(jnp.float32) + d_x).astype(jnp.bfloat16)
    return (grad_rows, d_wqkv, d_wout)


def local(tokens, cotangent, norm1_gain, w_qkv, w_out, pos_bias, norm2_gain, w_up, w_down):
    tile_rows, tile_cols, channels = tokens.shape
    row_devices = lax.axis_size("gy")
    column_devices = lax.axis_size("gx")
    layout = geometry(tile_rows, tile_cols, row_devices, column_devices)
    factor = 1.0 / math.sqrt(tile_rows * tile_cols * row_devices * column_devices)
    sent = lax.all_to_all(
        lax.all_to_all(
            outbound(jnp.stack([tokens, cotangent]), layout),
            "gy",
            split_axis=1,
            concat_axis=1,
            tiled=True,
        ),
        "gx",
        split_axis=4,
        concat_axis=4,
        tiled=True,
    )
    grouped = inbound(sent, layout)
    x_rows = grouped[0]
    g_rows = grouped[1]
    attended, saved = attention_forward(x_rows, norm1_gain, w_qkv, w_out, pos_bias)
    grad_rows, d_wqkv, d_wout = attention_backward(saved, g_rows, norm1_gain, w_qkv, w_out)
    mixed_rows = feed_forward(attended, norm2_gain, w_up, w_down)
    returned = lax.all_to_all(
        lax.all_to_all(
            homeward(jnp.stack([mixed_rows, grad_rows]), layout),
            "gy",
            split_axis=1,
            concat_axis=1,
            tiled=True,
        ),
        "gx",
        split_axis=4,
        concat_axis=4,
        tiled=True,
    )
    tiles = returned.reshape(2, tile_rows, tile_cols, channels)
    mixed = tiles[0]
    grad_tokens = tiles[1]
    totals = lax.psum((d_wqkv, d_wout), ("gy", "gx"))
    return (mixed, grad_tokens, totals[0] * factor, totals[1] * factor)


def solution(mesh):
    placed = (P("gy", "gx", None), P("gy", "gx", None), P(), P(), P(), P(), P(), P(), P())
    return jax.shard_map(
        local,
        mesh=mesh,
        in_specs=placed,
        out_specs=(P("gy", "gx", None), P("gy", "gx", None), P(), P()),
        check_vma=False,
    )
```

profile of v0, /device:TPU:0, one launch (start us, length us, event | category | flops | bytes accessed | tf_op | source)
XLA Modules:
  0.0 695.5 jit_solution(8668510211476164699)
XLA Ops:
  7.2 0.0 copy-start
  7.2 2.7 pad_maximum_fusion
  9.9 56.5 %all_to_all.20 = bf16[2,16,2,1,8,16,256]{6,5,4,2,0,3,1:T(8,128)(2,1)S(1)} all-to-all(bf16[2,16,2,1,8,16,256]{6,5,4,2,0,3,1:T(8,128)(2,1)S(1)} %pad_maximum_fusion), channel_id=1, replica_groups=mesh['gy'=16,'gx'=8] {'gy'}, dimensions={1} | all-to-all | bytes 8388608 | tf_op jit(solution)/shard_map/all_to_all | solution.py:168
  66.4 2.6 copy.89
  69.0 6.8 all-to-all-start.1
  75.8 0.1 copy.98
  75.9 59.0 %all-to-all-done.1 = bf16[2,16,2,1,8,16,256]{6,5,2,1,0,3,4:T(8,128)(2,1)} async-done(((bf16[2,16,2,1,8,16,256]{6,5,2,1,0,3,4:T(8,128)(2,1)}), bf16[2,16,2,1,8,16,256]{6,5,2,1,0,3,4:T(8,128)(2,1)}, u32[]{:S(2)}, u32[]{:S(2)}) %all-to-all-start.1) | async-done | bytes 4194336 | tf_op jit(solution)/shard_map/all_to_all | solution.py:167
  134.9 2.8 copy.90
  137.7 0.6 convert_reduce_fusion.1
  138.3 2.7 slice_convert_fusion
  141.0 1.4 multiply_reduce_fusion.2
  142.4 0.1 copy.92
  142.6 0.8 copy.93
  143.4 1.1 rsqrt.21
  144.5 6.6 copy.91
  151.1 0.1 div.29
  151.3 2.9 multiply_convert_fusion.2
  154.2 4.5 convolution_convert_fusion
  158.7 8.7 %copy.94 = bf16[4096,768]{0,1:T(8,128)(2,1)} copy(bf16[4096,768]{1,0:T(8,128)(2,1)} %convolution_convert_fusion) | data formatting | bytes 12582912 | tf_op jit(solution)/shard_map/convert_element_type | solution.py:105
  167.4 18.0 %reshape.135 = bf16[64,64,3,8,32]{1,0,4,3,2:T(8,128)(2,1)} reshape(bf16[4096,768]{0,1:T(8,128)(2,1)} %copy.94) | data formatting | bytes 12582912 | tf_op jit(solution)/shard_map/reshape | solution.py:106
  185.4 9.3 %fusion.77 = (bf16[64,64,1,8,32]{1,0,4,3,2:T(8,128)(2,1)}, bf16[64,64,1,8,32]{1,0,4,3,2:T(8,128)(2,1)}, bf16[64,64,1,8,32]{1,0,4,3,2:T(8,128)(2,1)}) fusion(bf16[64,64,3,8,32]{1,0,4,3,2:T(8,128)(2,1)} %reshape.135), kind=kLoop, calls=%fused_computation.86 | loop fusion | bytes 12582912 | tf_op jit(solution)/shard_map/slice | solution.py:109
  194.7 0.8 copy.101
  195.5 1.3 copy-done.3
  196.8 0.7 convolution_convert_fusion.1
  197.6 2.9 copy.102
  200.4 7.0 %reshape.137 = bf16[64,64,8,32]{1,0,3,2:T(8,128)(2,1)} reshape(bf16[4096,256]{0,1:T(8,128)(2,1)} %copy.102) | data formatting | bytes 4194304 | tf_op jit(solution)/shard_map/reshape | solution.py:135
  207.5 20.4 %fusion.43 = f32[64,8,64,64]{2,3,1,0:T(8,128)} fusion(bf16[64,64,1,8,32]{1,0,4,3,2:T(8,128)(2,1)} %get-tuple-element.9, bf16[64,64,1,8,32]{1,0,4,3,2:T(8,128)(2,1)} %get-tuple-element.10), kind=kOutput, calls=%fused_computation.57 | convolution fusion | flops 134217728 | bytes 12582912 | tf_op jit(solution)/shard_map/nmhd,nkhd->nhmk/dot_general | solution.py:111
  227.9 17.9 %fusion.79 = (f32[64,8,64]{2,1,0:T(8,128)S(1)}, f32[64,8,64,64]{2,3,1,0:T(8,128)}) fusion(f32[64,8,64,64]{2,3,1,0:T(8,128)} %fusion.43, f32[8,64,64]{1,2,0:T(8,128)S(1)} %copy.98), kind=kOutput, calls=%fused_computation.88 | output fusion | flops 12582975 | bytes 17039360 | tf_op jit(solution)/shard_map/sub | solution.py:115
  245.7 20.4 %fusion.42 = f32[64,8,64,64]{2,3,1,0:T(8,128)} fusion(bf16[64,64,1,8,32]{1,0,4,3,2:T(8,128)(2,1)} %get-tuple-element.8, bf16[64,64,8,32]{1,0,3,2:T(8,128)(2,1)} %reshape.137), kind=kOutput, calls=%fused_computation.56 | convolution fusion | flops 134217728 | bytes 12582912 | tf_op jit(solution)/shard_map/nmhd,nkhd->nhmk/dot_general | solution.py:136
  266.1 31.2 %fusion.51 = bf16[64,64,1,8,32]{1,4,3,0,2:T(8,128)(2,1)} fusion(f32[64,8,64,64]{2,3,1,0:T(8,128)} %fusion.42, bf16[64,64,1,8,32]{1,0,4,3,2:T(8,128)(2,1)} %get-tuple-element.10, f32[64,8,64,64]{2,3,1,0:T(8,128)} %get-tuple-element.16, f32[64,8,64]{2,1,0:T(8,128)S(1)} %get-tuple-element.15), kind=kOutput, calls=%fused_computation.61 | convolution fusion | flops 148930624 | bytes 21102592 | tf_op jit(solution)/shard_map/nhmk,nkhd->nmhd/dot_general | solution.py:139
  297.3 28.8 %fusion.54 = bf16[64,64,1,8,32]{1,4,3,0,2:T(8,128)(2,1)} fusion(f32[64,8,64,64]{2,3,1,0:T(8,128)} %fusion.42, bf16[64,64,1,8,32]{1,0,4,3,2:T(8,128)(2,1)} %get-tuple-element.9, f32[64,8,64,64]{2,3,1,0:T(8,128)} %get-tuple-element.16, f32[64,8,64]{2,1,0:T(8,128)S(1)} %get-tuple-element.15), kind=kOutput, calls=%fused_computation.62 | convolution fusion | flops 148930624 | bytes 21102592 | tf_op jit(solution)/shard_map/nhmk,nmhd->nkhd/dot_general | solution.py:140
  326.1 11.1 %fusion.46 = bf16[64,64,1,8,32]{1,4,3,0,2:T(8,128)(2,1)} fusion(bf16[64,64,8,32]{1,0,3,2:T(8,128)(2,1)} %reshape.137, f32[64,8,64,64]{2,3,1,0:T(8,128)} %get-tuple-element.16, f32[64,8,64]{2,1,0:T(8,128)S(1)} %get-tuple-element.15), kind=kOutput, calls=%fused_computation.60 | convolution fusion | flops 138412032 | bytes 12713984 | tf_op jit(solution)/shard_map/nhmk,nmhd->nkhd/dot_general | solution.py:141
  337.2 18.0 %convert_bitcast_fusion = bf16[64,64,8,32]{1,3,2,0:T(8,128)(2,1)} fusion(bf16[64,64,1,8,32]{1,0,4,3,2:T(8,128)(2,1)} %get-tuple-element.8, f32[64,8,64,64]{2,3,1,0:T(8,128)} %get-tuple-element.16, f32[64,8,64]{2,1,0:T(8,128)S(1)} %get-tuple-element.15), kind=kOutput, calls=%fused_computation.49 | convolution fusion | flops 139460608 | bytes 12713984 | tf_op jit(solution)/shard_map/nhmk,nkhd->nmhd/dot_general | solution.py:117
  355.2 7.4 %maximum_convert_fusion = bf16[64,64,3,8,32]{1,4,3,0,2:T(8,128)(2,1)S(1)} fusion(bf16[64,64,1,8,32]{1,4,3,0,2:T(8,128)(2,1)} %fusion.46, bf16[64,64,1,8,32]{1,4,3,0,2:T(8,128)(2,1)} %fusion.54, bf16[64,64,1,8,32]{1,4,3,0,2:T(8,128)(2,1)} %fusion.51), kind=kLoop, calls=%fused_computation.2 | loop fusion | flops 6291456 | bytes 12582912 | tf_op jit(solution)/shard_map/convert_element_type | solution.py:144
  362.6 9.3 %copy.108 = bf16[64,64,3,8,32]{1,0,4,3,2:T(8,128)(2,1)} copy(bf16[64,64,3,8,32]{1,4,3,0,2:T(8,128)(2,1)S(1)} %maximum_convert_fusion) | data formatting | bytes 12582912 | tf_op jit(solution)/shard_map/convert_element_type | solution.py:144
  371.9 17.2 %convert_element_type.91 = bf16[4096,768]{0,1:T(8,128)(2,1)} reshape(bf16[64,64,3,8,32]{1,0,4,3,2:T(8,128)(2,1)} %copy.108) | data formatting | bytes 12582912 | tf_op jit(solution)/shard_map/convert_element_type | solution.py:144
  389.1 6.8 copy.100
  395.9 5.7 reshape.136
  401.6 4.3 convert_reduce_fusion
  406.0 1.3 copy-done.7
  407.3 1.3 fusion.34
  408.6 9.1 %fusion.27 = bf16[4096,256]{1,0:T(8,128)(2,1)S(1)} fusion(bf16[1024,256]{1,0:T(8,128)(2,1)S(1)} %copy-done, bf16[4096,256]{1,0:T(8,128)(2,1)} %copy-done.7, bf16[256,1024]{1,0:T(8,128)(2,1)} %param.16, f32[256]{0:T(256)S(1)} %copy-done.22, f32[4096]{0:T(1024)S(1)} %add_rsqrt_fusion.1, f32[4096]{0:T(1024)S(1)} %broadcast_multiply_fusion.5), kind=kOutput, calls=%fused_computation.32 | convolution fusion | flops 4341104640 | bytes 5276672 | tf_op jit(solution)/shard_map/dot_general | solution.py:92
  417.7 1.7 copy.109
  419.5 0.4 copy-done.1
  419.9 6.9 fusion.76
  426.9 3.3 add_convert_fusion
  430.2 1.7 copy.110
  431.9 0.4 pad_maximum_fusion.1
  432.3 0.5 copy.111
  432.8 53.3 %all_to_all.21 = bf16[2,16,2,1,8,16,256]{6,5,4,2,0,3,1:T(8,128)(2,1)S(1)} all-to-all(bf16[2,16,2,1,8,16,256]{6,5,4,2,0,3,1:T(8,128)(2,1)S(1)} %copy.111), channel_id=1, replica_groups=mesh['gy'=16,'gx'=8] {'gy'}, dimensions={1} | all-to-all | bytes 8388608 | tf_op jit(solution)/shard_map/all_to_all | solution.py:187
  486.1 2.6 copy.112
  488.8 5.6 all-to-all-start.3
  494.3 0.0 all-reduce.3.cloned.1.call-start
  494.4 2.6 multiply_convert_fusion.1
  497.0 0.8 copy.115
  497.8 1.5 fusion.81
  499.3 5.6 fusion.80
  504.9 0.0 all-reduce.3.cloned.1.call-update
  505.0 173.7 %all-reduce.3.cloned.1.call-done = (f32[256,768]{1,0:T(8,128)}, f32[256,256]{1,0:T(8,128)}) async-done(((f32[256,768]{1,0:T(8,128)}, f32[256,256]{1,0:T(8,128)}), (f32[256,768]{1,0:T(8,128)}, f32[256,256]{1,0:T(8,128)})) %all-reduce.3.cloned.1.call-update) | async-done | bytes 1048592 | tf_op jit(solution)/shard_map/psum | solution.py:202
  678.7 1.7 broadcast_multiply_fusion.1
  680.3 2.1 broadcast_multiply_fusion
  682.4 2.7 fusion.78
  685.1 1.6 copy.123
  686.7 1.6 copy.124
  (48 shorter events, 0.2 us)
Async XLA Ops:
  7.2 401.4 %copy-start = (bf16[1024,256]{1,0:T(8,128)(2,1)S(1)}, bf16[1024,256]{1,0:T(8,128)(2,1)}, u32[]{:S(2)}) copy-start(bf16[1024,256]{1,0:T(8,128)(2,1)} %param.17) | copy-start | bytes 1572868
  69.0 6.8 copy-start.15
  69.0 65.9 %all-to-all-start.1 = ((bf16[2,16,2,1,8,16,256]{6,5,2,1,0,3,4:T(8,128)(2,1)}), bf16[2,16,2,1,8,16,256]{6,5,2,1,0,3,4:T(8,128)(2,1)}, u32[]{:S(2)}, u32[]{:S(2)}) async-start(bf16[2,16,2,1,8,16,256]{6,5,2,1,0,3,4:T(8,128)(2,1)} %copy.89), calls=%async_computation.1 | async-start | bytes 8388608 | tf_op jit(solution)/shard_map/all_to_all | solution.py:167
  137.7 3.3 copy-start.2
  141.0 10.1 %copy-start.8 = (f32[2,2,16,8,8]{2,4,1,0,3:T(8,128)}, f32[2,2,16,8,8]{2,4,1,0,3:T(8,128)S(1)}, u32[]{:S(2)}) copy-start(f32[2,2,16,8,8]{2,4,1,0,3:T(8,128)S(1)} %broadcast_multiply_fusion.2) | copy-start | bytes 49156
  142.6 8.6 %copy-start.10 = (f32[2,2,16,8,8]{2,4,1,0,3:T(8,128)}, f32[2,2,16,8,8]{2,4,1,0,3:T(8,128)S(1)}, u32[]{:S(2)}) copy-start(f32[2,2,16,8,8]{2,4,1,0,3:T(8,128)S(1)} %add_rsqrt_fusion) | copy-start | bytes 49156
  144.5 6.8 copy-start.16
  144.5 6.8 copy-start.20
  151.3 7.4 %copy-start.18 = (f32[4096]{0:T(1024)}, f32[4096]{0:T(1024)S(1)}, u32[]{:S(2)}) copy-start(f32[4096]{0:T(1024)S(1)} %div.29) | copy-start | bytes 49156
  151.3 2.9 copy-start.13
  194.7 2.1 copy-start.12
  195.5 1.3 copy-start.3
  401.6 4.3 copy-start.5
  401.6 7.0 %copy-start.22 = (f32[256]{0:T(256)S(1)}, f32[256]{0:T(256)}, u32[]{:S(2)}) copy-start(f32[256]{0:T(256)} %param.15) | copy-start | bytes 3076
  405.9 1.3 copy-start.7
  408.6 10.9 %copy-start.14 = (bf16[256,768]{1,0:T(8,128)(2,1)S(1)}, bf16[256,768]{1,0:T(8,128)(2,1)}, u32[]{:S(2)}) copy-start(bf16[256,768]{1,0:T(8,128)(2,1)} %param.12) | copy-start | bytes 1179652
  408.6 10.9 %copy-start.17 = (f32[4096]{0:T(1024)S(1)}, f32[4096]{0:T(1024)}, u32[]{:S(2)}) copy-start(f32[4096]{0:T(1024)} %copy-done.16) | copy-start | bytes 49156
  408.6 10.9 %copy-start.19 = (f32[4096]{0:T(1024)S(1)}, f32[4096]{0:T(1024)}, u32[]{:S(2)}) copy-start(f32[4096]{0:T(1024)} %copy-done.18) | copy-start | bytes 49156
  417.7 2.2 copy-start.1
  417.7 2.2 copy-start.21
  419.9 7.0 %copy-start.4 = (bf16[1,2,2,16,8,8,1,256]{7,5,4,3,2,1,6,0:T(8,128)(2,1)S(1)}, bf16[1,2,2,16,8,8,1,256]{7,5,4,3,2,1,6,0:T(8,128)(2,1)}, u32[]{:S(2)}) copy-start(bf16[1,2,2,16,8,8,1,256]{7,5,4,3,2,1,6,0:T(8,128)(2,1)} %copy-done.3) | copy-start | bytes 6291460
  488.7 5.6 copy-start.9
  488.7 5.6 copy-start.11
  488.8 193.7 %all-to-all-start.3 = ((bf16[2,16,2,1,8,16,256]{6,5,2,1,0,3,4:T(8,128)(2,1)}), bf16[2,16,2,1,8,16,256]{6,5,2,1,0,3,4:T(8,128)(2,1)}, u32[]{:S(2)}, u32[]{:S(2)}) async-start(bf16[2,16,2,1,8,16,256]{6,5,2,1,0,3,4:T(8,128)(2,1)} %copy.112), calls=%async_computation.3 | async-start | bytes 8388608 | tf_op jit(solution)/shard_map/all_to_all | solution.py:186
  494.3 184.3 %all-reduce.3.cloned.1.call-start = ((), (), s32[]{:S(2)}) async-start(), calls=%async_computation.4 | async-start | bytes 2097152 | tf_op jit(solution)/shard_map/psum | solution.py:202
  494.4 3.4 copy-start.6
Sparse Core Ops, SparseCore 0:
  505.1 173.5 all-reduce.2
where the time goes:
time: 708 us; the launch traced here: 695 us
  waiting for transfers between devices  233 us (33%)
  matrix products  162 us (23%)
  local copies, waits for them, and re-layouts  116 us (16%)
  blocking collectives  110 us (16%)
  other arithmetic  47 us (7%)
  between operations  14.9 us (2%)
  starting transfers between devices  12.4 us (2%)
    psum x1, waiting for transfers between devices, local(): totals = lax.psum((d_wqkv, d_wout), ('gy', 'gx'))  174 us
    all_to_all x1, waiting for transfers between devices, local(): lax.all_to_all(lax.all_to_all(outbound(jnp.stack([tokens, cotangent]), la...  59 us
    all_to_all x1, blocking collectives, local(): lax.all_to_all(outbound(jnp.stack([tokens, cotangent]), layout), 'gy', sp...  56.5 us
    all_to_all x1, blocking collectives, local(): lax.all_to_all(homeward(jnp.stack([mixed_rows, grad_rows]), layout), 'gy'...  53.3 us
    dot_general x1, matrix products, attention_backward(): jnp.einsum('nhmk,nkhd->nmhd', d_scaled, keys, preferred_element_type=jnp....  31.2 us
    dot_general x1, matrix products, attention_backward(): jnp.einsum('nhmk,nmhd->nkhd', d_scaled, query, preferred_element_type=jnp...  28.8 us
    convert_element_type x2, local copies, waits for them, and re-layouts, attention_backward(): d_qkv = jnp.stack([d_query, d_keys, d_values], axis=2).astype(jnp.bfloat1...  26.5 us
    dot_general x1, matrix products, attention_forward(): jnp.einsum('nmhd,nkhd->nhmk', query, keys, preferred_element_type=jnp.flo...  20.4 us
  transfers between devices with their start and end apart: 3, of which 2 were waited for; matrix products, arithmetic and copies ran while one was open for 2% of the time, Pallas kernels for 0%

commit v1 on v0

v1 whole, which is shorter than its diff:
```python
import functools
import math

import jax
import jax.numpy as jnp
from jax import lax
from jax.experimental import pallas as pl
from jax.experimental.pallas import tpu as pltpu
from jax.sharding import PartitionSpec as P

GRID = 8
MEMBERS = GRID * GRID
EPSILON = 1e-05
LOG2E = math.log2(math.e)
AXES = ("gy", "gx")
LANES = 128
BLOCK = 16
BATCH = 4


def dot(a, b, contract=((1,), (0,))):
    return lax.dot_general(a, b, (contract, ((), ())), preferred_element_type=jnp.float32)


def normalize(wide, gain):
    centre = jnp.mean(wide, axis=-1, keepdims=True)
    shifted = wide - centre
    variance = jnp.mean(shifted * shifted, axis=-1, keepdims=True)
    inverse = lax.rsqrt(variance + EPSILON)
    unit = shifted * inverse
    return unit * gain, unit, inverse


def gelu(x):
    inner = x * (0.7978845608028654 + 0.035677408136300125 * (x * x))
    half = 0.5 * x
    return half + half * jnp.tanh(inner)


def pick_heads(full, lane_head, per):
    out = full[(per - 1) * MEMBERS : per * MEMBERS]
    for h in range(per - 2, -1, -1):
        out = jnp.where(lane_head == h, full[h * MEMBERS : (h + 1) * MEMBERS], out)
    return out


def kernel(
    width,
    data_ref,
    gain1_ref,
    wqkv_ref,
    wout_ref,
    bias_ref,
    gain2_ref,
    wup_ref,
    wdown_ref,
    mask_ref,
    out_ref,
    dqkv_acc_ref,
    dout_acc_ref,
    xs_ref,
    gs_ref,
    mixed_ref,
    grad_ref,
):
    channels = wout_ref.shape[0]
    halves = channels // LANES
    per = LANES // width
    tokens = MEMBERS * BLOCK
    scale = 1.0 / math.sqrt(width)

    @pl.when((pl.program_id(0) == 0) & (pl.program_id(1) == 0))
    def _():
        dqkv_acc_ref[...] = jnp.zeros_like(dqkv_acc_ref)
        dout_acc_ref[...] = jnp.zeros_like(dout_acc_ref)

    for j in range(halves):
        lanes = slice(j * LANES, (j + 1) * LANES)
        xs_ref[j] = data_ref[:, 0, :, 0, :, lanes].reshape(tokens, LANES).astype(jnp.float32)
        gs_ref[j] = data_ref[:, 0, :, 1, :, lanes].reshape(tokens, LANES).astype(jnp.float32)

    lane_head = lax.broadcasted_iota(jnp.int32, (MEMBERS, LANES), 1) // width

    def grouped(ref, rows):
        return jnp.concatenate(
            [jnp.concatenate([ref[j, r, :] for j in range(halves)], axis=1) for r in rows], axis=0
        )

    def step(i, carry):
        rows = [pl.ds(i * BATCH + g, MEMBERS, stride=BLOCK) for g in range(BATCH)]
        x = grouped(xs_ref, rows)
        cot = grouped(gs_ref, rows)
        normed_wide, unit, inverse = normalize(x, gain1_ref[...])
        normed = normed_wide.astype(jnp.bfloat16)
        cot_low = cot.astype(jnp.bfloat16)
        qkv = dot(normed, wqkv_ref[...]).astype(jnp.bfloat16)
        d_context = dot(cot_low, wout_ref[...], ((1,), (1,))).astype(jnp.bfloat16)
        mask = mask_ref[...]
        contexts, d_qkvs = [], []
        for g in range(BATCH):
            part = slice(g * MEMBERS, (g + 1) * MEMBERS)
            ctx_parts, dq_parts, dk_parts, dv_parts = [], [], [], []
            for j in range(halves):
                at = j * LANES
                q = qkv[part, at : at + LANES]
                k = qkv[part, channels + at : channels + at + LANES]
                v = qkv[part, 2 * channels + at : 2 * channels + at + LANES]
                dc = d_context[part, at : at + LANES]
                q_heads = jnp.concatenate([q] * per, axis=0) * mask
                dc_heads = jnp.concatenate([dc] * per, axis=0) * mask
                scores = dot(k, q_heads, ((1,), (1,))) * (scale * LOG2E) + bias_ref[j]
                e = jnp.exp2(scores - jnp.max(scores, axis=0, keepdims=True))
                probs = e * (1.0 / jnp.sum(e, axis=0, keepdims=True))
                probs_low = probs.astype(jnp.bfloat16)
                d_probs = dot(v, dc_heads, ((1,), (1,)))
                delta = jnp.sum(probs * d_probs, axis=0, keepdims=True)
                d_scaled = (probs * (d_probs - delta) * scale).astype(jnp.bfloat16)
                dv_parts.append(dot(probs_low, dc_heads))
                dk_parts.append(dot(d_scaled, q_heads))
                ctx_parts.append(pick_heads(dot(probs_low, v, ((0,), (0,))), lane_head, per))
                dq_parts.append(pick_heads(dot(d_scaled, k, ((0,), (0,))), lane_head, per))
            contexts.append(jnp.concatenate(ctx_parts, axis=1))
            d_qkvs.append(jnp.concatenate(dq_parts + dk_parts + dv_parts, axis=1))
        context = jnp.concatenate(contexts, axis=0).astype(jnp.bfloat16)
        d_qkv = jnp.concatenate(d_qkvs, axis=0).astype(jnp.bfloat16)
        dout_acc_ref[...] += dot(context, cot_low, ((0,), (0,)))
        dqkv_acc_ref[...] += dot(normed, d_qkv, ((0,), (0,)))
        d_unit = dot(d_qkv, wqkv_ref[...], ((1,), (1,))) * gain1_ref[...]
        grad = cot + inverse * (
            d_unit
            - jnp.mean(d_unit, axis=-1, keepdims=True)
            - unit * jnp.mean(d_unit * unit, axis=-1, keepdims=True)
        )
        attended = (x + dot(context, wout_ref[...])).astype(jnp.bfloat16).astype(jnp.float32)
        normed2 = normalize(attended, gain2_ref[...])[0].astype(jnp.bfloat16)
        hidden = gelu(dot(normed2, wup_ref[...])).astype(jnp.bfloat16)
        mixed = attended + dot(hidden, wdown_ref[...])
        for g in range(BATCH):
            part = slice(g * MEMBERS, (g + 1) * MEMBERS)
            for j in range(halves):
                lanes = slice(j * LANES, (j + 1) * LANES)
                mixed_ref[j, rows[g], :] = mixed[part, lanes]
                grad_ref[j, rows[g], :] = grad[part, lanes]
        return carry

    lax.fori_loop(0, BLOCK // BATCH, step, 0)
    shape = (GRID, GRID, BLOCK, LANES)
    for j in range(halves):
        lanes = slice(j * LANES, (j + 1) * LANES)
        out_ref[:, 0, :, 0, :, lanes] = mixed_ref[j].reshape(shape).astype(jnp.bfloat16)
        out_ref[:, 0, :, 1, :, lanes] = grad_ref[j].reshape(shape).astype(jnp.bfloat16)


def fused(data, gain1, wqkv, wout, bias, gain2, wup, wdown, mask, width):
    _, classes, _, _, positions, channels = data.shape
    halves = channels // LANES
    tokens = MEMBERS * BLOCK
    whole = lambda a: pl.BlockSpec(a.shape, lambda c, p: (0,) * a.ndim)
    block = pl.BlockSpec((GRID, 1, GRID, 2, BLOCK, channels), lambda c, p: (0, c, 0, 0, p, 0))
    count = classes * positions * MEMBERS
    weights = (gain1, wqkv, wout, bias, gain2, wup, wdown, mask)
    ff = wup.shape[1]
    return pl.pallas_call(
        functools.partial(kernel, width),
        grid=(classes, positions // BLOCK),
        in_specs=[block] + [whole(a) for a in weights],
        out_specs=[
            block,
            pl.BlockSpec((channels, 3 * channels), lambda c, p: (0, 0)),
            pl.BlockSpec((channels, channels), lambda c, p: (0, 0)),
        ],
        out_shape=[
            jax.ShapeDtypeStruct(data.shape, jnp.bfloat16),
            jax.ShapeDtypeStruct((channels, 3 * channels), jnp.float32),
            jax.ShapeDtypeStruct((channels, channels), jnp.float32),
        ],
        scratch_shapes=[pltpu.VMEM((halves, tokens, LANES), jnp.float32)] * 4,
        compiler_params=pltpu.CompilerParams(vmem_limit_bytes=40 * 1024 * 1024),
        cost_estimate=pl.CostEstimate(
            flops=count * 2 * channels * (12 * channels + 2 * ff),
            bytes_accessed=2 * 2 * data.size,
            transcendentals=count * ff,
        ),
    )(data, *weights)


def prepared(gain1, gain2, pos_bias, channels):
    heads, members, _ = pos_bias.shape
    width = channels // heads
    per = LANES // width
    halves = channels // LANES
    bias = (pos_bias * LOG2E).transpose(2, 0, 1).reshape(members, halves, per * members)
    bias = bias.transpose(1, 0, 2)
    row_head = lax.broadcasted_iota(jnp.int32, (per * members, LANES), 0) // members
    lane_head = lax.broadcasted_iota(jnp.int32, (per * members, LANES), 1) // width
    mask = (row_head == lane_head).astype(jnp.bfloat16)
    return gain1.reshape(1, -1), gain2.reshape(1, -1), bias, mask, width


def reduce_everywhere(partial):
    devices = lax.axis_size(AXES)
    rows, columns = partial.shape
    pieces = partial.astype(jnp.bfloat16).reshape(devices, rows // devices, columns)
    pieces = lax.all_to_all(pieces, AXES, 0, 0, tiled=True)
    total = jnp.sum(pieces.astype(jnp.float32), axis=0).astype(jnp.bfloat16)
    spread = jnp.broadcast_to(total[None], pieces.shape)
    return lax.all_to_all(spread, AXES, 0, 0, tiled=True).astype(jnp.float32).reshape(rows, columns)


def local(tokens, cotangent, norm1_gain, w_qkv, w_out, pos_bias, norm2_gain, w_up, w_down):
    tile_rows, tile_cols, channels = tokens.shape
    row_devices = lax.axis_size("gy")
    column_devices = lax.axis_size("gx")
    devices = row_devices * column_devices
    classes = row_devices // GRID
    positions = tile_rows * tile_cols // devices
    factor = 1.0 / math.sqrt(tile_rows * tile_cols * devices)
    gain1, gain2, bias, mask, width = prepared(norm1_gain, norm2_gain, pos_bias, channels)

    sent = jnp.stack(
        [
            tokens.reshape(devices, positions, channels),
            cotangent.reshape(devices, positions, channels),
        ],
        axis=1,
    )
    data = lax.all_to_all(sent, AXES, 0, 0, tiled=True)
    data = data.reshape(GRID, classes, GRID, 2, positions, channels)
    out, d_wqkv, d_wout = fused(
        data, gain1, w_qkv, w_out, bias, gain2, w_up, w_down, mask, width
    )
    back = lax.all_to_all(
        out.reshape(devices, 2, positions, channels), AXES, 0, 0, tiled=True
    )
    mixed = back[:, 0].reshape(tokens.shape)
    grad_tokens = back[:, 1].reshape(tokens.shape)
    partial = jnp.concatenate([d_wqkv.reshape(-1, channels), d_wout], axis=0)
    total = reduce_everywhere(partial) * factor
    grad_qkv = total[: 3 * channels].reshape(channels, 3 * channels)
    return (mixed, grad_tokens, grad_qkv, total[3 * channels :])


def solution(mesh):
    placed = (P("gy", "gx", None), P("gy", "gx", None), P(), P(), P(), P(), P(), P(), P())
    return jax.shard_map(
        local,
        mesh=mesh,
        in_specs=placed,
        out_specs=(P("gy", "gx", None), P("gy", "gx", None), P(), P()),
        check_vma=False,
    )
```

time: 708 us -> 238 us (0.34); the launches traced: 695 us -> 237 us
  matrix products: 162 us -> 0 us
  waiting for transfers between devices: 233 us -> 101 us
  local copies, waits for them, and re-layouts: 116 us -> 8.9 us
  blocking collectives: 110 us -> 36.5 us
  Pallas kernels: 0 us -> 67.3 us
  other arithmetic: 47 us -> 5.13 us
  between operations: 14.9 us -> 0.83 us
    psum x1 -> x0, waiting for transfers between devices: 174 us -> none  [local(): totals = lax.psum((d_wqkv, d_wout), ('gy', 'gx'))]
    dot_general x13 -> x0, matrix products: 162 us -> none  [the longest x1 31.2 us: attention_backward(): jnp.einsum('nhmk,nkhd->nmhd', d_scaled, keys, preferred_element_type=jnp....]
    all_to_all x2, blocking collectives: 110 us -> 36.5 us  [the longest x1 18.7 us: reduce_everywhere(): pieces = lax.all_to_all(pieces, AXES, 0, 0, tiled=True)]
    pallas_call x0 -> x1, Pallas kernels: none -> 67.3 us  [fused(): pl.pallas_call(functools.partial(kernel, width), grid=(classes, positions...]
    convert_element_type x7 -> x0, local copies, waits for them, and re-layouts: 52.3 us -> none  [the longest x2 26.5 us: attention_backward(): d_qkv = jnp.stack([d_query, d_keys, d_values], axis=2).astype(jnp.bfloat1...]
    all_to_all x2, waiting for transfers between devices: 59 us -> 101 us  [the longest x1 51.3 us: local(): data = lax.all_to_all(sent, AXES, 0, 0, tiled=True)]
    reshape x4 -> x3, local copies, waits for them, and re-layouts: 31.2 us -> 1.4 us  [the longest x1 1.1 us: local(): grad_qkv = total[:3 * channels].reshape(channels, 3 * channels)]
    convert_element_type x5 -> x2, other arithmetic: 18.9 us -> 0.21 us  [the longest x1 0.17 us: prepared(): mask = (row_head == lane_head).astype(jnp.bfloat16)]
  transfers between devices with their start and end apart: 3 -> 2, of which waited for: 2 -> 2; matrix products, arithmetic and copies ran while one was open for 2% -> 1% of each run, Pallas kernels for 0% -> 0%
where the time goes in v1:
time: 238 us; the launch traced here: 237 us
  waiting for transfers between devices  101 us (42%)
  Pallas kernels  67.3 us (28%)
  blocking collectives  36.5 us (15%)
  starting transfers between devices  17.5 us (7%)
  local copies, waits for them, and re-layouts  8.9 us (4%)
  other arithmetic  5.13 us (2%)
    pallas_call x1, Pallas kernels, fused(): pl.pallas_call(functools.partial(kernel, width), grid=(classes, positions...  67.3 us
    all_to_all x1, waiting for transfers between devices, local(): data = lax.all_to_all(sent, AXES, 0, 0, tiled=True)  51.3 us
    all_to_all x1, waiting for transfers between devices, local(): lax.all_to_all(out.reshape(devices, 2, positions, channels), AXES, 0, 0,...  49.7 us
    all_to_all x1, blocking collectives, reduce_everywhere(): pieces = lax.all_to_all(pieces, AXES, 0, 0, tiled=True)  18.7 us
    all_to_all x1, blocking collectives, reduce_everywhere(): lax.all_to_all(spread, AXES, 0, 0, tiled=True).astype(jnp.float32)  17.8 us
    all_to_all x1, starting transfers between devices, local(): data = lax.all_to_all(sent, AXES, 0, 0, tiled=True)  11.7 us
    all_to_all x1, starting transfers between devices, local(): lax.all_to_all(out.reshape(devices, 2, positions, channels), AXES, 0, 0,...  5.83 us
  transfers between devices with their start and end apart: 2, of which 2 were waited for; matrix products, arithmetic and copies ran while one was open for 1% of the time, Pallas kernels for 0%

profile of v1, /device:TPU:0, one launch (start us, length us, event | category | flops | bytes accessed | tf_op | source)
XLA Modules:
  0.0 237.3 jit_solution(2908662108979092879)
XLA Ops:
  0.6 4.6 %pad_maximum_fusion = bf16[128,2,32,256]{3,2,1,0:T(8,128)(2,1)} fusion(bf16[128,1,32,256]{3,2,1,0:T(8,128)(2,1)} %bitcast.24, bf16[128,1,32,256]{3,2,1,0:T(8,128)(2,1)} %bitcast.25), kind=kLoop, calls=%fused_computation | loop fusion | flops 2097152 | bytes 8388608 | tf_op jit(solution)/shard_map/stack | solution.py:220
  5.2 0.0 copy-start.7
  5.2 0.0 copy-start.1
  5.2 0.0 copy-start.2
  5.2 0.0 copy-start.3
  5.2 0.0 copy-start.4
  5.2 0.0 copy-start.5
  5.3 0.0 copy-start.6
  5.3 11.7 %all-to-all-start = ((bf16[128,2,32,256]{3,2,1,0:T(8,128)(2,1)}), bf16[128,2,32,256]{3,2,1,0:T(8,128)(2,1)}, u32[]{:S(2)}, u32[]{:S(2)}) async-start(bf16[128,2,32,256]{3,2,1,0:T(8,128)(2,1)} %pad_maximum_fusion), calls=%async_computation | async-start | bytes 8388608 | tf_op jit(solution)/shard_map/all_to_all | solution.py:227
  17.0 0.0 copy-done.7
  17.0 0.1 copy.18
  17.2 0.2 fusion.mask_ref
  17.3 51.3 %all-to-all-done = bf16[128,2,32,256]{3,2,1,0:T(8,128)(2,1)} async-done(((bf16[128,2,32,256]{3,2,1,0:T(8,128)(2,1)}), bf16[128,2,32,256]{3,2,1,0:T(8,128)(2,1)}, u32[]{:S(2)}, u32[]{:S(2)}) %all-to-all-start) | async-done | bytes 4194336 | tf_op jit(solution)/shard_map/all_to_all | solution.py:227
  68.7 0.0 copy-done.1
  68.7 0.0 copy-done.2
  68.7 0.0 copy-done.3
  68.7 0.0 copy-done.4
  68.7 0.0 copy-done.5
  68.7 0.0 copy-done.6
  68.7 67.3 %shard_map.120 = (bf16[8,2,8,2,32,256]{5,4,3,2,1,0:T(8,128)(2,1)S(1)}, f32[256,768]{1,0:T(8,128)S(1)}, f32[256,256]{1,0:T(8,128)S(1)}) custom-call(bf16[8,2,8,2,32,256]{5,4,3,2,1,0:T(8,128)(2,1)} %bitcast.4.data_ref, f32[1,256]{1,0:T(1,128)S(1)} %bitcast.22, bf16[256,768]{1,0:T(8,128)(2,1)S(1)} %copy-done.3, bf16[256,256]{1,0:T(8,128)(2,1)S(1)} %copy-done.4, ...), custom_call_target="tpu_custom_call" | custom-call | flops 10737418240 | bytes 8388608 | tf_op jit(solution)/shard_map/pallas_call | solution.py:163
  136.0 0.0 copy-start
  136.0 2.0 copy-done
  138.0 0.2 reshape.45
  138.3 18.7 %all_to_all.20 = bf16[128,8,256]{2,1,0:T(8,128)(2,1)S(1)} all-to-all(bf16[128,8,256]{2,1,0:T(8,128)(2,1)S(1)} %maximum_bitcast_fusion), channel_id=1, replica_groups=mesh['gy'=16,'gx'=8] {'gy','gx'}, dimensions={0} | all-to-all | bytes 1048576 | tf_op jit(solution)/shard_map/all_to_all | solution.py:204
  157.0 0.1 reduce_sum.12
  157.2 17.8 %all_to_all.21 = bf16[128,8,256]{2,1,0:T(8,128)(2,1)S(1)} all-to-all(bf16[128,8,256]{2,1,0:T(8,128)(2,1)S(1)} %broadcast_in_dim.2), channel_id=1, replica_groups=mesh['gy'=16,'gx'=8] {'gy','gx'}, dimensions={0} | all-to-all | bytes 1048576 | tf_op jit(solution)/shard_map/all_to_all | solution.py:207
  175.0 5.8 %all-to-all-start.1 = ((bf16[128,2,32,256]{3,2,1,0:T(8,128)(2,1)}), bf16[128,2,32,256]{3,2,1,0:T(8,128)(2,1)}, u32[]{:S(2)}, u32[]{:S(2)}) async-start(bf16[128,2,32,256]{3,2,1,0:T(8,128)(2,1)} %bitcast.20), calls=%async_computation.1 | async-start | bytes 8388608 | tf_op jit(solution)/shard_map/all_to_all | solution.py:232
  180.8 0.1 convert_multiply_fusion
  181.0 0.1 slice.23
  181.0 1.1 reshape.46
  182.1 0.7 slice_bitcast_fusion
  182.8 49.7 %all-to-all-done.1 = bf16[128,2,32,256]{3,2,1,0:T(8,128)(2,1)} async-done(((bf16[128,2,32,256]{3,2,1,0:T(8,128)(2,1)}), bf16[128,2,32,256]{3,2,1,0:T(8,128)(2,1)}, u32[]{:S(2)}, u32[]{:S(2)}) %all-to-all-start.1) | async-done | bytes 4194336 | tf_op jit(solution)/shard_map/all_to_all | solution.py:232
  232.6 4.7 %fusion.1 = (bf16[128,1,32,256]{3,2,1,0:T(8,128)(2,1)}, bf16[128,1,32,256]{3,2,1,0:T(8,128)(2,1)}) fusion(bf16[128,2,32,256]{3,2,1,0:T(8,128)(2,1)} %all-to-all-done.1), kind=kLoop, calls=%fused_computation.17 | loop fusion | bytes 8388608 | tf_op jit(solution)/shard_map/slice | solution.py:236
  (9 shorter events, 0.2 us)
Async XLA Ops:
  5.2 11.7 %copy-start.7 = (f32[8,64,64]{2,1,0:T(8,128)S(1)}, f32[8,64,64]{2,1,0:T(8,128)}, u32[]{:S(2)}) copy-start(f32[8,64,64]{2,1,0:T(8,128)} %param.14) | copy-start | bytes 393220
  5.2 63.5 %copy-start.1 = (bf16[256,1024]{1,0:T(8,128)(2,1)S(1)}, bf16[256,1024]{1,0:T(8,128)(2,1)}, u32[]{:S(2)}) copy-start(bf16[256,1024]{1,0:T(8,128)(2,1)} %wup_ref.1) | copy-start | bytes 1572868
  5.2 63.5 %copy-start.2 = (bf16[1024,256]{1,0:T(8,128)(2,1)S(1)}, bf16[1024,256]{1,0:T(8,128)(2,1)}, u32[]{:S(2)}) copy-start(bf16[1024,256]{1,0:T(8,128)(2,1)} %wdown_ref.1) | copy-start | bytes 1572868
  5.2 63.5 %copy-start.3 = (bf16[256,768]{1,0:T(8,128)(2,1)S(1)}, bf16[256,768]{1,0:T(8,128)(2,1)}, u32[]{:S(2)}) copy-start(bf16[256,768]{1,0:T(8,128)(2,1)} %wqkv_ref.1) | copy-start | bytes 1179652
  5.2 63.5 %copy-start.4 = (bf16[256,256]{1,0:T(8,128)(2,1)S(1)}, bf16[256,256]{1,0:T(8,128)(2,1)}, u32[]{:S(2)}) copy-start(bf16[256,256]{1,0:T(8,128)(2,1)} %wout_ref.1) | copy-start | bytes 393220
  5.2 63.5 %copy-start.5 = (f32[256]{0:T(256)S(1)}, f32[256]{0:T(256)}, u32[]{:S(2)}) copy-start(f32[256]{0:T(256)} %param.11) | copy-start | bytes 3076
  5.3 63.5 %copy-start.6 = (f32[256]{0:T(256)S(1)}, f32[256]{0:T(256)}, u32[]{:S(2)}) copy-start(f32[256]{0:T(256)} %param.15) | copy-start | bytes 3076
  5.3 63.4 %all-to-all-start = ((bf16[128,2,32,256]{3,2,1,0:T(8,128)(2,1)}), bf16[128,2,32,256]{3,2,1,0:T(8,128)(2,1)}, u32[]{:S(2)}, u32[]{:S(2)}) async-start(bf16[128,2,32,256]{3,2,1,0:T(8,128)(2,1)} %pad_maximum_fusion), calls=%async_computation | async-start | bytes 8388608 | tf_op jit(solution)/shard_map/all_to_all | solution.py:227
  136.0 2.0 copy-start
  175.0 57.6 %all-to-all-start.1 = ((bf16[128,2,32,256]{3,2,1,0:T(8,128)(2,1)}), bf16[128,2,32,256]{3,2,1,0:T(8,128)(2,1)}, u32[]{:S(2)}, u32[]{:S(2)}) async-start(bf16[128,2,32,256]{3,2,1,0:T(8,128)(2,1)} %bitcast.20), calls=%async_computation.1 | async-start | bytes 8388608 | tf_op jit(solution)/shard_map/all_to_all | solution.py:232

commit v2 on v1

v2 whole, which is shorter than its diff:
```python
import functools
import math

import jax
import jax.numpy as jnp
from jax import lax
from jax.experimental import pallas as pl
from jax.experimental.pallas import tpu as pltpu
from jax.sharding import PartitionSpec as P

GRID = 8
MEMBERS = GRID * GRID
EPSILON = 1e-05
LOG2E = math.log2(math.e)
AXES = ("gy", "gx")
LANES = 128
BLOCK = 16
BATCH = 4
VMEM_LIMIT = 60 * 1024 * 1024


def dot(a, b, contract=((1,), (0,))):
    return lax.dot_general(a, b, (contract, ((), ())), preferred_element_type=jnp.float32)


def normalize(wide, gain):
    centre = jnp.mean(wide, axis=-1, keepdims=True)
    shifted = wide - centre
    variance = jnp.mean(shifted * shifted, axis=-1, keepdims=True)
    inverse = lax.rsqrt(variance + EPSILON)
    unit = shifted * inverse
    return unit * gain, unit, inverse


def gelu(x):
    inner = x * (0.7978845608028654 + 0.035677408136300125 * (x * x))
    half = 0.5 * x
    return half + half * jnp.tanh(inner)


def pick_heads(full, lane_head, per):
    out = full[(per - 1) * MEMBERS : per * MEMBERS]
    for h in range(per - 2, -1, -1):
        out = jnp.where(lane_head == h, full[h * MEMBERS : (h + 1) * MEMBERS], out)
    return out


def load_tokens(scratch_ref, data_ref):
    halves, tokens, _ = scratch_ref.shape
    for j in range(halves):
        lanes = slice(j * LANES, (j + 1) * LANES)
        scratch_ref[j] = data_ref[:, 0, :, :, lanes].reshape(tokens, LANES).astype(jnp.float32)


def store_tokens(data_ref, scratch_ref):
    halves = scratch_ref.shape[0]
    for j in range(halves):
        lanes = slice(j * LANES, (j + 1) * LANES)
        wide = scratch_ref[j].reshape(GRID, GRID, BLOCK, LANES)
        data_ref[:, 0, :, :, lanes] = wide.astype(jnp.bfloat16)


def group_rows(i):
    return [pl.ds(i * BATCH + g, MEMBERS, stride=BLOCK) for g in range(BATCH)]


def gather_groups(ref, rows):
    halves = ref.shape[0]
    return jnp.concatenate(
        [jnp.concatenate([ref[j, r, :] for j in range(halves)], axis=1) for r in rows], axis=0
    )


def scatter_groups(ref, rows, values):
    for g, r in enumerate(rows):
        for j in range(ref.shape[0]):
            ref[j, r, :] = values[g * MEMBERS : (g + 1) * MEMBERS, j * LANES : (j + 1) * LANES]


def forward_kernel(
    width,
    data_ref,
    gain1_ref,
    wqkv_ref,
    wout_ref,
    bias_ref,
    gain2_ref,
    wup_ref,
    wdown_ref,
    mask_ref,
    out_ref,
    qkv_ref,
    probs_ref,
    context_ref,
    xs_ref,
    mixed_ref,
):
    channels = wout_ref.shape[0]
    halves = channels // LANES
    per = LANES // width
    scale = 1.0 / math.sqrt(width)
    count = BATCH * MEMBERS
    load_tokens(xs_ref, data_ref)
    lane_head = lax.broadcasted_iota(jnp.int32, (MEMBERS, LANES), 1) // width

    def step(i, carry):
        rows = group_rows(i)
        here = pl.ds(pl.multiple_of(i * count, count), count)
        x = gather_groups(xs_ref, rows)
        normed = normalize(x, gain1_ref[...])[0].astype(jnp.bfloat16)
        qkv = dot(normed, wqkv_ref[...]).astype(jnp.bfloat16)
        qkv_ref[here, :] = qkv
        mask = mask_ref[...]
        contexts = []
        for g in range(BATCH):
            part = slice(g * MEMBERS, (g + 1) * MEMBERS)
            ctx_parts = []
            for j in range(halves):
                at = j * LANES
                q = qkv[part, at : at + LANES]
                k = qkv[part, channels + at : channels + at + LANES]
                v = qkv[part, 2 * channels + at : 2 * channels + at + LANES]
                q_heads = jnp.concatenate([q] * per, axis=0) * mask
                scores = dot(k, q_heads, ((1,), (1,))) * (scale * LOG2E) + bias_ref[j]
                e = jnp.exp2(scores - jnp.max(scores, axis=0, keepdims=True))
                probs = (e * (1.0 / jnp.sum(e, axis=0, keepdims=True))).astype(jnp.bfloat16)
                slot = (i * BATCH + g) * halves + j
                probs_ref[pl.ds(pl.multiple_of(slot * MEMBERS, MEMBERS), MEMBERS), :] = probs
                ctx_parts.append(pick_heads(dot(probs, v, ((0,), (0,))), lane_head, per))
            contexts.append(jnp.concatenate(ctx_parts, axis=1))
        context = jnp.concatenate(contexts, axis=0).astype(jnp.bfloat16)
        context_ref[here, :] = context
        attended = (x + dot(context, wout_ref[...])).astype(jnp.bfloat16).astype(jnp.float32)
        normed2 = normalize(attended, gain2_ref[...])[0].astype(jnp.bfloat16)
        hidden = gelu(dot(normed2, wup_ref[...])).astype(jnp.bfloat16)
        scatter_groups(mixed_ref, rows, attended + dot(hidden, wdown_ref[...]))
        return carry

    lax.fori_loop(0, BLOCK // BATCH, step, 0)
    store_tokens(out_ref, mixed_ref)


def backward_kernel(
    width,
    data_ref,
    cot_ref,
    qkv_ref,
    probs_ref,
    context_ref,
    gain1_ref,
    wqkv_ref,
    wout_ref,
    mask_ref,
    out_ref,
    dqkv_acc_ref,
    dout_acc_ref,
    xs_ref,
    gs_ref,
    grad_ref,
):
    channels = wout_ref.shape[0]
    halves = channels // LANES
    per = LANES // width
    scale = 1.0 / math.sqrt(width)
    count = BATCH * MEMBERS

    @pl.when((pl.program_id(0) == 0) & (pl.program_id(1) == 0))
    def _():
        dqkv_acc_ref[...] = jnp.zeros_like(dqkv_acc_ref)
        dout_acc_ref[...] = jnp.zeros_like(dout_acc_ref)

    load_tokens(xs_ref, data_ref)
    load_tokens(gs_ref, cot_ref)
    lane_head = lax.broadcasted_iota(jnp.int32, (MEMBERS, LANES), 1) // width

    def step(i, carry):
        rows = group_rows(i)
        here = pl.ds(pl.multiple_of(i * count, count), count)
        cot = gather_groups(gs_ref, rows)
        cot_low = cot.astype(jnp.bfloat16)
        d_context = dot(cot_low, wout_ref[...], ((1,), (1,))).astype(jnp.bfloat16)
        qkv = qkv_ref[here, :]
        mask = mask_ref[...]
        d_qkvs = []
        for g in range(BATCH):
            part = slice(g * MEMBERS, (g + 1) * MEMBERS)
            dq_parts, dk_parts, dv_parts = [], [], []
            for j in range(halves):
                at = j * LANES
                q = qkv[part, at : at + LANES]
                k = qkv[part, channels + at : channels + at + LANES]
                v = qkv[part, 2 * channels + at : 2 * channels + at + LANES]
                dc = d_context[part, at : at + LANES]
                q_heads = jnp.concatenate([q] * per, axis=0) * mask
                dc_heads = jnp.concatenate([dc] * per, axis=0) * mask
                slot = (i * BATCH + g) * halves + j
                probs_low = probs_ref[pl.ds(pl.multiple_of(slot * MEMBERS, MEMBERS), MEMBERS), :]
                probs = probs_low.astype(jnp.float32)
                d_probs = dot(v, dc_heads, ((1,), (1,)))
                delta = jnp.sum(probs * d_probs, axis=0, keepdims=True)
                d_scaled = (probs * (d_probs - delta) * scale).astype(jnp.bfloat16)
                dv_parts.append(dot(probs_low, dc_heads))
                dk_parts.append(dot(d_scaled, q_heads))
                dq_parts.append(pick_heads(dot(d_scaled, k, ((0,), (0,))), lane_head, per))
            d_qkvs.append(jnp.concatenate(dq_parts + dk_parts + dv_parts, axis=1))
        d_qkv = jnp.concatenate(d_qkvs, axis=0).astype(jnp.bfloat16)
        x = gather_groups(xs_ref, rows)
        normed_wide, unit, inverse = normalize(x, gain1_ref[...])
        dout_acc_ref[...] += dot(context_ref[here, :], cot_low, ((0,), (0,)))
        dqkv_acc_ref[...] += dot(normed_wide.astype(jnp.bfloat16), d_qkv, ((0,), (0,)))
        d_unit = dot(d_qkv, wqkv_ref[...], ((1,), (1,))) * gain1_ref[...]
        grad = cot + inverse * (
            d_unit
            - jnp.mean(d_unit, axis=-1, keepdims=True)
            - unit * jnp.mean(d_unit * unit, axis=-1, keepdims=True)
        )
        scatter_groups(grad_ref, rows, grad)
        return carry

    lax.fori_loop(0, BLOCK // BATCH, step, 0)
    store_tokens(out_ref, grad_ref)


def specs(data):
    _, classes, _, positions, channels = data.shape
    steps = positions // BLOCK
    grid = (classes, steps)
    block = pl.BlockSpec((GRID, 1, GRID, BLOCK, channels), lambda c, p: (0, c, 0, p, 0))
    whole = lambda a: pl.BlockSpec(a.shape, lambda c, p: (0,) * a.ndim)
    flat = lambda rows, width: pl.BlockSpec((rows, width), lambda c, p: (c * steps + p, 0))
    return grid, block, whole, flat, classes * positions


PARAMS = pltpu.CompilerParams(vmem_limit_bytes=VMEM_LIMIT)


def forward(data, gain1, wqkv, wout, bias, gain2, wup, wdown, mask, width):
    grid, block, whole, flat, groups = specs(data)
    channels = data.shape[-1]
    halves = channels // LANES
    tokens = MEMBERS * BLOCK
    count = groups * MEMBERS
    ff = wup.shape[1]
    row_width = mask.shape[0]
    weights = (gain1, wqkv, wout, bias, gain2, wup, wdown, mask)
    return pl.pallas_call(
        functools.partial(forward_kernel, width),
        grid=grid,
        in_specs=[block] + [whole(a) for a in weights],
        out_specs=[
            block,
            flat(tokens, 3 * channels),
            flat(tokens * halves, row_width),
            flat(tokens, channels),
        ],
        out_shape=[
            jax.ShapeDtypeStruct(data.shape, jnp.bfloat16),
            jax.ShapeDtypeStruct((count, 3 * channels), jnp.bfloat16),
            jax.ShapeDtypeStruct((count * halves, row_width), jnp.bfloat16),
            jax.ShapeDtypeStruct((count, channels), jnp.bfloat16),
        ],
        scratch_shapes=[pltpu.VMEM((halves, tokens, LANES), jnp.float32)] * 2,
        compiler_params=PARAMS,
        cost_estimate=pl.CostEstimate(
            flops=count * 2 * channels * (16 * channels + 2 * ff),
            bytes_accessed=2 * count * channels * 8,
            transcendentals=count * ff,
        ),
    )(data, *weights)


def backward(data, cot, qkv, probs, context, gain1, wqkv, wout, mask, width):
    grid, block, whole, flat, groups = specs(data)
    channels = data.shape[-1]
    halves = channels // LANES
    tokens = MEMBERS * BLOCK
    count = groups * MEMBERS
    weights = (gain1, wqkv, wout, mask)
    return pl.pallas_call(
        functools.partial(backward_kernel, width),
        grid=grid,
        in_specs=[
            block,
            block,
            flat(tokens, 3 * channels),
            flat(tokens * halves, mask.shape[0]),
            flat(tokens, channels),
        ]
        + [whole(a) for a in weights],
        out_specs=[
            block,
            pl.BlockSpec((channels, 3 * channels), lambda c, p: (0, 0)),
            pl.BlockSpec((channels, channels), lambda c, p: (0, 0)),
        ],
        out_shape=[
            jax.ShapeDtypeStruct(data.shape, jnp.bfloat16),
            jax.ShapeDtypeStruct((channels, 3 * channels), jnp.float32),
            jax.ShapeDtypeStruct((channels, channels), jnp.float32),
        ],
        scratch_shapes=[pltpu.VMEM((halves, tokens, LANES), jnp.float32)] * 3,
        compiler_params=PARAMS,
        cost_estimate=pl.CostEstimate(
            flops=count * 2 * channels * 24 * channels,
            bytes_accessed=2 * count * channels * 10,
            transcendentals=0,
        ),
    )(data, cot, qkv, probs, context, *weights)


def run_kernel(data, gain1, wqkv, wout, pos_bias, gain2, wup, wdown):
    gain1, gain2, bias, mask, width = prepared(gain1, gain2, pos_bias, data.shape[-1])
    tokens, cot = data[:, :, :, 0], data[:, :, :, 1]
    mixed, qkv, probs, context = forward(
        tokens, gain1, wqkv, wout, bias, gain2, wup, wdown, mask, width
    )
    grad, a, b = backward(tokens, cot, qkv, probs, context, gain1, wqkv, wout, mask, width)
    return jnp.stack([mixed, grad], axis=3), a, b


def prepared(gain1, gain2, pos_bias, channels):
    heads, members, _ = pos_bias.shape
    width = channels // heads
    per = LANES // width
    halves = channels // LANES
    bias = (pos_bias * LOG2E).transpose(2, 0, 1).reshape(members, halves, per * members)
    bias = bias.transpose(1, 0, 2)
    row_head = lax.broadcasted_iota(jnp.int32, (per * members, LANES), 0) // members
    lane_head = lax.broadcasted_iota(jnp.int32, (per * members, LANES), 1) // width
    mask = (row_head == lane_head).astype(jnp.bfloat16)
    return gain1.reshape(1, -1), gain2.reshape(1, -1), bias, mask, width


def exchange(pieces):
    return lax.all_to_all(pieces, AXES, 0, 0, tiled=True)


def local(tokens, cotangent, norm1_gain, w_qkv, w_out, pos_bias, norm2_gain, w_up, w_down):
    tile_rows, tile_cols, channels = tokens.shape
    devices = lax.axis_size(AXES)
    classes = lax.axis_size("gy") // GRID
    positions = tile_rows * tile_cols // devices
    factor = 1.0 / math.sqrt(tile_rows * tile_cols * devices)
    gain1, gain2, bias, mask, width = prepared(norm1_gain, norm2_gain, pos_bias, channels)
    sent = (devices, positions, channels)
    kept = (GRID, classes, GRID, positions, channels)

    data = exchange(tokens.reshape(sent)).reshape(kept)
    cot = exchange(cotangent.reshape(sent)).reshape(kept)
    mixed, qkv, probs, context = forward(
        data, gain1, w_qkv, w_out, bias, gain2, w_up, w_down, mask, width
    )
    mixed = exchange(mixed.reshape(sent))
    grad, d_wqkv, d_wout = backward(
        data, cot, qkv, probs, context, gain1, w_qkv, w_out, mask, width
    )
    partial = jnp.concatenate([d_wqkv.reshape(-1, channels), d_wout], axis=0)
    pieces = partial.astype(jnp.bfloat16).reshape(devices, -1, channels)
    joined = jnp.concatenate([grad.reshape(sent), pieces], axis=1)
    joined, mixed = lax.optimization_barrier((joined, mixed))
    joined = exchange(joined)
    total = jnp.sum(joined[:, positions:].astype(jnp.float32), axis=0) * factor
    total = total.astype(jnp.bfloat16)
    total = exchange(jnp.broadcast_to(total[None], pieces.shape)).astype(jnp.float32)
    total = total.reshape(-1, channels)
    grad_qkv = total[: 3 * channels].reshape(channels, 3 * channels)
    grad_tokens = joined[:, :positions].reshape(tokens.shape)
    return (mixed.reshape(tokens.shape), grad_tokens, grad_qkv, total[3 * channels :])


def solution(mesh):
    placed = (P("gy", "gx", None), P("gy", "gx", None), P(), P(), P(), P(), P(), P(), P())
    return jax.shard_map(
        local,
        mesh=mesh,
        in_specs=placed,
        out_specs=(P("gy", "gx", None), P("gy", "gx", None), P(), P()),
        check_vma=False,
    )
```

time: 238 us -> 215 us (0.903)
  waiting for transfers between devices: 101 us -> 11.8 us
  blocking collectives: 36.5 us -> 85.3 us
  Pallas kernels: 67.3 us -> 82.8 us
  starting transfers between devices: 17.5 us -> 20.2 us
    all_to_all x2 -> x3, waiting for transfers between devices: 101 us -> 11.8 us  [exchange(): return lax.all_to_all(pieces, AXES, 0, 0, tiled=True)]
    all_to_all x2, blocking collectives: 36.5 us -> 85.3 us  [exchange(): return lax.all_to_all(pieces, AXES, 0, 0, tiled=True)]
    pallas_call x1 -> x2, Pallas kernels: 67.3 us -> 82.8 us  [the longest x1 42.5 us: backward(): pl.pallas_call(functools.partial(backward_kernel, width), grid=grid, in_s...]
    slice x2, local copies, waits for them, and re-layouts: 5.42 us -> 2.33 us  [the longest x1 1.61 us: local(): grad_tokens = joined[:, :positions].reshape(tokens.shape)]
    all_to_all x2 -> x3, starting transfers between devices: 17.5 us -> 20.2 us  [exchange(): return lax.all_to_all(pieces, AXES, 0, 0, tiled=True)]
  transfers between devices with their start and end apart: 2 -> 3, of which waited for: 2 -> 1; matrix products, arithmetic and copies ran while one was open for 1% -> 3% of each run, Pallas kernels for 0% -> 39%
where the time goes in v2:
time: 215 us; the launch traced here: 214 us
  blocking collectives  85.3 us (40%)
  Pallas kernels  82.8 us (39%)
  starting transfers between devices  20.2 us (9%)
  waiting for transfers between devices  11.8 us (5%)
  local copies, waits for them, and re-layouts  8.41 us (4%)
  other arithmetic  5.12 us (2%)
    all_to_all x2, blocking collectives, exchange(): return lax.all_to_all(pieces, AXES, 0, 0, tiled=True)  85.3 us
    pallas_call x1, Pallas kernels, backward(): pl.pallas_call(functools.partial(backward_kernel, width), grid=grid, in_s...  42.5 us
    pallas_call x1, Pallas kernels, forward(): pl.pallas_call(functools.partial(forward_kernel, width), grid=grid, in_sp...  40.3 us
    all_to_all x3, starting transfers between devices, exchange(): return lax.all_to_all(pieces, AXES, 0, 0, tiled=True)  20.2 us
    all_to_all x3, waiting for transfers between devices, exchange(): return lax.all_to_all(pieces, AXES, 0, 0, tiled=True)  11.8 us
  transfers between devices with their start and end apart: 3, of which 1 were waited for; matrix products, arithmetic and copies ran while one was open for 3% of the time, Pallas kernels for 39%

profile of v2, /device:TPU:0, one launch (start us, length us, event | category | flops | bytes accessed | tf_op | source)
XLA Modules:
  0.0 214.4 jit_solution(17201277511593690060)
XLA Ops:
  0.6 40.7 %all_to_all.25 = bf16[128,32,256]{2,1,0:T(8,128)(2,1)} all-to-all(bf16[128,32,256]{2,1,0:T(8,128)(2,1)} %bitcast.18), channel_id=1, replica_groups=mesh['gy'=16,'gx'=8] {'gy','gx'}, dimensions={0} | all-to-all | bytes 4194304 | tf_op jit(solution)/shard_map/all_to_all | solution.py:334
  41.3 0.0 copy-start.2
  41.3 4.8 %all-to-all-start.1 = ((bf16[128,32,256]{2,1,0:T(8,128)(2,1)}), bf16[128,32,256]{2,1,0:T(8,128)(2,1)S(1)}, u32[]{:S(2)}, u32[]{:S(2)}) async-start(bf16[128,32,256]{2,1,0:T(8,128)(2,1)} %bitcast.2), calls=%async_computation.1 | async-start | bytes 4194304 | tf_op jit(solution)/shard_map/all_to_all | solution.py:334
  46.2 0.0 copy-done.2
  46.2 0.8 copy.14
  47.0 0.8 fusion.mask_ref
  47.8 40.3 %shard_map.120 = (bf16[8,2,8,32,256]{4,3,2,1,0:T(8,128)(2,1)}, bf16[4096,768]{1,0:T(8,128)(2,1)}, bf16[8192,256]{1,0:T(8,128)(2,1)}, bf16[4096,256]{1,0:T(8,128)(2,1)}) custom-call(bf16[8,2,8,32,256]{4,3,2,1,0:T(8,128)(2,1)} %bitcast.19, f32[1,256]{1,0:T(1,128)} %bitcast.28, bf16[256,768]{1,0:T(8,128)(2,1)} %wqkv_ref.3, bf16[256,256]{1,0:T(8,128)(2,1)} %wout_ref.3, ...), custom_call_target="tpu_custom_call" | custom-call | flops 12884901888 | bytes 16777216 | tf_op jit(solution)/shard_map/pallas_call | solution.py:246
  88.2 0.0 all-to-all-done.1
  88.2 0.0 copy-start
  88.2 10.3 %all-to-all-start.2 = ((bf16[128,32,256]{2,1,0:T(8,128)(2,1)}), bf16[128,32,256]{2,1,0:T(8,128)(2,1)}, u32[]{:S(2)}, u32[]{:S(2)}) async-start(bf16[128,32,256]{2,1,0:T(8,128)(2,1)} %bitcast.22), calls=%async_computation.2 | async-start | bytes 4194304 | tf_op jit(solution)/shard_map/all_to_all | solution.py:334
  98.5 0.0 copy-done
  98.5 42.5 %shard_map.121 = (bf16[8,2,8,32,256]{4,3,2,1,0:T(8,128)(2,1)}, f32[256,768]{1,0:T(8,128)}, f32[256,256]{1,0:T(8,128)}) custom-call(bf16[8,2,8,32,256]{4,3,2,1,0:T(8,128)(2,1)} %bitcast.20, bf16[8,2,8,32,256]{4,3,2,1,0:T(8,128)(2,1)} %bitcast.21, bf16[4096,768]{1,0:T(8,128)(2,1)} %get-tuple-element.13.qkv_ref, bf16[8192,256]{1,0:T(8,128)(2,1)} %get-tuple-element.14.probs_ref, ...), custom_call_target="tpu_custom_call" | custom-call | flops 12884901888 | bytes 20971520 | tf_op jit(solution)/shard_map/pallas_call | solution.py:279
  141.0 0.0 copy-start.1
  141.0 1.1 convert.8
  142.1 1.2 convert.7
  143.3 0.2 reshape.67
  143.5 0.0 copy-done.1
  143.6 1.7 pad_maximum_fusion
  145.3 0.0 all-to-all-done.2
  145.3 44.6 %all_to_all.26 = bf16[128,40,256]{2,1,0:T(8,128)(2,1)S(1)} all-to-all(bf16[128,40,256]{2,1,0:T(8,128)(2,1)} %pad_maximum_fusion), channel_id=1, replica_groups=mesh['gy'=16,'gx'=8] {'gy','gx'}, dimensions={0} | all-to-all | bytes 5242880 | tf_op jit(solution)/shard_map/all_to_all | solution.py:334
  189.8 0.1 convert_reduce_fusion
  190.0 0.8 broadcast_in_dim.2
  190.8 5.1 %all-to-all-start.4 = ((bf16[128,8,256]{2,1,0:T(8,128)(2,1)}), bf16[128,8,256]{2,1,0:T(8,128)(2,1)S(1)}, u32[]{:S(2)}, u32[]{:S(2)}) async-start(bf16[128,8,256]{2,1,0:T(8,128)(2,1)} %broadcast_in_dim.2), calls=%async_computation.4 | async-start | bytes 1048576 | tf_op jit(solution)/shard_map/all_to_all | solution.py:334
  195.9 1.6 slice.21
  197.5 11.8 %all-to-all-done.4 = bf16[128,8,256]{2,1,0:T(8,128)(2,1)S(1)} async-done(((bf16[128,8,256]{2,1,0:T(8,128)(2,1)}), bf16[128,8,256]{2,1,0:T(8,128)(2,1)S(1)}, u32[]{:S(2)}, u32[]{:S(2)}) %all-to-all-start.4) | async-done | bytes 524320 | tf_op jit(solution)/shard_map/all_to_all | solution.py:334
  209.3 0.1 slice.23
  209.4 1.1 reshape.71
  210.5 0.1 convert_element_type.27
  210.5 0.7 slice_bitcast_fusion
  211.3 3.1 %copy.18 = bf16[32,128,256]{2,1,0:T(8,128)(2,1)} copy(bf16[32,128,256]{2,1,0:T(8,128)(2,1)} %bitcast.12) | data formatting | bytes 4194304
  (7 shorter events, 0.1 us)
Async XLA Ops:
  41.3 4.8 %copy-start.2 = (f32[8,64,64]{2,1,0:T(8,128)S(1)}, f32[8,64,64]{2,1,0:T(8,128)}, u32[]{:S(2)}) copy-start(f32[8,64,64]{2,1,0:T(8,128)} %param.14) | copy-start | bytes 393220
  41.3 46.8 %all-to-all-start.1 = ((bf16[128,32,256]{2,1,0:T(8,128)(2,1)}), bf16[128,32,256]{2,1,0:T(8,128)(2,1)S(1)}, u32[]{:S(2)}, u32[]{:S(2)}) async-start(bf16[128,32,256]{2,1,0:T(8,128)(2,1)} %bitcast.2), calls=%async_computation.1 | async-start | bytes 4194304 | tf_op jit(solution)/shard_map/all_to_all | solution.py:334
  88.2 10.3 %copy-start = (bf16[128,32,256]{2,1,0:T(8,128)(2,1)}, bf16[128,32,256]{2,1,0:T(8,128)(2,1)S(1)}, u32[]{:S(2)}) copy-start(bf16[128,32,256]{2,1,0:T(8,128)(2,1)S(1)} %all-to-all-done.1) | copy-start | bytes 6291460
  88.2 57.1 %all-to-all-start.2 = ((bf16[128,32,256]{2,1,0:T(8,128)(2,1)}), bf16[128,32,256]{2,1,0:T(8,128)(2,1)}, u32[]{:S(2)}, u32[]{:S(2)}) async-start(bf16[128,32,256]{2,1,0:T(8,128)(2,1)} %bitcast.22), calls=%async_computation.2 | async-start | bytes 4194304 | tf_op jit(solution)/shard_map/all_to_all | solution.py:334
  141.0 2.5 %copy-start.1 = (bf16[8,2,8,32,256]{4,3,2,1,0:T(8,128)(2,1)S(1)}, bf16[8,2,8,32,256]{4,3,2,1,0:T(8,128)(2,1)}, u32[]{:S(2)}) copy-start(bf16[8,2,8,32,256]{4,3,2,1,0:T(8,128)(2,1)} %get-tuple-element.16) | copy-start | bytes 6291460
  190.8 18.5 %all-to-all-start.4 = ((bf16[128,8,256]{2,1,0:T(8,128)(2,1)}), bf16[128,8,256]{2,1,0:T(8,128)(2,1)S(1)}, u32[]{:S(2)}, u32[]{:S(2)}) async-start(bf16[128,8,256]{2,1,0:T(8,128)(2,1)} %broadcast_in_dim.2), calls=%async_computation.4 | async-start | bytes 1048576 | tf_op jit(solution)/shard_map/all_to_all | solution.py:334

commit v3 on v2

--- a/solution.py
+++ b/solution.py
@@ -15,8 +15,9 @@
 AXES = ("gy", "gx")
 LANES = 128
 BLOCK = 16
-BATCH = 4
-VMEM_LIMIT = 60 * 1024 * 1024
+DENSE = 16
+UNROLL = 16
+VMEM_LIMIT = 62 * 1024 * 1024 + 512 * 1024
 
 
 def dot(a, b, contract=((1,), (0,))):
@@ -61,7 +62,12 @@
 
 
 def group_rows(i):
-    return [pl.ds(i * BATCH + g, MEMBERS, stride=BLOCK) for g in range(BATCH)]
+    return [pl.ds(i * DENSE + g, MEMBERS, stride=BLOCK) for g in range(DENSE)]
+
+
+def token_rows(i):
+    count = DENSE * MEMBERS
+    return pl.ds(pl.multiple_of(i * count, count), count)
 
 
 def gather_groups(ref, rows):
@@ -75,6 +81,14 @@
     for g, r in enumerate(rows):
         for j in range(ref.shape[0]):
             ref[j, r, :] = values[g * MEMBERS : (g + 1) * MEMBERS, j * LANES : (j + 1) * LANES]
+
+
+def repeat(count, step):
+    def body(i, carry):
+        step(i)
+        return carry
+
+    lax.fori_loop(0, count, body, 0)
 
 
 def forward_kernel(
@@ -99,44 +113,50 @@
     halves = channels // LANES
     per = LANES // width
     scale = 1.0 / math.sqrt(width)
-    count = BATCH * MEMBERS
     load_tokens(xs_ref, data_ref)
     lane_head = lax.broadcasted_iota(jnp.int32, (MEMBERS, LANES), 1) // width
 
-    def step(i, carry):
+    def project(i):
+        x = gather_groups(xs_ref, group_rows(i))
+        normed = normalize(x, gain1_ref[...])[0].astype(jnp.bfloat16)
+        qkv_ref[token_rows(i), :] = dot(normed, wqkv_ref[...]).astype(jnp.bfloat16)
+
+    def attend(i):
+        units = []
+        for g in range(UNROLL):
+            part = pl.ds(pl.multiple_of((i * UNROLL + g) * MEMBERS, MEMBERS), MEMBERS)
+            for j in range(halves):
+                slot = (i * UNROLL + g) * halves + j
+                units.append((part, j * LANES, j, pl.ds(pl.multiple_of(slot * MEMBERS, MEMBERS), MEMBERS)))
+        scores, probs = [], []
+        for part, at, j, slot in units:
+            q = qkv_ref[part, at : at + LANES]
+            k = qkv_ref[part, channels + at : channels + at + LANES]
+            q_heads = jnp.concatenate([q] * per, axis=0) * mask_ref[...]
+            scores.append(dot(k, q_heads, ((1,), (1,))))
+        for (part, at, j, slot), raw in zip(units, scores):
+            raw = raw * (scale * LOG2E) + bias_ref[j]
+            e = jnp.exp2(raw - jnp.max(raw, axis=0, keepdims=True))
+            low = (e * (1.0 / jnp.sum(e, axis=0, keepdims=True))).astype(jnp.bfloat16)
+            probs_ref[slot, :] = low
+            probs.append(low)
+        for (part, at, j, slot), low in zip(units, probs):
+            v = qkv_ref[part, 2 * channels + at : 2 * channels + at + LANES]
+            context = pick_heads(dot(low, v, ((0,), (0,))), lane_head, per)
+            context_ref[part, at : at + LANES] = context.astype(jnp.bfloat16)
+
+    def finish(i):
         rows = group_rows(i)
-        here = pl.ds(pl.multiple_of(i * count, count), count)
         x = gather_groups(xs_ref, rows)
-        normed = normalize(x, gain1_ref[...])[0].astype(jnp.bfloat16)
-        qkv = dot(normed, wqkv_ref[...]).astype(jnp.bfloat16)
-        qkv_ref[here, :] = qkv
-        mask = mask_ref[...]
-        contexts = []
-        for g in range(BATCH):
-            part = slice(g * MEMBERS, (g + 1) * MEMBERS)
-            ctx_parts = []
-            for j in range(halves):
-                at = j * LANES
-                q = qkv[part, at : at + LANES]
-                k = qkv[part, channels + at : channels + at + LANES]
-                v = qkv[part, 2 * channels + at : 2 * channels + at + LANES]
-                q_heads = jnp.concatenate([q] * per, axis=0) * mask
-                scores = dot(k, q_heads, ((1,), (1,))) * (scale * LOG2E) + bias_ref[j]
-                e = jnp.exp2(scores - jnp.max(scores, axis=0, keepdims=True))
-                probs = (e * (1.0 / jnp.sum(e, axis=0, keepdims=True))).astype(jnp.bfloat16)
-                slot = (i * BATCH + g) * halves + j
-                probs_ref[pl.ds(pl.multiple_of(slot * MEMBERS, MEMBERS), MEMBERS), :] = probs
-                ctx_parts.append(pick_heads(dot(probs, v, ((0,), (0,))), lane_head, per))
-            contexts.append(jnp.concatenate(ctx_parts, axis=1))
-        context = jnp.concatenate(contexts, axis=0).astype(jnp.bfloat16)
-        context_ref[here, :] = context
+        context = context_ref[token_rows(i), :]
         attended = (x + dot(context, wout_ref[...])).astype(jnp.bfloat16).astype(jnp.float32)
         normed2 = normalize(attended, gain2_ref[...])[0].astype(jnp.bfloat16)
         hidden = gelu(dot(normed2, wup_ref[...])).astype(jnp.bfloat16)
         scatter_groups(mixed_ref, rows, attended + dot(hidden, wdown_ref[...]))
-        return carry
-
-    lax.fori_loop(0, BLOCK // BATCH, step, 0)
+
+    repeat(BLOCK // DENSE, project)
+    repeat(BLOCK // UNROLL, attend)
+    repeat(BLOCK // DENSE, finish)
     store_tokens(out_ref, mixed_ref)
 
 
@@ -152,73 +172,89 @@
     wout_ref,
     mask_ref,
     out_ref,
-    dqkv_acc_ref,
-    dout_acc_ref,
+    partial_ref,
+    acc_ref,
     xs_ref,
     gs_ref,
     grad_ref,
+    dctx_ref,
+    dqkv_ref,
 ):
     channels = wout_ref.shape[0]
     halves = channels // LANES
     per = LANES // width
     scale = 1.0 / math.sqrt(width)
-    count = BATCH * MEMBERS
 
     @pl.when((pl.program_id(0) == 0) & (pl.program_id(1) == 0))
     def _():
-        dqkv_acc_ref[...] = jnp.zeros_like(dqkv_acc_ref)
-        dout_acc_ref[...] = jnp.zeros_like(dout_acc_ref)
+        acc_ref[...] = jnp.zeros_like(acc_ref)
 
     load_tokens(xs_ref, data_ref)
     load_tokens(gs_ref, cot_ref)
     lane_head = lax.broadcasted_iota(jnp.int32, (MEMBERS, LANES), 1) // width
 
-    def step(i, carry):
+    def project(i):
+        here = token_rows(i)
+        cot = gather_groups(gs_ref, group_rows(i)).astype(jnp.bfloat16)
+        dctx_ref[here, :] = dot(cot, wout_ref[...], ((1,), (1,))).astype(jnp.bfloat16)
+        acc_ref[3] += dot(context_ref[here, :], cot, ((0,), (0,)))
+
+    def attend(i):
+        units = []
+        for g in range(UNROLL):
+            part = pl.ds(pl.multiple_of((i * UNROLL + g) * MEMBERS, MEMBERS), MEMBERS)
+            for j in range(halves):
+                slot = (i * UNROLL + g) * halves + j
+                units.append((part, j * LANES, pl.ds(pl.multiple_of(slot * MEMBERS, MEMBERS), MEMBERS)))
+
+        def put(n, part, at, value):
+            to = n * channels + at
+            dqkv_ref[part, to : to + LANES] = value.astype(jnp.bfloat16)
+
+        d_probs, d_scaled = [], []
+        for part, at, slot in units:
+            v = qkv_ref[part, 2 * channels + at : 2 * channels + at + LANES]
+            dc_heads = jnp.concatenate([dctx_ref[part, at : at + LANES]] * per, axis=0) * mask_ref[...]
+            d_probs.append(dot(v, dc_heads, ((1,), (1,))))
+            put(2, part, at, dot(probs_ref[slot, :], dc_heads))
+        for (part, at, slot), dp in zip(units, d_probs):
+            probs = probs_ref[slot, :].astype(jnp.float32)
+            delta = jnp.sum(probs * dp, axis=0, keepdims=True)
+            d_scaled.append((probs * (dp - delta) * scale).astype(jnp.bfloat16))
+        for (part, at, slot), ds in zip(units, d_scaled):
+            q_heads = jnp.concatenate([qkv_ref[part, at : at + LANES]] * per, axis=0) * mask_ref[...]
+            put(1, part, at, dot(ds, q_heads))
+            k = qkv_ref[part, channels + at : channels + at + LANES]
+            put(0, part, at, pick_heads(dot(ds, k, ((0,), (0,))), lane_head, per))
+
+    def finish(i):
         rows = group_rows(i)
-        here = pl.ds(pl.multiple_of(i * count, count), count)
-        cot = gather_groups(gs_ref, rows)
-        cot_low = cot.astype(jnp.bfloat16)
-        d_context = dot(cot_low, wout_ref[...], ((1,), (1,))).astype(jnp.bfloat16)
-        qkv = qkv_ref[here, :]
-        mask = mask_ref[...]
-        d_qkvs = []
-        for g in range(BATCH):
-            part = slice(g * MEMBERS, (g + 1) * MEMBERS)
-            dq_parts, dk_parts, dv_parts = [], [], []
-            for j in range(halves):
-                at = j * LANES
-                q = qkv[part, at : at + LANES]
-                k = qkv[part, channels + at : channels + at + LANES]
-                v = qkv[part, 2 * channels + at : 2 * channels + at + LANES]
-                dc = d_context[part, at : at + LANES]
-                q_heads = jnp.concatenate([q] * per, axis=0) * mask
-                dc_heads = jnp.concatenate([dc] * per, axis=0) * mask
-                slot = (i * BATCH + g) * halves + j
-                probs_low = probs_ref[pl.ds(pl.multiple_of(slot * MEMBERS, MEMBERS), MEMBERS), :]
-                probs = probs_low.astype(jnp.float32)
-                d_probs = dot(v, dc_heads, ((1,), (1,)))
-                delta = jnp.sum(probs * d_probs, axis=0, keepdims=True)
-                d_scaled = (probs * (d_probs - delta) * scale).astype(jnp.bfloat16)
-                dv_parts.append(dot(probs_low, dc_heads))
-                dk_parts.append(dot(d_scaled, q_heads))
-                dq_parts.append(pick_heads(dot(d_scaled, k, ((0,), (0,))), lane_head, per))
-            d_qkvs.append(jnp.concatenate(dq_parts + dk_parts + dv_parts, axis=1))
-        d_qkv = jnp.concatenate(d_qkvs, axis=0).astype(jnp.bfloat16)
         x = gather_groups(xs_ref, rows)
+        d_qkv = dqkv_ref[token_rows(i), :]
         normed_wide, unit, inverse = normalize(x, gain1_ref[...])
-        dout_acc_ref[...] += dot(context_ref[here, :], cot_low, ((0,), (0,)))
-        dqkv_acc_ref[...] += dot(normed_wide.astype(jnp.bfloat16), d_qkv, ((0,), (0,)))
+        d_weight = dot(normed_wide.astype(jnp.bfloat16), d_qkv, ((0,), (0,)))
+        for n in range(3):
+            acc_ref[n] += d_weight[:, n * channels : (n + 1) * channels]
         d_unit = dot(d_qkv, wqkv_ref[...], ((1,), (1,))) * gain1_ref[...]
-        grad = cot + inverse * (
+        grad = gather_groups(gs_ref, rows) + inverse * (
             d_unit
             - jnp.mean(d_unit, axis=-1, keepdims=True)
             - unit * jnp.mean(d_unit * unit, axis=-1, keepdims=True)
         )
         scatter_groups(grad_ref, rows, grad)
-        return carry
-
-    lax.fori_loop(0, BLOCK // BATCH, step, 0)
+
+    repeat(BLOCK // DENSE, project)
+    repeat(BLOCK // UNROLL, attend)
+    repeat(BLOCK // DENSE, finish)
     store_tokens(out_ref, grad_ref)
+
+    last = (pl.program_id(0) == pl.num_programs(0) - 1) & (
+        pl.program_id(1) == pl.num_programs(1) - 1
+    )
+
+    @pl.when(last)
+    def _():
+        partial_ref[...] = acc_ref[...].reshape(partial_ref.shape).astype(jnp.bfloat16)
 
 
 def specs(data):
@@ -289,15 +325,18 @@
         + [whole(a) for a in weights],
         out_specs=[
             block,
-            pl.BlockSpec((channels, 3 * channels), lambda c, p: (0, 0)),
-            pl.BlockSpec((channels, channels), lambda c, p: (0, 0)),
+            pl.BlockSpec((4 * channels, channels), lambda c, p: (0, 0)),
         ],
         out_shape=[
             jax.ShapeDtypeStruct(data.shape, jnp.bfloat16),
-            jax.ShapeDtypeStruct((channels, 3 * channels), jnp.float32),
-            jax.ShapeDtypeStruct((channels, channels), jnp.float32),
+            jax.ShapeDtypeStruct((4 * channels, channels), jnp.bfloat16),
         ],
-        scratch_shapes=[pltpu.VMEM((halves, tokens, LANES), jnp.float32)] * 3,
+        scratch_shapes=[pltpu.VMEM((4, channels, channels), jnp.float32)]
+        + [pltpu.VMEM((halves, tokens, LANES), jnp.float32)] * 3
+        + [
+            pltpu.VMEM((tokens, channels), jnp.bfloat16),
+            pltpu.VMEM((tokens, 3 * channels), jnp.bfloat16),
+        ],
         compiler_params=PARAMS,
         cost_estimate=pl.CostEstimate(
             flops=count * 2 * channels * 24 * channels,
@@ -313,8 +352,9 @@
     mixed, qkv, probs, context = forward(
         tokens, gain1, wqkv, wout, bias, gain2, wup, wdown, mask, width
     )
-    grad, a, b = backward(tokens, cot, qkv, probs, context, gain1, wqkv, wout, mask, width)
-    return jnp.stack([mixed, grad], axis=3), a, b
+    grad, p = backward(tokens, cot, qkv, probs, context, gain1, wqkv, wout, mask, width)
+    p = p.astype(jnp.float32).reshape(4, 256, 256)
+    return jnp.stack([mixed, grad], axis=3), jnp.concatenate([p[0], p[1], p[2]], axis=1), p[3]
 
 
 def prepared(gain1, gain2, pos_bias, channels):
@@ -330,6 +370,25 @@
     return gain1.reshape(1, -1), gain2.reshape(1, -1), bias, mask, width
 
 
+def place_kernel(source_ref, out_ref):
+    out_ref[...] = source_ref[...]
+
+
+def placed(values):
+    rows, columns, channels = values.shape
+    block = pl.BlockSpec((rows // 4, columns, channels), lambda i: (i, 0, 0))
+    return pl.pallas_call(
+        place_kernel,
+        grid=(4,),
+        in_specs=[block],
+        out_specs=block,
+        out_shape=jax.ShapeDtypeStruct(values.shape, values.dtype),
+        cost_estimate=pl.CostEstimate(
+            flops=0, bytes_accessed=4 * values.size, transcendentals=0
+        ),
+    )(values)
+
+
 def exchange(pieces):
     return lax.all_to_all(pieces, AXES, 0, 0, tiled=True)
 
@@ -349,22 +408,20 @@
     mixed, qkv, probs, context = forward(
         data, gain1, w_qkv, w_out, bias, gain2, w_up, w_down, mask, width
     )
-    mixed = exchange(mixed.reshape(sent))
-    grad, d_wqkv, d_wout = backward(
+    mixed = exchange(mixed.reshape(sent)).reshape(tokens.shape)
+    grad, partial = backward(
         data, cot, qkv, probs, context, gain1, w_qkv, w_out, mask, width
     )
-    partial = jnp.concatenate([d_wqkv.reshape(-1, channels), d_wout], axis=0)
-    pieces = partial.astype(jnp.bfloat16).reshape(devices, -1, channels)
+    pieces = partial.reshape(devices, -1, channels)
     joined = jnp.concatenate([grad.reshape(sent), pieces], axis=1)
     joined, mixed = lax.optimization_barrier((joined, mixed))
     joined = exchange(joined)
     total = jnp.sum(joined[:, positions:].astype(jnp.float32), axis=0) * factor
-    total = total.astype(jnp.bfloat16)
-    total = exchange(jnp.broadcast_to(total[None], pieces.shape)).astype(jnp.float32)
-    total = total.reshape(-1, channels)
-    grad_qkv = total[: 3 * channels].reshape(channels, 3 * channels)
+    total = exchange(jnp.broadcast_to(total.astype(jnp.bfloat16)[None], pieces.shape))
+    blocks = total.astype(jnp.float32).reshape(4, channels, channels)
+    grad_qkv = jnp.concatenate([blocks[0], blocks[1], blocks[2]], axis=1)
     grad_tokens = joined[:, :positions].reshape(tokens.shape)
-    return (mixed.reshape(tokens.shape), grad_tokens, grad_qkv, total[3 * channels :])
+    return (placed(mixed), grad_tokens, grad_qkv, blocks[3])
 
 
 def solution(mesh):

time: 215 us -> 178 us (0.83)
  Pallas kernels: 82.8 us -> 52.5 us
  local copies, waits for them, and re-layouts: 8.41 us -> 3.99 us
  blocking collectives: 85.3 us -> 82.8 us
    pallas_call x1, Pallas kernels: 42.5 us -> 23.1 us  [backward(): pl.pallas_call(functools.partial(backward_kernel, width), grid=grid, in_s...]
    pallas_call x1, Pallas kernels: 40.3 us -> 25.6 us  [forward(): pl.pallas_call(functools.partial(forward_kernel, width), grid=grid, in_sp...]
    pallas_call x0 -> x1, Pallas kernels: none -> 3.78 us  [placed(): pl.pallas_call(place_kernel, grid=(4,), in_specs=[block], out_specs=block...]
    unnamed x7 -> x2, local copies, waits for them, and re-layouts: 3.14 us -> 0.01 us
    all_to_all x2, blocking collectives: 85.3 us -> 82.8 us  [exchange(): return lax.all_to_all(pieces, AXES, 0, 0, tiled=True)]
    another operation x2 -> x0, other arithmetic: 2.29 us -> none
  transfers between devices with their start and end apart: 3 -> 3, of which waited for: 1 -> 3; matrix products, arithmetic and copies ran while one was open for 3% -> 4% of each run, Pallas kernels for 39% -> 30%
where the time goes in v3:
time: 178 us; the launch traced here: 177 us
  blocking collectives  82.8 us (47%)
  Pallas kernels  52.5 us (29%)
  starting transfers between devices  19.6 us (11%)
  waiting for transfers between devices  12 us (7%)
  other arithmetic  5.45 us (3%)
  local copies, waits for them, and re-layouts  3.99 us (2%)
    all_to_all x2, blocking collectives, exchange(): return lax.all_to_all(pieces, AXES, 0, 0, tiled=True)  82.8 us
    pallas_call x1, Pallas kernels, forward(): pl.pallas_call(functools.partial(forward_kernel, width), grid=grid, in_sp...  25.6 us
    pallas_call x1, Pallas kernels, backward(): pl.pallas_call(functools.partial(backward_kernel, width), grid=grid, in_s...  23.1 us
    all_to_all x3, starting transfers between devices, exchange(): return lax.all_to_all(pieces, AXES, 0, 0, tiled=True)  19.6 us
    all_to_all x3, waiting for transfers between devices, exchange(): return lax.all_to_all(pieces, AXES, 0, 0, tiled=True)  12 us
    pallas_call x1, Pallas kernels, placed(): pl.pallas_call(place_kernel, grid=(4,), in_specs=[block], out_specs=block...  3.78 us
  transfers between devices with their start and end apart: 3, of which 3 were waited for; matrix products, arithmetic and copies ran while one was open for 4% of the time, Pallas kernels for 30%

profile of v3, /device:TPU:0, one launch (start us, length us, event | category | flops | bytes accessed | tf_op | source)
XLA Modules:
  0.0 177.1 jit_solution(8364151123119521395)
XLA Ops:
  0.6 40.7 %all_to_all.25 = bf16[128,32,256]{2,1,0:T(8,128)(2,1)} all-to-all(bf16[128,32,256]{2,1,0:T(8,128)(2,1)} %bitcast.23), channel_id=1, replica_groups=mesh['gy'=16,'gx'=8] {'gy','gx'}, dimensions={0} | all-to-all | bytes 4194304 | tf_op jit(solution)/shard_map/all_to_all | solution.py:393
  41.3 0.0 copy-start
  41.3 5.9 %all-to-all-start.1 = ((bf16[128,32,256]{2,1,0:T(8,128)(2,1)}), bf16[128,32,256]{2,1,0:T(8,128)(2,1)}, u32[]{:S(2)}, u32[]{:S(2)}) async-start(bf16[128,32,256]{2,1,0:T(8,128)(2,1)} %bitcast.2), calls=%async_computation.1 | async-start | bytes 4194304 | tf_op jit(solution)/shard_map/all_to_all | solution.py:393
  47.3 0.0 copy-done
  47.3 0.8 copy.14
  48.1 0.8 fusion.mask_ref
  48.9 25.6 %shard_map.120 = (bf16[8,2,8,32,256]{4,3,2,1,0:T(8,128)(2,1)}, bf16[4096,768]{1,0:T(8,128)(2,1)}, bf16[8192,256]{1,0:T(8,128)(2,1)}, bf16[4096,256]{1,0:T(8,128)(2,1)}) custom-call(bf16[8,2,8,32,256]{4,3,2,1,0:T(8,128)(2,1)} %bitcast.24, f32[1,256]{1,0:T(1,128)} %bitcast.33, bf16[256,768]{1,0:T(8,128)(2,1)} %wqkv_ref.3, bf16[256,256]{1,0:T(8,128)(2,1)} %wout_ref.3, ...), custom_call_target="tpu_custom_call" | custom-call | flops 12884901888 | bytes 16777216 | tf_op jit(solution)/shard_map/pallas_call | solution.py:282
  74.5 1.8 all-to-all-done.1
  76.3 8.6 %all-to-all-start.2 = ((bf16[128,32,256]{2,1,0:T(8,128)(2,1)}), bf16[128,32,256]{2,1,0:T(8,128)(2,1)}, u32[]{:S(2)}, u32[]{:S(2)}) async-start(bf16[128,32,256]{2,1,0:T(8,128)(2,1)} %bitcast.27), calls=%async_computation.2 | async-start | bytes 4194304 | tf_op jit(solution)/shard_map/all_to_all | solution.py:393
  84.9 23.1 %shard_map.121 = (bf16[8,2,8,32,256]{4,3,2,1,0:T(8,128)(2,1)}, bf16[1024,256]{1,0:T(8,128)(2,1)}) custom-call(bf16[8,2,8,32,256]{4,3,2,1,0:T(8,128)(2,1)} %bitcast.25, bf16[8,2,8,32,256]{4,3,2,1,0:T(8,128)(2,1)} %bitcast.3.cot_ref, bf16[4096,768]{1,0:T(8,128)(2,1)} %get-tuple-element.12.qkv_ref, bf16[8192,256]{1,0:T(8,128)(2,1)} %get-tuple-element.13.probs_ref, ...), custom_call_target="tpu_custom_call" | custom-call | flops 12884901888 | bytes 20971520 | tf_op jit(solution)/shard_map/pallas_call | solution.py:315
  108.0 3.5 %pad_maximum_fusion = bf16[128,40,256]{2,1,0:T(8,128)(2,1)} fusion(bf16[128,8,256]{2,1,0:T(8,128)(2,1)} %bitcast.30, bf16[128,32,256]{2,1,0:T(8,128)(2,1)} %bitcast.28), kind=kLoop, calls=%fused_computation | loop fusion | flops 5242880 | bytes 5242880 | tf_op jit(solution)/shard_map/concatenate | solution.py:416
  111.5 2.3 %all-to-all-done.2 = bf16[128,32,256]{2,1,0:T(8,128)(2,1)} async-done(((bf16[128,32,256]{2,1,0:T(8,128)(2,1)}), bf16[128,32,256]{2,1,0:T(8,128)(2,1)}, u32[]{:S(2)}, u32[]{:S(2)}) %all-to-all-start.2) | async-done | bytes 2097184 | tf_op jit(solution)/shard_map/all_to_all | solution.py:393
  113.8 42.1 %all_to_all.26 = bf16[128,40,256]{2,1,0:T(8,128)(2,1)S(1)} all-to-all(bf16[128,40,256]{2,1,0:T(8,128)(2,1)} %pad_maximum_fusion), channel_id=1, replica_groups=mesh['gy'=16,'gx'=8] {'gy','gx'}, dimensions={0} | all-to-all | bytes 5242880 | tf_op jit(solution)/shard_map/all_to_all | solution.py:393
  155.9 0.1 convert_reduce_fusion
  156.0 0.8 broadcast_in_dim.2
  156.9 5.1 %all-to-all-start.4 = ((bf16[128,8,256]{2,1,0:T(8,128)(2,1)}), bf16[128,8,256]{2,1,0:T(8,128)(2,1)S(1)}, u32[]{:S(2)}, u32[]{:S(2)}) async-start(bf16[128,8,256]{2,1,0:T(8,128)(2,1)} %broadcast_in_dim.2), calls=%async_computation.4 | async-start | bytes 1048576 | tf_op jit(solution)/shard_map/all_to_all | solution.py:393
  161.9 3.8 %shard_map.122 = bf16[32,128,256]{2,1,0:T(8,128)(2,1)} custom-call(bf16[32,128,256]{2,1,0:T(8,128)(2,1)} %bitcast.12.source_ref), custom_call_target="tpu_custom_call" | custom-call | bytes 4194304 | tf_op jit(solution)/shard_map/pallas_call | solution.py:380
  165.7 1.6 slice.28
  167.3 8.0 %all-to-all-done.4 = bf16[128,8,256]{2,1,0:T(8,128)(2,1)S(1)} async-done(((bf16[128,8,256]{2,1,0:T(8,128)(2,1)}), bf16[128,8,256]{2,1,0:T(8,128)(2,1)S(1)}, u32[]{:S(2)}, u32[]{:S(2)}) %all-to-all-start.4) | async-done | bytes 524320 | tf_op jit(solution)/shard_map/all_to_all | solution.py:393
  175.3 0.1 convert_element_type.21
  175.4 0.8 slice_bitcast_fusion
  176.2 0.9 pad_maximum_fusion.1
  (6 shorter events, 0.1 us)
Async XLA Ops:
  41.3 5.9 %copy-start = (f32[8,64,64]{2,1,0:T(8,128)S(1)}, f32[8,64,64]{2,1,0:T(8,128)}, u32[]{:S(2)}) copy-start(f32[8,64,64]{2,1,0:T(8,128)} %param.14) | copy-start | bytes 393220
  41.3 34.9 %all-to-all-start.1 = ((bf16[128,32,256]{2,1,0:T(8,128)(2,1)}), bf16[128,32,256]{2,1,0:T(8,128)(2,1)}, u32[]{:S(2)}, u32[]{:S(2)}) async-start(bf16[128,32,256]{2,1,0:T(8,128)(2,1)} %bitcast.2), calls=%async_computation.1 | async-start | bytes 4194304 | tf_op jit(solution)/shard_map/all_to_all | solution.py:393
  76.3 37.5 %all-to-all-start.2 = ((bf16[128,32,256]{2,1,0:T(8,128)(2,1)}), bf16[128,32,256]{2,1,0:T(8,128)(2,1)}, u32[]{:S(2)}, u32[]{:S(2)}) async-start(bf16[128,32,256]{2,1,0:T(8,128)(2,1)} %bitcast.27), calls=%async_computation.2 | async-start | bytes 4194304 | tf_op jit(solution)/shard_map/all_to_all | solution.py:393
  156.9 18.5 %all-to-all-start.4 = ((bf16[128,8,256]{2,1,0:T(8,128)(2,1)}), bf16[128,8,256]{2,1,0:T(8,128)(2,1)S(1)}, u32[]{:S(2)}, u32[]{:S(2)}) async-start(bf16[128,8,256]{2,1,0:T(8,128)(2,1)} %broadcast_in_dim.2), calls=%async_computation.4 | async-start | bytes 1048576 | tf_op jit(solution)/shard_map/all_to_all | solution.py:393

commit v4 on v3

--- a/solution.py
+++ b/solution.py
@@ -15,8 +15,8 @@
 AXES = ("gy", "gx")
 LANES = 128
 BLOCK = 16
-DENSE = 16
-UNROLL = 16
+DENSE = 8
+UNROLL = 8
 VMEM_LIMIT = 62 * 1024 * 1024 + 512 * 1024
 
 
@@ -61,13 +61,19 @@
         data_ref[:, 0, :, :, lanes] = wide.astype(jnp.bfloat16)
 
 
+def head_mask(shape, width):
+    row_head = lax.broadcasted_iota(jnp.int32, shape, 0) // MEMBERS
+    lane_head = lax.broadcasted_iota(jnp.int32, shape, 1) // width
+    return (row_head == lane_head).astype(jnp.float32).astype(jnp.bfloat16)
+
+
 def group_rows(i):
     return [pl.ds(i * DENSE + g, MEMBERS, stride=BLOCK) for g in range(DENSE)]
 
 
 def token_rows(i):
     count = DENSE * MEMBERS
-    return pl.ds(pl.multiple_of(i * count, count), count)
+    return pl.ds(i * count, count)
 
 
 def gather_groups(ref, rows):
@@ -84,11 +90,8 @@
 
 
 def repeat(count, step):
-    def body(i, carry):
+    for i in range(count):
         step(i)
-        return carry
-
-    lax.fori_loop(0, count, body, 0)
 
 
 def forward_kernel(
@@ -97,22 +100,31 @@
     gain1_ref,
     wqkv_ref,
     wout_ref,
-    bias_ref,
+    pos_ref,
     gain2_ref,
     wup_ref,
     wdown_ref,
-    mask_ref,
     out_ref,
     qkv_ref,
     probs_ref,
     context_ref,
     xs_ref,
     mixed_ref,
+    mask_ref,
+    bias_ref,
 ):
     channels = wout_ref.shape[0]
     halves = channels // LANES
     per = LANES // width
     scale = 1.0 / math.sqrt(width)
+    @pl.when((pl.program_id(0) == 0) & (pl.program_id(1) == 0))
+    def _():
+        mask_ref[...] = head_mask(mask_ref.shape, width)
+        for j in range(halves):
+            for h in range(per):
+                lanes = slice(h * MEMBERS, (h + 1) * MEMBERS)
+                bias_ref[j, :, lanes] = pos_ref[j * per + h].T * LOG2E
+
     load_tokens(xs_ref, data_ref)
     lane_head = lax.broadcasted_iota(jnp.int32, (MEMBERS, LANES), 1) // width
 
@@ -124,10 +136,10 @@
     def attend(i):
         units = []
         for g in range(UNROLL):
-            part = pl.ds(pl.multiple_of((i * UNROLL + g) * MEMBERS, MEMBERS), MEMBERS)
+            part = pl.ds((i * UNROLL + g) * MEMBERS, MEMBERS)
             for j in range(halves):
                 slot = (i * UNROLL + g) * halves + j
-                units.append((part, j * LANES, j, pl.ds(pl.multiple_of(slot * MEMBERS, MEMBERS), MEMBERS)))
+                units.append((part, j * LANES, j, pl.ds(slot * MEMBERS, MEMBERS)))
         scores, probs = [], []
         for part, at, j, slot in units:
             q = qkv_ref[part, at : at + LANES]
@@ -151,12 +163,20 @@
         context = context_ref[token_rows(i), :]
         attended = (x + dot(context, wout_ref[...])).astype(jnp.bfloat16).astype(jnp.float32)
         normed2 = normalize(attended, gain2_ref[...])[0].astype(jnp.bfloat16)
-        hidden = gelu(dot(normed2, wup_ref[...])).astype(jnp.bfloat16)
-        scatter_groups(mixed_ref, rows, attended + dot(hidden, wdown_ref[...]))
-
-    repeat(BLOCK // DENSE, project)
-    repeat(BLOCK // UNROLL, attend)
-    repeat(BLOCK // DENSE, finish)
+        mixed = attended
+        wide = wup_ref.shape[1] // 2
+        for f in range(2):
+            at = slice(f * wide, (f + 1) * wide)
+            hidden = gelu(dot(normed2, wup_ref[:, at])).astype(jnp.bfloat16)
+            mixed = mixed + dot(hidden, wdown_ref[at, :])
+        scatter_groups(mixed_ref, rows, mixed)
+
+    project(0)
+    project(1)
+    attend(0)
+    attend(1)
+    finish(0)
+    finish(1)
     store_tokens(out_ref, mixed_ref)
 
 
@@ -170,24 +190,33 @@
     gain1_ref,
     wqkv_ref,
     wout_ref,
-    mask_ref,
     out_ref,
-    partial_ref,
     acc_ref,
     xs_ref,
     gs_ref,
     grad_ref,
     dctx_ref,
     dqkv_ref,
+    mask_ref,
+    stage_ref,
+    pieces_ref,
+    sent,
+    sent_pieces,
 ):
     channels = wout_ref.shape[0]
     halves = channels // LANES
     per = LANES // width
     scale = 1.0 / math.sqrt(width)
 
-    @pl.when((pl.program_id(0) == 0) & (pl.program_id(1) == 0))
+    steps = pl.num_programs(1)
+    turn = pl.program_id(0) * steps + pl.program_id(1)
+    last = pl.num_programs(0) * steps - 1
+    positions = steps * BLOCK
+
+    @pl.when(turn == 0)
     def _():
         acc_ref[...] = jnp.zeros_like(acc_ref)
+        mask_ref[...] = head_mask(mask_ref.shape, width)
 
     load_tokens(xs_ref, data_ref)
     load_tokens(gs_ref, cot_ref)
@@ -197,15 +226,17 @@
         here = token_rows(i)
         cot = gather_groups(gs_ref, group_rows(i)).astype(jnp.bfloat16)
         dctx_ref[here, :] = dot(cot, wout_ref[...], ((1,), (1,))).astype(jnp.bfloat16)
-        acc_ref[3] += dot(context_ref[here, :], cot, ((0,), (0,)))
+        d_weight = dot(context_ref[here, :], cot, ((0,), (0,)))
+        for n in range(halves):
+            acc_ref[3 * halves + n] += d_weight[:, n * LANES : (n + 1) * LANES]
 
     def attend(i):
         units = []
         for g in range(UNROLL):
-            part = pl.ds(pl.multiple_of((i * UNROLL + g) * MEMBERS, MEMBERS), MEMBERS)
+            part = pl.ds((i * UNROLL + g) * MEMBERS, MEMBERS)
             for j in range(halves):
                 slot = (i * UNROLL + g) * halves + j
-                units.append((part, j * LANES, pl.ds(pl.multiple_of(slot * MEMBERS, MEMBERS), MEMBERS)))
+                units.append((part, j * LANES, pl.ds(slot * MEMBERS, MEMBERS)))
 
         def put(n, part, at, value):
             to = n * channels + at
@@ -233,8 +264,8 @@
         d_qkv = dqkv_ref[token_rows(i), :]
         normed_wide, unit, inverse = normalize(x, gain1_ref[...])
         d_weight = dot(normed_wide.astype(jnp.bfloat16), d_qkv, ((0,), (0,)))
-        for n in range(3):
-            acc_ref[n] += d_weight[:, n * channels : (n + 1) * channels]
+        for n in range(3 * halves):
+            acc_ref[n] += d_weight[:, n * LANES : (n + 1) * LANES]
         d_unit = dot(d_qkv, wqkv_ref[...], ((1,), (1,))) * gain1_ref[...]
         grad = gather_groups(gs_ref, rows) + inverse * (
             d_unit
@@ -243,18 +274,43 @@
         )
         scatter_groups(grad_ref, rows, grad)
 
-    repeat(BLOCK // DENSE, project)
-    repeat(BLOCK // UNROLL, attend)
-    repeat(BLOCK // DENSE, finish)
-    store_tokens(out_ref, grad_ref)
-
-    last = (pl.program_id(0) == pl.num_programs(0) - 1) & (
-        pl.program_id(1) == pl.num_programs(1) - 1
-    )
-
-    @pl.when(last)
+    project(0)
+    project(1)
+    attend(0)
+    attend(1)
+    finish(0)
+    finish(1)
+
+    def send(n, j):
+        rows = pl.ds(j * positions + n % steps * BLOCK, BLOCK)
+        return pltpu.make_async_copy(
+            stage_ref.at[n % 2, j], out_ref.at[:, n // steps, :, rows, :], sent.at[n % 2, j]
+        )
+
+    @pl.when(turn >= 2)
     def _():
-        partial_ref[...] = acc_ref[...].reshape(partial_ref.shape).astype(jnp.bfloat16)
+        for j in range(halves):
+            send(turn - 2, j).wait()
+
+    for j in range(halves):
+        wide = grad_ref[j].reshape(GRID, GRID, BLOCK, LANES)
+        stage_ref[turn % 2, j] = wide.astype(jnp.bfloat16)
+        send(turn, j).start()
+
+    @pl.when(turn == last)
+    def _():
+        pieces_ref[...] = acc_ref[...].reshape(pieces_ref.shape).astype(jnp.bfloat16)
+        tail = pltpu.make_async_copy(
+            pieces_ref,
+            out_ref.at[:, :, :, pl.ds(halves * positions, pieces_ref.shape[3]), :],
+            sent_pieces,
+        )
+        tail.start()
+        for j in range(halves):
+            send(turn - 1, j).wait()
+        for j in range(halves):
+            send(turn, j).wait()
+        tail.wait()
 
 
 def specs(data):
@@ -270,15 +326,15 @@
 PARAMS = pltpu.CompilerParams(vmem_limit_bytes=VMEM_LIMIT)
 
 
-def forward(data, gain1, wqkv, wout, bias, gain2, wup, wdown, mask, width):
+def forward(data, gain1, wqkv, wout, pos_bias, gain2, wup, wdown, width):
     grid, block, whole, flat, groups = specs(data)
     channels = data.shape[-1]
     halves = channels // LANES
     tokens = MEMBERS * BLOCK
     count = groups * MEMBERS
     ff = wup.shape[1]
-    row_width = mask.shape[0]
-    weights = (gain1, wqkv, wout, bias, gain2, wup, wdown, mask)
+    row_width = LANES // width * MEMBERS
+    weights = (gain1, wqkv, wout, pos_bias, gain2, wup, wdown)
     return pl.pallas_call(
         functools.partial(forward_kernel, width),
         grid=grid,
@@ -295,7 +351,11 @@
             jax.ShapeDtypeStruct((count * halves, row_width), jnp.bfloat16),
             jax.ShapeDtypeStruct((count, channels), jnp.bfloat16),
         ],
-        scratch_shapes=[pltpu.VMEM((halves, tokens, LANES), jnp.float32)] * 2,
+        scratch_shapes=[pltpu.VMEM((halves, tokens, LANES), jnp.float32)] * 2
+        + [
+            pltpu.VMEM((row_width, LANES), jnp.bfloat16),
+            pltpu.VMEM((halves, MEMBERS, row_width), jnp.float32),
+        ],
         compiler_params=PARAMS,
         cost_estimate=pl.CostEstimate(
             flops=count * 2 * channels * (16 * channels + 2 * ff),
@@ -305,13 +365,18 @@
     )(data, *weights)
 
 
-def backward(data, cot, qkv, probs, context, gain1, wqkv, wout, mask, width):
+def backward(data, cot, qkv, probs, context, gain1, wqkv, wout, width):
     grid, block, whole, flat, groups = specs(data)
     channels = data.shape[-1]
     halves = channels // LANES
     tokens = MEMBERS * BLOCK
     count = groups * MEMBERS
-    weights = (gain1, wqkv, wout, mask)
+    row_width = LANES // width * MEMBERS
+    devices = GRID * GRID * data.shape[1]
+    positions = data.shape[3]
+    piece = 4 * halves * channels // devices
+    rows = halves * positions + piece
+    weights = (gain1, wqkv, wout)
     return pl.pallas_call(
         functools.partial(backward_kernel, width),
         grid=grid,
@@ -319,23 +384,22 @@
             block,
             block,
             flat(tokens, 3 * channels),
-            flat(tokens * halves, mask.shape[0]),
+            flat(tokens * halves, row_width),
             flat(tokens, channels),
         ]
         + [whole(a) for a in weights],
-        out_specs=[
-            block,
-            pl.BlockSpec((4 * channels, channels), lambda c, p: (0, 0)),
-        ],
-        out_shape=[
-            jax.ShapeDtypeStruct(data.shape, jnp.bfloat16),
-            jax.ShapeDtypeStruct((4 * channels, channels), jnp.bfloat16),
-        ],
-        scratch_shapes=[pltpu.VMEM((4, channels, channels), jnp.float32)]
+        out_specs=pl.BlockSpec(memory_space=pl.ANY),
+        out_shape=jax.ShapeDtypeStruct(data.shape[:3] + (rows, LANES), jnp.bfloat16),
+        scratch_shapes=[pltpu.VMEM((4 * halves, channels, LANES), jnp.float32)]
         + [pltpu.VMEM((halves, tokens, LANES), jnp.float32)] * 3
         + [
             pltpu.VMEM((tokens, channels), jnp.bfloat16),
             pltpu.VMEM((tokens, 3 * channels), jnp.bfloat16),
+            pltpu.VMEM((row_width, LANES), jnp.bfloat16),
+            pltpu.VMEM((2, halves, GRID, GRID, BLOCK, LANES), jnp.bfloat16),
+            pltpu.VMEM(data.shape[:3] + (piece, LANES), jnp.bfloat16),
+            pltpu.SemaphoreType.DMA((2, halves)),
+            pltpu.SemaphoreType.DMA,
         ],
         compiler_params=PARAMS,
         cost_estimate=pl.CostEstimate(
@@ -344,30 +408,6 @@
             transcendentals=0,
         ),
     )(data, cot, qkv, probs, context, *weights)
-
-
-def run_kernel(data, gain1, wqkv, wout, pos_bias, gain2, wup, wdown):
-    gain1, gain2, bias, mask, width = prepared(gain1, gain2, pos_bias, data.shape[-1])
-    tokens, cot = data[:, :, :, 0], data[:, :, :, 1]
-    mixed, qkv, probs, context = forward(
-        tokens, gain1, wqkv, wout, bias, gain2, wup, wdown, mask, width
-    )
-    grad, p = backward(tokens, cot, qkv, probs, context, gain1, wqkv, wout, mask, width)
-    p = p.astype(jnp.float32).reshape(4, 256, 256)
-    return jnp.stack([mixed, grad], axis=3), jnp.concatenate([p[0], p[1], p[2]], axis=1), p[3]
-
-
-def prepared(gain1, gain2, pos_bias, channels):
-    heads, members, _ = pos_bias.shape
-    width = channels // heads
-    per = LANES // width
-    halves = channels // LANES
-    bias = (pos_bias * LOG2E).transpose(2, 0, 1).reshape(members, halves, per * members)
-    bias = bias.transpose(1, 0, 2)
-    row_head = lax.broadcasted_iota(jnp.int32, (per * members, LANES), 0) // members
-    lane_head = lax.broadcasted_iota(jnp.int32, (per * members, LANES), 1) // width
-    mask = (row_head == lane_head).astype(jnp.bfloat16)
-    return gain1.reshape(1, -1), gain2.reshape(1, -1), bias, mask, width
 
 
 def place_kernel(source_ref, out_ref):
@@ -389,6 +429,39 @@
     )(values)
 
 
+def join_kernel(halves, source_ref, out_ref):
+    rows, columns, channels = out_ref.shape
+    devices = source_ref.shape[0]
+    positions = rows * columns // devices
+    for j in range(halves):
+        part = source_ref[:, j * positions : (j + 1) * positions, :]
+        out_ref[:, :, j * LANES : (j + 1) * LANES] = part.reshape(rows, columns, LANES)
+
+
+def joined_halves(values, shape):
+    rows, columns, channels = shape
+    devices, height, _ = values.shape
+    return pl.pallas_call(
+        functools.partial(join_kernel, channels // LANES),
+        grid=(4,),
+        in_specs=[pl.BlockSpec((devices // 4, height, LANES), lambda i: (i, 0, 0))],
+        out_specs=pl.BlockSpec((rows // 4, columns, channels), lambda i: (i, 0, 0)),
+        out_shape=jax.ShapeDtypeStruct(shape, values.dtype),
+        cost_estimate=pl.CostEstimate(
+            flops=0, bytes_accessed=4 * values.size, transcendentals=0
+        ),
+    )(values)
+
+
+def by_blocks(pieces, channels):
+    blocks = pieces.astype(jnp.float32).reshape(-1, channels, LANES)
+    split = 3 * channels // LANES
+    return (
+        jnp.concatenate([blocks[n] for n in range(split)], axis=1),
+        jnp.concatenate([blocks[n] for n in range(split, blocks.shape[0])], axis=1),
+    )
+
+
 def exchange(pieces):
     return lax.all_to_all(pieces, AXES, 0, 0, tiled=True)
 
@@ -399,29 +472,25 @@
     classes = lax.axis_size("gy") // GRID
     positions = tile_rows * tile_cols // devices
     factor = 1.0 / math.sqrt(tile_rows * tile_cols * devices)
-    gain1, gain2, bias, mask, width = prepared(norm1_gain, norm2_gain, pos_bias, channels)
+    width = channels // pos_bias.shape[0]
+    own = positions * channels // LANES
+    gain1, gain2 = norm1_gain.reshape(1, -1), norm2_gain.reshape(1, -1)
     sent = (devices, positions, channels)
     kept = (GRID, classes, GRID, positions, channels)
 
     data = exchange(tokens.reshape(sent)).reshape(kept)
     cot = exchange(cotangent.reshape(sent)).reshape(kept)
     mixed, qkv, probs, context = forward(
-        data, gain1, w_qkv, w_out, bias, gain2, w_up, w_down, mask, width
+        data, gain1, w_qkv, w_out, pos_bias, gain2, w_up, w_down, width
     )
     mixed = exchange(mixed.reshape(sent)).reshape(tokens.shape)
-    grad, partial = backward(
-        data, cot, qkv, probs, context, gain1, w_qkv, w_out, mask, width
-    )
-    pieces = partial.reshape(devices, -1, channels)
-    joined = jnp.concatenate([grad.reshape(sent), pieces], axis=1)
-    joined, mixed = lax.optimization_barrier((joined, mixed))
-    joined = exchange(joined)
-    total = jnp.sum(joined[:, positions:].astype(jnp.float32), axis=0) * factor
-    total = exchange(jnp.broadcast_to(total.astype(jnp.bfloat16)[None], pieces.shape))
-    blocks = total.astype(jnp.float32).reshape(4, channels, channels)
-    grad_qkv = jnp.concatenate([blocks[0], blocks[1], blocks[2]], axis=1)
-    grad_tokens = joined[:, :positions].reshape(tokens.shape)
-    return (placed(mixed), grad_tokens, grad_qkv, blocks[3])
+    grad = backward(data, cot, qkv, probs, context, gain1, w_qkv, w_out, width)
+    grad, mixed = lax.optimization_barrier((grad.reshape(devices, -1, LANES), mixed))
+    grad = exchange(grad)
+    total = jnp.sum(grad[:, own:].astype(jnp.float32), axis=0) * factor
+    total = jnp.broadcast_to(total.astype(jnp.bfloat16)[None], (devices,) + total.shape)
+    grad_qkv, grad_out = by_blocks(exchange(total), channels)
+    return (placed(mixed), joined_halves(grad, tokens.shape), grad_qkv, grad_out)
 
 
 def solution(mesh):

time: 178 us -> 173 us (0.972)
  waiting for transfers between devices: 12 us -> 18.2 us
  other arithmetic: 5.45 us -> 0.86 us
  starting transfers between devices: 19.6 us -> 16.6 us
  blocking collectives: 82.8 us -> 80.5 us
  local copies, waits for them, and re-layouts: 3.99 us -> 2.06 us
    all_to_all x3, waiting for transfers between devices: 12 us -> 18.2 us  [exchange(): return lax.all_to_all(pieces, AXES, 0, 0, tiled=True)]
    pallas_call x0 -> x1, Pallas kernels: none -> 3.99 us  [joined_halves(): pl.pallas_call(functools.partial(join_kernel, channels // LANES), grid=(4...]
    concatenate x2 -> x1, other arithmetic: 4.4 us -> 0.72 us  [by_blocks(): jnp.concatenate([blocks[n] for n in range(split, blocks.shape[0])], axis=1)]
    all_to_all x3, starting transfers between devices: 19.6 us -> 16.6 us  [exchange(): return lax.all_to_all(pieces, AXES, 0, 0, tiled=True)]
    all_to_all x2, blocking collectives: 82.8 us -> 80.5 us  [exchange(): return lax.all_to_all(pieces, AXES, 0, 0, tiled=True)]
  transfers between devices with their start and end apart: 3 -> 3, of which waited for: 3 -> 3; matrix products, arithmetic and copies ran while one was open for 4% -> 0% of each run, Pallas kernels for 30% -> 31%
where the time goes in v4:
time: 173 us; the launch traced here: 172 us
  blocking collectives  80.5 us (47%)
  Pallas kernels  53.1 us (31%)
  waiting for transfers between devices  18.2 us (11%)
  starting transfers between devices  16.6 us (10%)
  local copies, waits for them, and re-layouts  2.06 us (1%)
    all_to_all x2, blocking collectives, exchange(): return lax.all_to_all(pieces, AXES, 0, 0, tiled=True)  80.5 us
    pallas_call x1, Pallas kernels, forward(): pl.pallas_call(functools.partial(forward_kernel, width), grid=grid, in_sp...  24 us
    pallas_call x1, Pallas kernels, backward(): pl.pallas_call(functools.partial(backward_kernel, width), grid=grid, in_s...  21.4 us
    all_to_all x3, waiting for transfers between devices, exchange(): return lax.all_to_all(pieces, AXES, 0, 0, tiled=True)  18.2 us
    all_to_all x3, starting transfers between devices, exchange(): return lax.all_to_all(pieces, AXES, 0, 0, tiled=True)  16.6 us
    pallas_call x1, Pallas kernels, joined_halves(): pl.pallas_call(functools.partial(join_kernel, channels // LANES), grid=(4...  3.99 us
    pallas_call x1, Pallas kernels, placed(): pl.pallas_call(place_kernel, grid=(4,), in_specs=[block], out_specs=block...  3.78 us
  transfers between devices with their start and end apart: 3, of which 3 were waited for; matrix products, arithmetic and copies ran while one was open for 0% of the time, Pallas kernels for 31%

profile of v4, /device:TPU:0, one launch (start us, length us, event | category | flops | bytes accessed | tf_op | source)
XLA Modules:
  0.0 172.2 jit_solution(12190377385558016575)
XLA Ops:
  0.6 40.7 %all_to_all.25 = bf16[128,32,256]{2,1,0:T(8,128)(2,1)} all-to-all(bf16[128,32,256]{2,1,0:T(8,128)(2,1)} %bitcast.18), channel_id=1, replica_groups=mesh['gy'=16,'gx'=8] {'gy','gx'}, dimensions={0} | all-to-all | bytes 4194304 | tf_op jit(solution)/shard_map/all_to_all | solution.py:466
  41.3 5.8 %all-to-all-start.1 = ((bf16[128,32,256]{2,1,0:T(8,128)(2,1)}), bf16[128,32,256]{2,1,0:T(8,128)(2,1)}, u32[]{:S(2)}, u32[]{:S(2)}) async-start(bf16[128,32,256]{2,1,0:T(8,128)(2,1)} %bitcast.2), calls=%async_computation.1 | async-start | bytes 4194304 | tf_op jit(solution)/shard_map/all_to_all | solution.py:466
  47.1 24.0 %shard_map.120 = (bf16[8,2,8,32,256]{4,3,2,1,0:T(8,128)(2,1)}, bf16[4096,768]{1,0:T(8,128)(2,1)}, bf16[8192,256]{1,0:T(8,128)(2,1)}, bf16[4096,256]{1,0:T(8,128)(2,1)}) custom-call(bf16[8,2,8,32,256]{4,3,2,1,0:T(8,128)(2,1)} %bitcast.19, f32[1,256]{1,0:T(1,128)} %bitcast.31, bf16[256,768]{1,0:T(8,128)(2,1)} %wqkv_ref.3, bf16[256,256]{1,0:T(8,128)(2,1)} %wout_ref.3, ...), custom_call_target="tpu_custom_call" | custom-call | flops 12884901888 | bytes 16777216 | tf_op jit(solution)/shard_map/pallas_call | solution.py:338
  71.1 5.1 %all-to-all-done.1 = bf16[128,32,256]{2,1,0:T(8,128)(2,1)} async-done(((bf16[128,32,256]{2,1,0:T(8,128)(2,1)}), bf16[128,32,256]{2,1,0:T(8,128)(2,1)}, u32[]{:S(2)}, u32[]{:S(2)}) %all-to-all-start.1) | async-done | bytes 2097184 | tf_op jit(solution)/shard_map/all_to_all | solution.py:466
  76.1 5.8 %all-to-all-start.2 = ((bf16[128,32,256]{2,1,0:T(8,128)(2,1)}), bf16[128,32,256]{2,1,0:T(8,128)(2,1)}, u32[]{:S(2)}, u32[]{:S(2)}) async-start(bf16[128,32,256]{2,1,0:T(8,128)(2,1)} %bitcast.21), calls=%async_computation.2 | async-start | bytes 4194304 | tf_op jit(solution)/shard_map/all_to_all | solution.py:466
  81.9 21.4 %shard_map.121 = bf16[8,2,8,80,128]{4,3,2,1,0:T(8,128)(2,1)} custom-call(bf16[8,2,8,32,256]{4,3,2,1,0:T(8,128)(2,1)} %bitcast.20, bf16[8,2,8,32,256]{4,3,2,1,0:T(8,128)(2,1)} %bitcast.3.cot_ref, bf16[4096,768]{1,0:T(8,128)(2,1)} %get-tuple-element.10.qkv_ref, bf16[8192,256]{1,0:T(8,128)(2,1)} %get-tuple-element.11.probs_ref, ...), custom_call_target="tpu_custom_call" | custom-call | flops 12884901888 | bytes 20971520 | tf_op jit(solution)/shard_map/pallas_call | solution.py:380
  103.3 7.6 %all-to-all-done.2 = bf16[128,32,256]{2,1,0:T(8,128)(2,1)} async-done(((bf16[128,32,256]{2,1,0:T(8,128)(2,1)}), bf16[128,32,256]{2,1,0:T(8,128)(2,1)}, u32[]{:S(2)}, u32[]{:S(2)}) %all-to-all-start.2) | async-done | bytes 2097184 | tf_op jit(solution)/shard_map/all_to_all | solution.py:466
  110.9 39.8 %all_to_all.26.source_ref = bf16[128,80,128]{2,1,0:T(8,128)(2,1)S(1)} all-to-all(bf16[128,80,128]{2,1,0:T(8,128)(2,1)} %bitcast.17), channel_id=1, replica_groups=mesh['gy'=16,'gx'=8] {'gy','gx'}, dimensions={0} | all-to-all | bytes 5242880 | tf_op jit(solution)/shard_map/all_to_all | solution.py:466
  150.7 0.0 copy-start
  150.7 0.1 convert_reduce_fusion
  150.8 1.0 broadcast_in_dim.2
  151.9 5.1 %all-to-all-start.4 = ((bf16[128,16,128]{2,1,0:T(8,128)(2,1)}), bf16[128,16,128]{2,1,0:T(8,128)(2,1)S(1)}, u32[]{:S(2)}, u32[]{:S(2)}) async-start(bf16[128,16,128]{2,1,0:T(8,128)(2,1)} %broadcast_in_dim.2), calls=%async_computation.4 | async-start | bytes 1048576 | tf_op jit(solution)/shard_map/all_to_all | solution.py:466
  157.0 3.8 %shard_map.122 = bf16[32,128,256]{2,1,0:T(8,128)(2,1)} custom-call(bf16[32,128,256]{2,1,0:T(8,128)(2,1)} %bitcast.8.source_ref), custom_call_target="tpu_custom_call" | custom-call | bytes 4194304 | tf_op jit(solution)/shard_map/pallas_call | solution.py:420
  160.7 0.0 copy-done
  160.7 4.0 %shard_map.123 = bf16[32,128,256]{2,1,0:T(8,128)(2,1)} custom-call(bf16[128,80,128]{2,1,0:T(8,128)(2,1)} %copy-done), custom_call_target="tpu_custom_call" | custom-call | bytes 5242880 | tf_op jit(solution)/shard_map/pallas_call | solution.py:444
  164.7 5.6 %all-to-all-done.4 = bf16[128,16,128]{2,1,0:T(8,128)(2,1)S(1)} async-done(((bf16[128,16,128]{2,1,0:T(8,128)(2,1)}), bf16[128,16,128]{2,1,0:T(8,128)(2,1)S(1)}, u32[]{:S(2)}, u32[]{:S(2)}) %all-to-all-start.4) | async-done | bytes 524320 | tf_op jit(solution)/shard_map/all_to_all | solution.py:466
  170.3 0.1 fusion
  170.5 0.7 pad_maximum_fusion
  171.3 0.0 copy-start.1
  171.3 0.9 copy-done.1
  (7 shorter events, 0.1 us)
Async XLA Ops:
  41.3 34.8 %all-to-all-start.1 = ((bf16[128,32,256]{2,1,0:T(8,128)(2,1)}), bf16[128,32,256]{2,1,0:T(8,128)(2,1)}, u32[]{:S(2)}, u32[]{:S(2)}) async-start(bf16[128,32,256]{2,1,0:T(8,128)(2,1)} %bitcast.2), calls=%async_computation.1 | async-start | bytes 4194304 | tf_op jit(solution)/shard_map/all_to_all | solution.py:466
  76.1 34.8 %all-to-all-start.2 = ((bf16[128,32,256]{2,1,0:T(8,128)(2,1)}), bf16[128,32,256]{2,1,0:T(8,128)(2,1)}, u32[]{:S(2)}, u32[]{:S(2)}) async-start(bf16[128,32,256]{2,1,0:T(8,128)(2,1)} %bitcast.21), calls=%async_computation.2 | async-start | bytes 4194304 | tf_op jit(solution)/shard_map/all_to_all | solution.py:466
  150.7 10.1 %copy-start = (bf16[128,80,128]{2,1,0:T(8,128)(2,1)}, bf16[128,80,128]{2,1,0:T(8,128)(2,1)S(1)}, u32[]{:S(2)}) copy-start(bf16[128,80,128]{2,1,0:T(8,128)(2,1)S(1)} %all_to_all.26.source_ref) | copy-start | bytes 7864324
  151.9 18.5 %all-to-all-start.4 = ((bf16[128,16,128]{2,1,0:T(8,128)(2,1)}), bf16[128,16,128]{2,1,0:T(8,128)(2,1)S(1)}, u32[]{:S(2)}, u32[]{:S(2)}) async-start(bf16[128,16,128]{2,1,0:T(8,128)(2,1)} %broadcast_in_dim.2), calls=%async_computation.4 | async-start | bytes 1048576 | tf_op jit(solution)/shard_map/all_to_all | solution.py:466
  171.3 0.9 copy-start.1

commit v5 on v4

--- a/solution.py
+++ b/solution.py
@@ -9,6 +9,7 @@
 from jax.sharding import PartitionSpec as P
 
 GRID = 8
+CORES = 2
 MEMBERS = GRID * GRID
 EPSILON = 1e-05
 LOG2E = math.log2(math.e)
@@ -17,7 +18,7 @@
 BLOCK = 16
 DENSE = 8
 UNROLL = 8
-VMEM_LIMIT = 62 * 1024 * 1024 + 512 * 1024
+VMEM_LIMIT = 36 * 1024 * 1024
 
 
 def dot(a, b, contract=((1,), (0,))):
@@ -182,6 +183,7 @@
 
 def backward_kernel(
     width,
+    core_ref,
     data_ref,
     cot_ref,
     qkv_ref,
@@ -191,6 +193,8 @@
     wqkv_ref,
     wout_ref,
     out_ref,
+    own_ref,
+    other_ref,
     acc_ref,
     xs_ref,
     gs_ref,
@@ -199,9 +203,7 @@
     dqkv_ref,
     mask_ref,
     stage_ref,
-    pieces_ref,
     sent,
-    sent_pieces,
 ):
     channels = wout_ref.shape[0]
     halves = channels // LANES
@@ -211,7 +213,6 @@
     steps = pl.num_programs(1)
     turn = pl.program_id(0) * steps + pl.program_id(1)
     last = pl.num_programs(0) * steps - 1
-    positions = steps * BLOCK
 
     @pl.when(turn == 0)
     def _():
@@ -226,9 +227,7 @@
         here = token_rows(i)
         cot = gather_groups(gs_ref, group_rows(i)).astype(jnp.bfloat16)
         dctx_ref[here, :] = dot(cot, wout_ref[...], ((1,), (1,))).astype(jnp.bfloat16)
-        d_weight = dot(context_ref[here, :], cot, ((0,), (0,)))
-        for n in range(halves):
-            acc_ref[3 * halves + n] += d_weight[:, n * LANES : (n + 1) * LANES]
+        acc_ref[3] += dot(context_ref[here, :], cot, ((0,), (0,)))
 
     def attend(i):
         units = []
@@ -251,6 +250,7 @@
         for (part, at, slot), dp in zip(units, d_probs):
             probs = probs_ref[slot, :].astype(jnp.float32)
             delta = jnp.sum(probs * dp, axis=0, keepdims=True)
+            delta = delta / jnp.sum(probs, axis=0, keepdims=True)
             d_scaled.append((probs * (dp - delta) * scale).astype(jnp.bfloat16))
         for (part, at, slot), ds in zip(units, d_scaled):
             q_heads = jnp.concatenate([qkv_ref[part, at : at + LANES]] * per, axis=0) * mask_ref[...]
@@ -264,8 +264,8 @@
         d_qkv = dqkv_ref[token_rows(i), :]
         normed_wide, unit, inverse = normalize(x, gain1_ref[...])
         d_weight = dot(normed_wide.astype(jnp.bfloat16), d_qkv, ((0,), (0,)))
-        for n in range(3 * halves):
-            acc_ref[n] += d_weight[:, n * LANES : (n + 1) * LANES]
+        for n in range(3):
+            acc_ref[n] += d_weight[:, n * channels : (n + 1) * channels]
         d_unit = dot(d_qkv, wqkv_ref[...], ((1,), (1,))) * gain1_ref[...]
         grad = gather_groups(gs_ref, rows) + inverse * (
             d_unit
@@ -281,36 +281,39 @@
     finish(0)
     finish(1)
 
-    def send(n, j):
-        rows = pl.ds(j * positions + n % steps * BLOCK, BLOCK)
+    def send(n):
+        rows = pl.ds(n % steps * BLOCK, BLOCK)
         return pltpu.make_async_copy(
-            stage_ref.at[n % 2, j], out_ref.at[:, n // steps, :, rows, :], sent.at[n % 2, j]
+            stage_ref.at[n % 2], out_ref.at[:, n // steps, :, rows, :], sent.at[n % 2]
         )
 
     @pl.when(turn >= 2)
     def _():
-        for j in range(halves):
-            send(turn - 2, j).wait()
+        send(turn - 2).wait()
 
     for j in range(halves):
         wide = grad_ref[j].reshape(GRID, GRID, BLOCK, LANES)
-        stage_ref[turn % 2, j] = wide.astype(jnp.bfloat16)
-        send(turn, j).start()
+        stage_ref[turn % 2, :, :, :, j * LANES : (j + 1) * LANES] = wide.astype(jnp.bfloat16)
+    send(turn).start()
 
     @pl.when(turn == last)
     def _():
-        pieces_ref[...] = acc_ref[...].reshape(pieces_ref.shape).astype(jnp.bfloat16)
-        tail = pltpu.make_async_copy(
-            pieces_ref,
-            out_ref.at[:, :, :, pl.ds(halves * positions, pieces_ref.shape[3]), :],
-            sent_pieces,
-        )
-        tail.start()
-        for j in range(halves):
-            send(turn - 1, j).wait()
-        for j in range(halves):
-            send(turn, j).wait()
-        tail.wait()
+        count = own_ref.shape[0] // GRID
+        halved = acc_ref[...].reshape(GRID, CORES, count, channels).astype(jnp.bfloat16)
+        first, second = (halved[:, c].reshape(own_ref.shape) for c in range(CORES))
+
+        @pl.when(core_ref[0] == 0)
+        def _():
+            own_ref[...] = first
+            other_ref[...] = second
+
+        @pl.when(core_ref[0] == 1)
+        def _():
+            own_ref[...] = second
+            other_ref[...] = first
+
+        send(turn - 1).wait()
+        send(turn).wait()
 
 
 def specs(data):
@@ -346,10 +349,10 @@
             flat(tokens, channels),
         ],
         out_shape=[
-            jax.ShapeDtypeStruct(data.shape, jnp.bfloat16),
-            jax.ShapeDtypeStruct((count, 3 * channels), jnp.bfloat16),
-            jax.ShapeDtypeStruct((count * halves, row_width), jnp.bfloat16),
-            jax.ShapeDtypeStruct((count, channels), jnp.bfloat16),
+            pltpu.VMEM(data.shape, jnp.bfloat16),
+            pltpu.HBM((count, 3 * channels), jnp.bfloat16),
+            pltpu.HBM((count * halves, row_width), jnp.bfloat16),
+            pltpu.HBM((count, channels), jnp.bfloat16),
         ],
         scratch_shapes=[pltpu.VMEM((halves, tokens, LANES), jnp.float32)] * 2
         + [
@@ -365,22 +368,25 @@
     )(data, *weights)
 
 
-def backward(data, cot, qkv, probs, context, gain1, wqkv, wout, width):
+def backward(core, data, cot, qkv, probs, context, gain1, wqkv, wout, width):
     grid, block, whole, flat, groups = specs(data)
     channels = data.shape[-1]
     halves = channels // LANES
     tokens = MEMBERS * BLOCK
     count = groups * MEMBERS
     row_width = LANES // width * MEMBERS
-    devices = GRID * GRID * data.shape[1]
-    positions = data.shape[3]
-    piece = 4 * halves * channels // devices
-    rows = halves * positions + piece
+    rows = data.shape[3] + 4 * channels // (GRID * CORES * GRID)
+    pieces = (4 * channels // CORES, channels)
+    qkv, probs, context = (
+        pltpu.with_memory_space_constraint(a, pltpu.HBM) for a in (qkv, probs, context)
+    )
+    cot = pltpu.with_memory_space_constraint(cot, pltpu.HBM)
     weights = (gain1, wqkv, wout)
     return pl.pallas_call(
         functools.partial(backward_kernel, width),
         grid=grid,
         in_specs=[
+            pl.BlockSpec(memory_space=pltpu.SMEM),
             block,
             block,
             flat(tokens, 3 * channels),
@@ -388,18 +394,24 @@
             flat(tokens, channels),
         ]
         + [whole(a) for a in weights],
-        out_specs=pl.BlockSpec(memory_space=pl.ANY),
-        out_shape=jax.ShapeDtypeStruct(data.shape[:3] + (rows, LANES), jnp.bfloat16),
-        scratch_shapes=[pltpu.VMEM((4 * halves, channels, LANES), jnp.float32)]
+        out_specs=[
+            pl.BlockSpec(memory_space=pl.ANY),
+            pl.BlockSpec(pieces, lambda c, p: (0, 0)),
+            pl.BlockSpec(pieces, lambda c, p: (0, 0)),
+        ],
+        out_shape=[
+            pltpu.VMEM(data.shape[:3] + (rows, channels), jnp.bfloat16),
+            jax.ShapeDtypeStruct(pieces, jnp.bfloat16),
+            jax.ShapeDtypeStruct(pieces, jnp.bfloat16),
+        ],
+        scratch_shapes=[pltpu.VMEM((4, channels, channels), jnp.float32)]
         + [pltpu.VMEM((halves, tokens, LANES), jnp.float32)] * 3
         + [
             pltpu.VMEM((tokens, channels), jnp.bfloat16),
             pltpu.VMEM((tokens, 3 * channels), jnp.bfloat16),
             pltpu.VMEM((row_width, LANES), jnp.bfloat16),
-            pltpu.VMEM((2, halves, GRID, GRID, BLOCK, LANES), jnp.bfloat16),
-            pltpu.VMEM(data.shape[:3] + (piece, LANES), jnp.bfloat16),
-            pltpu.SemaphoreType.DMA((2, halves)),
-            pltpu.SemaphoreType.DMA,
+            pltpu.VMEM((2, GRID, GRID, BLOCK, channels), jnp.bfloat16),
+            pltpu.SemaphoreType.DMA((2,)),
         ],
         compiler_params=PARAMS,
         cost_estimate=pl.CostEstimate(
@@ -407,14 +419,14 @@
             bytes_accessed=2 * count * channels * 10,
             transcendentals=0,
         ),
-    )(data, cot, qkv, probs, context, *weights)
+    )(core, data, cot, qkv, probs, context, *weights)
 
 
 def place_kernel(source_ref, out_ref):
     out_ref[...] = source_ref[...]
 
 
-def placed(values):
+def placed(values, space=None):
     rows, columns, channels = values.shape
     block = pl.BlockSpec((rows // 4, columns, channels), lambda i: (i, 0, 0))
     return pl.pallas_call(
@@ -422,29 +434,27 @@
         grid=(4,),
         in_specs=[block],
         out_specs=block,
-        out_shape=jax.ShapeDtypeStruct(values.shape, values.dtype),
+        out_shape=(space or jax.ShapeDtypeStruct)(values.shape, values.dtype),
         cost_estimate=pl.CostEstimate(
             flops=0, bytes_accessed=4 * values.size, transcendentals=0
         ),
     )(values)
 
 
-def join_kernel(halves, source_ref, out_ref):
+def trim_kernel(source_ref, out_ref):
     rows, columns, channels = out_ref.shape
-    devices = source_ref.shape[0]
-    positions = rows * columns // devices
-    for j in range(halves):
-        part = source_ref[:, j * positions : (j + 1) * positions, :]
-        out_ref[:, :, j * LANES : (j + 1) * LANES] = part.reshape(rows, columns, LANES)
-
-
-def joined_halves(values, shape):
+    positions = rows * columns // source_ref.shape[0]
+    out_ref[...] = source_ref[:, :positions, :].reshape(out_ref.shape)
+
+
+def trimmed(values, shape):
     rows, columns, channels = shape
     devices, height, _ = values.shape
+    values = pltpu.with_memory_space_constraint(values, pltpu.VMEM)
     return pl.pallas_call(
-        functools.partial(join_kernel, channels // LANES),
+        trim_kernel,
         grid=(4,),
-        in_specs=[pl.BlockSpec((devices // 4, height, LANES), lambda i: (i, 0, 0))],
+        in_specs=[pl.BlockSpec((devices // 4, height, channels), lambda i: (i, 0, 0))],
         out_specs=pl.BlockSpec((rows // 4, columns, channels), lambda i: (i, 0, 0)),
         out_shape=jax.ShapeDtypeStruct(shape, values.dtype),
         cost_estimate=pl.CostEstimate(
@@ -453,44 +463,54 @@
     )(values)
 
 
-def by_blocks(pieces, channels):
-    blocks = pieces.astype(jnp.float32).reshape(-1, channels, LANES)
-    split = 3 * channels // LANES
-    return (
-        jnp.concatenate([blocks[n] for n in range(split)], axis=1),
-        jnp.concatenate([blocks[n] for n in range(split, blocks.shape[0])], axis=1),
-    )
-
-
-def exchange(pieces):
-    return lax.all_to_all(pieces, AXES, 0, 0, tiled=True)
-
-
 def local(tokens, cotangent, norm1_gain, w_qkv, w_out, pos_bias, norm2_gain, w_up, w_down):
     tile_rows, tile_cols, channels = tokens.shape
+    columns = lax.axis_size("gx")
     devices = lax.axis_size(AXES)
-    classes = lax.axis_size("gy") // GRID
-    positions = tile_rows * tile_cols // devices
+    core = lax.axis_index("gy") % CORES
+    positions = tile_rows * tile_cols // MEMBERS
     factor = 1.0 / math.sqrt(tile_rows * tile_cols * devices)
     width = channels // pos_bias.shape[0]
-    own = positions * channels // LANES
     gain1, gain2 = norm1_gain.reshape(1, -1), norm2_gain.reshape(1, -1)
-    sent = (devices, positions, channels)
-    kept = (GRID, classes, GRID, positions, channels)
+    sent = (MEMBERS, positions, channels)
+    kept = (GRID, 1, GRID, positions, channels)
+    def device(row, c, column):
+        return (row * CORES + c) * columns + column
+
+    members = [(row, column) for row in range(GRID) for column in range(GRID)]
+    peers = [[device(row, c, column) for row, column in members] for c in range(CORES)]
+    partner = [
+        (device(row, c, column), device(row, 1 - c, column))
+        for row, column in members
+        for c in range(CORES)
+    ]
+
+    def exchange(pieces):
+        return lax.all_to_all(pieces, AXES, 0, 0, axis_index_groups=peers, tiled=True)
 
     data = exchange(tokens.reshape(sent)).reshape(kept)
-    cot = exchange(cotangent.reshape(sent)).reshape(kept)
+    cot = exchange(placed(cotangent, pltpu.VMEM).reshape(sent)).reshape(kept)
     mixed, qkv, probs, context = forward(
         data, gain1, w_qkv, w_out, pos_bias, gain2, w_up, w_down, width
     )
     mixed = exchange(mixed.reshape(sent)).reshape(tokens.shape)
-    grad = backward(data, cot, qkv, probs, context, gain1, w_qkv, w_out, width)
-    grad, mixed = lax.optimization_barrier((grad.reshape(devices, -1, LANES), mixed))
+    grad, own_pieces, other_pieces = backward(
+        core.reshape(1), data, cot, qkv, probs, context, gain1, w_qkv, w_out, width
+    )
+    pair = own_pieces.astype(jnp.float32) + lax.ppermute(
+        other_pieces, AXES, partner
+    ).astype(jnp.float32)
+    pair = pair.astype(jnp.bfloat16).reshape(GRID, 1, GRID, -1, channels)
+    grad = lax.dynamic_update_slice(grad, pair, (0, 0, 0, positions, 0))
+    grad, mixed = lax.optimization_barrier((grad.reshape(MEMBERS, -1, channels), mixed))
     grad = exchange(grad)
-    total = jnp.sum(grad[:, own:].astype(jnp.float32), axis=0) * factor
+    total = jnp.sum(grad[:, positions:].astype(jnp.float32), axis=0) * factor
     total = jnp.broadcast_to(total.astype(jnp.bfloat16)[None], (devices,) + total.shape)
-    grad_qkv, grad_out = by_blocks(exchange(total), channels)
-    return (placed(mixed), joined_halves(grad, tokens.shape), grad_qkv, grad_out)
+    total, grad = lax.optimization_barrier((total, grad))
+    total = lax.all_to_all(total, AXES, 0, 0, tiled=True)
+    blocks = total.astype(jnp.float32).reshape(4, channels, channels)
+    grad_qkv = jnp.concatenate([blocks[0], blocks[1], blocks[2]], axis=1)
+    return (placed(mixed), trimmed(grad, tokens.shape), grad_qkv, blocks[3])
 
 
 def solution(mesh):

time: 173 us -> 170 us (0.983)
  blocking collectives: 80.5 us -> 38.1 us
  waiting for transfers between devices: 18.2 us -> 43.4 us
  starting transfers between devices: 16.6 us -> 28.8 us
    all_to_all x2 -> x1, blocking collectives: 80.5 us -> 38.1 us  [exchange(): lax.all_to_all(pieces, AXES, 0, 0, axis_index_groups=peers, tiled=True)]
    all_to_all x3 -> x4, waiting for transfers between devices: 18.2 us -> 41.9 us  [the longest x3 34.3 us: exchange(): lax.all_to_all(pieces, AXES, 0, 0, axis_index_groups=peers, tiled=True)]
    all_to_all x3 -> x4, starting transfers between devices: 16.6 us -> 28.7 us  [the longest x3 24.1 us: exchange(): lax.all_to_all(pieces, AXES, 0, 0, axis_index_groups=peers, tiled=True)]
    pallas_call x1 -> x2, Pallas kernels: 3.78 us -> 7.74 us  [placed(): pl.pallas_call(place_kernel, grid=(4,), in_specs=[block], out_specs=block...]
    pallas_call x1, Pallas kernels: 3.99 us -> 1.83 us  [trimmed(): pl.pallas_call(trim_kernel, grid=(4,), in_specs=[pl.BlockSpec((devices //...]
  transfers between devices with their start and end apart: 3 -> 5, of which waited for: 3 -> 5; matrix products, arithmetic and copies ran while one was open for 0% -> 0% of each run, Pallas kernels for 31% -> 32%
where the time goes in v5:
time: 170 us; the launch traced here: 169 us
  Pallas kernels  53.6 us (32%)
  waiting for transfers between devices  43.4 us (26%)
  blocking collectives  38.1 us (22%)
  starting transfers between devices  28.8 us (17%)
  local copies, waits for them, and re-layouts  3.08 us (2%)
    all_to_all x1, blocking collectives, exchange(): lax.all_to_all(pieces, AXES, 0, 0, axis_index_groups=peers, tiled=True)  38.1 us
    all_to_all x3, waiting for transfers between devices, exchange(): lax.all_to_all(pieces, AXES, 0, 0, axis_index_groups=peers, tiled=True)  34.3 us
    all_to_all x3, starting transfers between devices, exchange(): lax.all_to_all(pieces, AXES, 0, 0, axis_index_groups=peers, tiled=True)  24.1 us
    pallas_call x1, Pallas kernels, forward(): pl.pallas_call(functools.partial(forward_kernel, width), grid=grid, in_sp...  23.5 us
    pallas_call x1, Pallas kernels, backward(): pl.pallas_call(functools.partial(backward_kernel, width), grid=grid, in_s...  20.5 us
    pallas_call x2, Pallas kernels, placed(): pl.pallas_call(place_kernel, grid=(4,), in_specs=[block], out_specs=block...  7.74 us
    all_to_all x1, waiting for transfers between devices, local(): total = lax.all_to_all(total, AXES, 0, 0, tiled=True)  7.62 us
    all_to_all x1, starting transfers between devices, local(): total = lax.all_to_all(total, AXES, 0, 0, tiled=True)  4.62 us
  transfers between devices with their start and end apart: 5, of which 5 were waited for; matrix products, arithmetic and copies ran while one was open for 0% of the time, Pallas kernels for 32%

profile of v5, /device:TPU:0, one launch (start us, length us, event | category | flops | bytes accessed | tf_op | source)
XLA Modules:
  0.0 169.0 jit_solution(7777984641877980421)
XLA Ops:
  0.6 11.8 %all-to-all-start = ((bf16[64,64,256]{2,1,0:T(8,128)(2,1)}), bf16[64,64,256]{2,1,0:T(8,128)(2,1)}, u32[]{:S(2)}, u32[]{:S(2)}) async-start(bf16[64,64,256]{2,1,0:T(8,128)(2,1)} %bitcast.25), calls=%async_computation | async-start | bytes 4194304 | tf_op jit(solution)/shard_map/all_to_all | solution.py:489
  12.4 3.8 %shard_map.120 = bf16[32,128,256]{2,1,0:T(8,128)(2,1)} custom-call(bf16[32,128,256]{2,1,0:T(8,128)(2,1)} %source_ref.1), custom_call_target="tpu_custom_call" | custom-call | bytes 4194304 | tf_op jit(solution)/shard_map/pallas_call | solution.py:432
  16.2 25.0 %all-to-all-done = bf16[64,64,256]{2,1,0:T(8,128)(2,1)} async-done(((bf16[64,64,256]{2,1,0:T(8,128)(2,1)}), bf16[64,64,256]{2,1,0:T(8,128)(2,1)}, u32[]{:S(2)}, u32[]{:S(2)}) %all-to-all-start) | async-done | bytes 2097184 | tf_op jit(solution)/shard_map/all_to_all | solution.py:489
  41.2 0.0 copy-start.2
  41.2 0.0 copy-start.3
  41.2 0.0 copy-start.4
  41.2 0.0 copy-start.5
  41.2 0.0 copy-start.6
  41.2 0.0 copy-start.7
  41.2 0.0 copy-start.8
  41.2 6.1 %all-to-all-start.1 = ((bf16[64,64,256]{2,1,0:T(8,128)(2,1)}), bf16[64,64,256]{2,1,0:T(8,128)(2,1)}, u32[]{:S(2)}, u32[]{:S(2)}) async-start(bf16[64,64,256]{2,1,0:T(8,128)(2,1)} %bitcast.3), calls=%async_computation.1 | async-start | bytes 4194304 | tf_op jit(solution)/shard_map/all_to_all | solution.py:489
  47.4 0.0 copy-done.2
  47.4 0.0 copy-done.3
  47.4 0.0 copy-done.4
  47.4 0.0 copy-done.5
  47.4 0.0 copy-done.6
  47.4 0.0 copy-done.7
  47.4 0.0 copy-done.8
  47.4 23.5 %shard_map.121 = (bf16[8,1,8,64,256]{4,3,2,1,0:T(8,128)(2,1)}, bf16[4096,768]{1,0:T(8,128)(2,1)}, bf16[8192,256]{1,0:T(8,128)(2,1)}, bf16[4096,256]{1,0:T(8,128)(2,1)}) custom-call(bf16[8,1,8,64,256]{4,3,2,1,0:T(8,128)(2,1)} %bitcast.2.data_ref, f32[1,256]{1,0:T(1,128)S(1)} %bitcast.23, bf16[256,768]{1,0:T(8,128)(2,1)S(1)} %copy-done.4, ...), custom_call_target="tpu_custom_call" | custom-call | flops 12884901888 | bytes 16777216 | tf_op jit(solution)/shard_map/pallas_call | solution.py:341
  71.0 4.4 %all-to-all-done.1 = bf16[64,64,256]{2,1,0:T(8,128)(2,1)} async-done(((bf16[64,64,256]{2,1,0:T(8,128)(2,1)}), bf16[64,64,256]{2,1,0:T(8,128)(2,1)}, u32[]{:S(2)}, u32[]{:S(2)}) %all-to-all-start.1) | async-done | bytes 2097184 | tf_op jit(solution)/shard_map/all_to_all | solution.py:489
  75.3 6.2 %all-to-all-start.2 = ((bf16[64,64,256]{2,1,0:T(8,128)(2,1)}), bf16[64,64,256]{2,1,0:T(8,128)(2,1)}, u32[]{:S(2)}, u32[]{:S(2)}) async-start(bf16[64,64,256]{2,1,0:T(8,128)(2,1)} %bitcast.10), calls=%async_computation.2 | async-start | bytes 4194304 | tf_op jit(solution)/shard_map/all_to_all | solution.py:489
  81.6 20.5 %shard_map.122 = (bf16[8,1,8,72,256]{4,3,2,1,0:T(8,128)(2,1)S(1)}, bf16[512,256]{1,0:T(8,128)(2,1)S(1)}, bf16[512,256]{1,0:T(8,128)(2,1)S(1)}) custom-call(s32[1]{0:T(128)} %bitcast.core_ref, bf16[8,1,8,64,256]{4,3,2,1,0:T(8,128)(2,1)} %bitcast.2.data_ref, bf16[8,1,8,64,256]{4,3,2,1,0:T(8,128)(2,1)} %bitcast.4.cot_ref, ...), custom_call_target="tpu_custom_call" | custom-call | flops 12884901888 | bytes 20971520 | tf_op jit(solution)/shard_map/pallas_call | solution.py:385
  102.1 0.1 collective-permute-start
  102.2 1.5 collective-permute-done
  103.7 0.1 add_convert_fusion
  103.8 5.0 %all-to-all-done.2 = bf16[64,64,256]{2,1,0:T(8,128)(2,1)} async-done(((bf16[64,64,256]{2,1,0:T(8,128)(2,1)}), bf16[64,64,256]{2,1,0:T(8,128)(2,1)}, u32[]{:S(2)}, u32[]{:S(2)}) %all-to-all-start.2) | async-done | bytes 2097184 | tf_op jit(solution)/shard_map/all_to_all | solution.py:489
  108.8 38.1 %all_to_all.25.source_ref = bf16[64,72,256]{2,1,0:T(8,128)(2,1)S(1)} all-to-all(bf16[64,72,256]{2,1,0:T(8,128)(2,1)S(1)} %bitcast.21), channel_id=1, replica_groups={{0,1,2,3,4,5,6,7,16,17,18,19,20,21,22,23,32,33,34,35,36,37,38,39,48,49,..., dimensions={0} | all-to-all | bytes 4718592 | tf_op jit(solution)/shard_map/all_to_all | solution.py:489
  146.9 0.1 convert_reduce_fusion
  146.9 0.0 copy-start
  146.9 1.4 copy-done
  148.4 0.8 broadcast_in_dim.2
  149.2 4.6 %all-to-all-start.4 = ((bf16[128,8,256]{2,1,0:T(8,128)(2,1)}), bf16[128,8,256]{2,1,0:T(8,128)(2,1)S(1)}, u32[]{:S(2)}, u32[]{:S(2)}) async-start(bf16[128,8,256]{2,1,0:T(8,128)(2,1)} %broadcast_in_dim.2), calls=%async_computation.4 | async-start | bytes 1048576 | tf_op jit(solution)/shard_map/all_to_all | solution.py:510
  153.8 0.0 copy-start.1
  153.8 3.9 %shard_map.123 = bf16[32,128,256]{2,1,0:T(8,128)(2,1)} custom-call(bf16[32,128,256]{2,1,0:T(8,128)(2,1)} %bitcast.11.source_ref), custom_call_target="tpu_custom_call" | custom-call | bytes 4194304 | tf_op jit(solution)/shard_map/pallas_call | solution.py:432
  157.8 0.0 copy-done.1
  157.8 1.8 %shard_map.124 = bf16[32,128,256]{2,1,0:T(8,128)(2,1)} custom-call(bf16[64,72,256]{2,1,0:T(8,128)(2,1)S(1)} %copy-done.1), custom_call_target="tpu_custom_call" | custom-call | bytes 4718592 | tf_op jit(solution)/shard_map/pallas_call | solution.py:454
  159.6 7.6 %all-to-all-done.4 = bf16[128,8,256]{2,1,0:T(8,128)(2,1)S(1)} async-done(((bf16[128,8,256]{2,1,0:T(8,128)(2,1)}), bf16[128,8,256]{2,1,0:T(8,128)(2,1)S(1)}, u32[]{:S(2)}, u32[]{:S(2)}) %all-to-all-start.4) | async-done | bytes 524320 | tf_op jit(solution)/shard_map/all_to_all | solution.py:510
  167.2 0.1 convert_element_type.27
  167.3 0.8 slice_bitcast_fusion
  168.1 0.9 pad_maximum_fusion
  (2 shorter events, 0.0 us)
Async XLA Ops:
  0.6 40.6 %all-to-all-start = ((bf16[64,64,256]{2,1,0:T(8,128)(2,1)}), bf16[64,64,256]{2,1,0:T(8,128)(2,1)}, u32[]{:S(2)}, u32[]{:S(2)}) async-start(bf16[64,64,256]{2,1,0:T(8,128)(2,1)} %bitcast.25), calls=%async_computation | async-start | bytes 4194304 | tf_op jit(solution)/shard_map/all_to_all | solution.py:489
  41.2 6.2 %copy-start.2 = (bf16[256,1024]{1,0:T(8,128)(2,1)S(1)}, bf16[256,1024]{1,0:T(8,128)(2,1)}, u32[]{:S(2)}) copy-start(bf16[256,1024]{1,0:T(8,128)(2,1)} %wup_ref.1) | copy-start | bytes 1572868
  41.2 6.2 %copy-start.3 = (bf16[1024,256]{1,0:T(8,128)(2,1)S(1)}, bf16[1024,256]{1,0:T(8,128)(2,1)}, u32[]{:S(2)}) copy-start(bf16[1024,256]{1,0:T(8,128)(2,1)} %wdown_ref.1) | copy-start | bytes 1572868
  41.2 6.2 %copy-start.4 = (bf16[256,768]{1,0:T(8,128)(2,1)S(1)}, bf16[256,768]{1,0:T(8,128)(2,1)}, u32[]{:S(2)}) copy-start(bf16[256,768]{1,0:T(8,128)(2,1)} %wqkv_ref.3) | copy-start | bytes 1179652
  41.2 6.2 %copy-start.5 = (f32[8,64,64]{2,1,0:T(8,128)S(1)}, f32[8,64,64]{2,1,0:T(8,128)}, u32[]{:S(2)}) copy-start(f32[8,64,64]{2,1,0:T(8,128)} %pos_ref.1) | copy-start | bytes 393220
  41.2 6.2 %copy-start.6 = (bf16[256,256]{1,0:T(8,128)(2,1)S(1)}, bf16[256,256]{1,0:T(8,128)(2,1)}, u32[]{:S(2)}) copy-start(bf16[256,256]{1,0:T(8,128)(2,1)} %wout_ref.3) | copy-start | bytes 393220
  41.2 6.2 %copy-start.7 = (f32[256]{0:T(256)S(1)}, f32[256]{0:T(256)}, u32[]{:S(2)}) copy-start(f32[256]{0:T(256)} %param.15) | copy-start | bytes 3076
  41.2 6.2 %copy-start.8 = (f32[256]{0:T(256)S(1)}, f32[256]{0:T(256)}, u32[]{:S(2)}) copy-start(f32[256]{0:T(256)} %param.11) | copy-start | bytes 3076
  41.2 34.1 %all-to-all-start.1 = ((bf16[64,64,256]{2,1,0:T(8,128)(2,1)}), bf16[64,64,256]{2,1,0:T(8,128)(2,1)}, u32[]{:S(2)}, u32[]{:S(2)}) async-start(bf16[64,64,256]{2,1,0:T(8,128)(2,1)} %bitcast.3), calls=%async_computation.1 | async-start | bytes 4194304 | tf_op jit(solution)/shard_map/all_to_all | solution.py:489
  75.3 33.4 %all-to-all-start.2 = ((bf16[64,64,256]{2,1,0:T(8,128)(2,1)}), bf16[64,64,256]{2,1,0:T(8,128)(2,1)}, u32[]{:S(2)}, u32[]{:S(2)}) async-start(bf16[64,64,256]{2,1,0:T(8,128)(2,1)} %bitcast.10), calls=%async_computation.2 | async-start | bytes 4194304 | tf_op jit(solution)/shard_map/all_to_all | solution.py:489
  102.1 1.6 collective-permute-start
  146.9 1.4 copy-start
  149.2 18.0 %all-to-all-start.4 = ((bf16[128,8,256]{2,1,0:T(8,128)(2,1)}), bf16[128,8,256]{2,1,0:T(8,128)(2,1)S(1)}, u32[]{:S(2)}, u32[]{:S(2)}) async-start(bf16[128,8,256]{2,1,0:T(8,128)(2,1)} %broadcast_in_dim.2), calls=%async_computation.4 | async-start | bytes 1048576 | tf_op jit(solution)/shard_map/all_to_all | solution.py:510
  153.8 3.9 %copy-start.1 = (bf16[64,72,256]{2,1,0:T(8,128)(2,1)S(1)}, bf16[64,72,256]{2,1,0:T(8,128)(2,1)}, u32[]{:S(2)}) copy-start(bf16[64,72,256]{2,1,0:T(8,128)(2,1)} %copy-done) | copy-start | bytes 7077892

commit v6 on v5

--- a/solution.py
+++ b/solution.py
@@ -299,7 +299,7 @@
     @pl.when(turn == last)
     def _():
         count = own_ref.shape[0] // GRID
-        halved = acc_ref[...].reshape(GRID, CORES, count, channels).astype(jnp.bfloat16)
+        halved = acc_ref[...].reshape(GRID, CORES, count, channels)
         first, second = (halved[:, c].reshape(own_ref.shape) for c in range(CORES))
 
         @pl.when(core_ref[0] == 0)
@@ -401,8 +401,8 @@
         ],
         out_shape=[
             pltpu.VMEM(data.shape[:3] + (rows, channels), jnp.bfloat16),
-            jax.ShapeDtypeStruct(pieces, jnp.bfloat16),
-            jax.ShapeDtypeStruct(pieces, jnp.bfloat16),
+            jax.ShapeDtypeStruct(pieces, jnp.float32),
+            jax.ShapeDtypeStruct(pieces, jnp.float32),
         ],
         scratch_shapes=[pltpu.VMEM((4, channels, channels), jnp.float32)]
         + [pltpu.VMEM((halves, tokens, LANES), jnp.float32)] * 3
@@ -450,13 +450,13 @@
 def trimmed(values, shape):
     rows, columns, channels = shape
     devices, height, _ = values.shape
-    values = pltpu.with_memory_space_constraint(values, pltpu.VMEM)
     return pl.pallas_call(
         trim_kernel,
         grid=(4,),
         in_specs=[pl.BlockSpec((devices // 4, height, channels), lambda i: (i, 0, 0))],
         out_specs=pl.BlockSpec((rows // 4, columns, channels), lambda i: (i, 0, 0)),
         out_shape=jax.ShapeDtypeStruct(shape, values.dtype),
+        compiler_params=pltpu.CompilerParams(vmem_limit_bytes=16 * 1024 * 1024),
         cost_estimate=pl.CostEstimate(
             flops=0, bytes_accessed=4 * values.size, transcendentals=0
         ),
@@ -497,20 +497,18 @@
     grad, own_pieces, other_pieces = backward(
         core.reshape(1), data, cot, qkv, probs, context, gain1, w_qkv, w_out, width
     )
-    pair = own_pieces.astype(jnp.float32) + lax.ppermute(
-        other_pieces, AXES, partner
-    ).astype(jnp.float32)
+    pair = own_pieces + lax.ppermute(other_pieces, AXES, partner)
     pair = pair.astype(jnp.bfloat16).reshape(GRID, 1, GRID, -1, channels)
     grad = lax.dynamic_update_slice(grad, pair, (0, 0, 0, positions, 0))
     grad, mixed = lax.optimization_barrier((grad.reshape(MEMBERS, -1, channels), mixed))
     grad = exchange(grad)
     total = jnp.sum(grad[:, positions:].astype(jnp.float32), axis=0) * factor
     total = jnp.broadcast_to(total.astype(jnp.bfloat16)[None], (devices,) + total.shape)
-    total, grad = lax.optimization_barrier((total, grad))
     total = lax.all_to_all(total, AXES, 0, 0, tiled=True)
     blocks = total.astype(jnp.float32).reshape(4, channels, channels)
     grad_qkv = jnp.concatenate([blocks[0], blocks[1], blocks[2]], axis=1)
-    return (placed(mixed), trimmed(grad, tokens.shape), grad_qkv, blocks[3])
+    grad, mixed = lax.optimization_barrier((trimmed(grad, tokens.shape), mixed))
+    return (placed(mixed), grad, grad_qkv, blocks[3])
 
 
 def solution(mesh):

time: 170 us -> 170 us (level)
  no operation moved by 1% of the time
where the time goes in v6:
time: 170 us; the launch traced here: 169 us
  Pallas kernels  53.5 us (31%)
  waiting for transfers between devices  42.8 us (25%)
  blocking collectives  39.4 us (23%)
  starting transfers between devices  28.8 us (17%)
  local copies, waits for them, and re-layouts  2.4 us (1%)
    all_to_all x1, blocking collectives, exchange(): lax.all_to_all(pieces, AXES, 0, 0, axis_index_groups=peers, tiled=True)  39.4 us
    all_to_all x3, waiting for transfers between devices, exchange(): lax.all_to_all(pieces, AXES, 0, 0, axis_index_groups=peers, tiled=True)  33.2 us
    all_to_all x3, starting transfers between devices, exchange(): lax.all_to_all(pieces, AXES, 0, 0, axis_index_groups=peers, tiled=True)  24.1 us
    pallas_call x1, Pallas kernels, forward(): pl.pallas_call(functools.partial(forward_kernel, width), grid=grid, in_sp...  23.5 us
    pallas_call x1, Pallas kernels, backward(): pl.pallas_call(functools.partial(backward_kernel, width), grid=grid, in_s...  20.5 us
    all_to_all x1, waiting for transfers between devices, local(): total = lax.all_to_all(total, AXES, 0, 0, tiled=True)  7.76 us
    pallas_call x2, Pallas kernels, placed(): pl.pallas_call(place_kernel, grid=(4,), in_specs=[block], out_specs=block...  7.57 us
    all_to_all x1, starting transfers between devices, local(): total = lax.all_to_all(total, AXES, 0, 0, tiled=True)  4.64 us
  transfers between devices with their start and end apart: 5, of which 5 were waited for; matrix products, arithmetic and copies ran while one was open for 0% of the time, Pallas kernels for 32%

profile of v6, /device:TPU:0, one launch (start us, length us, event | category | flops | bytes accessed | tf_op | source)
XLA Modules:
  0.0 168.9 jit_solution(14123298333946592361)
XLA Ops:
  0.6 11.8 %all-to-all-start = ((bf16[64,64,256]{2,1,0:T(8,128)(2,1)}), bf16[64,64,256]{2,1,0:T(8,128)(2,1)}, u32[]{:S(2)}, u32[]{:S(2)}) async-start(bf16[64,64,256]{2,1,0:T(8,128)(2,1)} %bitcast.25), calls=%async_computation | async-start | bytes 4194304 | tf_op jit(solution)/shard_map/all_to_all | solution.py:489
  12.4 3.8 %shard_map.120 = bf16[32,128,256]{2,1,0:T(8,128)(2,1)} custom-call(bf16[32,128,256]{2,1,0:T(8,128)(2,1)} %source_ref.1), custom_call_target="tpu_custom_call" | custom-call | bytes 4194304 | tf_op jit(solution)/shard_map/pallas_call | solution.py:432
  16.2 25.0 %all-to-all-done = bf16[64,64,256]{2,1,0:T(8,128)(2,1)} async-done(((bf16[64,64,256]{2,1,0:T(8,128)(2,1)}), bf16[64,64,256]{2,1,0:T(8,128)(2,1)}, u32[]{:S(2)}, u32[]{:S(2)}) %all-to-all-start) | async-done | bytes 2097184 | tf_op jit(solution)/shard_map/all_to_all | solution.py:489
  41.2 0.0 copy-start.1
  41.2 0.0 copy-start.2
  41.2 0.0 copy-start.3
  41.2 0.0 copy-start.4
  41.2 0.0 copy-start.5
  41.2 0.0 copy-start.6
  41.2 0.0 copy-start.7
  41.2 6.1 %all-to-all-start.1 = ((bf16[64,64,256]{2,1,0:T(8,128)(2,1)}), bf16[64,64,256]{2,1,0:T(8,128)(2,1)}, u32[]{:S(2)}, u32[]{:S(2)}) async-start(bf16[64,64,256]{2,1,0:T(8,128)(2,1)} %bitcast.3), calls=%async_computation.1 | async-start | bytes 4194304 | tf_op jit(solution)/shard_map/all_to_all | solution.py:489
  47.4 0.0 copy-done.1
  47.4 0.0 copy-done.2
  47.4 0.0 copy-done.3
  47.4 0.0 copy-done.4
  47.4 0.0 copy-done.5
  47.4 0.0 copy-done.6
  47.5 0.0 copy-done.7
  47.5 23.5 %shard_map.121 = (bf16[8,1,8,64,256]{4,3,2,1,0:T(8,128)(2,1)}, bf16[4096,768]{1,0:T(8,128)(2,1)}, bf16[8192,256]{1,0:T(8,128)(2,1)}, bf16[4096,256]{1,0:T(8,128)(2,1)}) custom-call(bf16[8,1,8,64,256]{4,3,2,1,0:T(8,128)(2,1)} %bitcast.2.data_ref, f32[1,256]{1,0:T(1,128)S(1)} %bitcast.23, bf16[256,768]{1,0:T(8,128)(2,1)S(1)} %copy-done.3, ...), custom_call_target="tpu_custom_call" | custom-call | flops 12884901888 | bytes 16777216 | tf_op jit(solution)/shard_map/pallas_call | solution.py:341
  71.0 4.4 %all-to-all-done.1 = bf16[64,64,256]{2,1,0:T(8,128)(2,1)} async-done(((bf16[64,64,256]{2,1,0:T(8,128)(2,1)}), bf16[64,64,256]{2,1,0:T(8,128)(2,1)}, u32[]{:S(2)}, u32[]{:S(2)}) %all-to-all-start.1) | async-done | bytes 2097184 | tf_op jit(solution)/shard_map/all_to_all | solution.py:489
  75.3 6.2 %all-to-all-start.2 = ((bf16[64,64,256]{2,1,0:T(8,128)(2,1)}), bf16[64,64,256]{2,1,0:T(8,128)(2,1)}, u32[]{:S(2)}, u32[]{:S(2)}) async-start(bf16[64,64,256]{2,1,0:T(8,128)(2,1)} %bitcast.10), calls=%async_computation.2 | async-start | bytes 4194304 | tf_op jit(solution)/shard_map/all_to_all | solution.py:489
  81.6 20.5 %shard_map.122 = (bf16[8,1,8,72,256]{4,3,2,1,0:T(8,128)(2,1)S(1)}, f32[512,256]{1,0:T(8,128)S(1)}, f32[512,256]{1,0:T(8,128)S(1)}) custom-call(s32[1]{0:T(128)} %bitcast.core_ref, bf16[8,1,8,64,256]{4,3,2,1,0:T(8,128)(2,1)} %bitcast.2.data_ref, bf16[8,1,8,64,256]{4,3,2,1,0:T(8,128)(2,1)} %bitcast.4.cot_ref, bf16[4096,768]{1,0:T(8,128)(2,1)} %get-tuple-element.15.qkv_ref, ...), custom_call_target="tpu_custom_call" | custom-call | flops 12884901888 | bytes 20971520 | tf_op jit(solution)/shard_map/pallas_call | solution.py:385
  102.1 0.0 copy-start
  102.1 0.1 collective-permute-start
  102.2 1.9 %collective-permute-done = f32[512,256]{1,0:T(8,128)S(1)} collective-permute-done((f32[512,256]{1,0:T(8,128)S(1)}, f32[512,256]{1,0:T(8,128)S(1)}, u32[]{:S(2)}, u32[]{:S(2)}) %collective-permute-start) | collective-permute-done | bytes 524320 | tf_op jit(solution)/shard_map/ppermute | solution.py:500
  104.1 0.1 add_convert_fusion
  104.2 0.0 copy-done
  104.2 0.8 constant_dynamic-update-slice_fusion
  105.0 3.8 %all-to-all-done.2 = bf16[64,64,256]{2,1,0:T(8,128)(2,1)} async-done(((bf16[64,64,256]{2,1,0:T(8,128)(2,1)}), bf16[64,64,256]{2,1,0:T(8,128)(2,1)}, u32[]{:S(2)}, u32[]{:S(2)}) %all-to-all-start.2) | async-done | bytes 2097184 | tf_op jit(solution)/shard_map/all_to_all | solution.py:489
  108.8 39.4 %all_to_all.25.source_ref = bf16[64,72,256]{2,1,0:T(8,128)(2,1)S(1)} all-to-all(bf16[64,72,256]{2,1,0:T(8,128)(2,1)} %bitcast.21), channel_id=1, replica_groups={{0,1,2,3,4,5,6,7,16,17,18,19,20,21,22,23,32,33,34,35,36,37,38,39,48,49,..., dimensions={0} | all-to-all | bytes 4718592 | tf_op jit(solution)/shard_map/all_to_all | solution.py:489
  148.2 0.1 convert_reduce_fusion
  148.3 0.8 broadcast_in_dim.2
  149.1 4.6 %all-to-all-start.4 = ((bf16[128,8,256]{2,1,0:T(8,128)(2,1)}), bf16[128,8,256]{2,1,0:T(8,128)(2,1)S(1)}, u32[]{:S(2)}, u32[]{:S(2)}) async-start(bf16[128,8,256]{2,1,0:T(8,128)(2,1)} %broadcast_in_dim.2), calls=%async_computation.4 | async-start | bytes 1048576 | tf_op jit(solution)/shard_map/all_to_all | solution.py:507
  153.8 1.9 %shard_map.123 = bf16[32,128,256]{2,1,0:T(8,128)(2,1)} custom-call(bf16[64,72,256]{2,1,0:T(8,128)(2,1)S(1)} %all_to_all.25.source_ref), custom_call_target="tpu_custom_call" | custom-call | bytes 4718592 | tf_op jit(solution)/shard_map/pallas_call | solution.py:453
  155.6 3.8 %shard_map.124 = bf16[32,128,256]{2,1,0:T(8,128)(2,1)} custom-call(bf16[32,128,256]{2,1,0:T(8,128)(2,1)} %bitcast.11.source_ref), custom_call_target="tpu_custom_call" | custom-call | bytes 4194304 | tf_op jit(solution)/shard_map/pallas_call | solution.py:432
  159.4 7.8 %all-to-all-done.4 = bf16[128,8,256]{2,1,0:T(8,128)(2,1)S(1)} async-done(((bf16[128,8,256]{2,1,0:T(8,128)(2,1)}), bf16[128,8,256]{2,1,0:T(8,128)(2,1)S(1)}, u32[]{:S(2)}, u32[]{:S(2)}) %all-to-all-start.4) | async-done | bytes 524320 | tf_op jit(solution)/shard_map/all_to_all | solution.py:507
  167.2 0.1 convert_element_type.19
  167.2 0.8 slice_bitcast_fusion
  168.0 0.9 pad_maximum_fusion
  (1 shorter events, 0.0 us)
Async XLA Ops:
  0.6 40.6 %all-to-all-start = ((bf16[64,64,256]{2,1,0:T(8,128)(2,1)}), bf16[64,64,256]{2,1,0:T(8,128)(2,1)}, u32[]{:S(2)}, u32[]{:S(2)}) async-start(bf16[64,64,256]{2,1,0:T(8,128)(2,1)} %bitcast.25), calls=%async_computation | async-start | bytes 4194304 | tf_op jit(solution)/shard_map/all_to_all | solution.py:489
  41.2 6.2 %copy-start.1 = (bf16[256,1024]{1,0:T(8,128)(2,1)S(1)}, bf16[256,1024]{1,0:T(8,128)(2,1)}, u32[]{:S(2)}) copy-start(bf16[256,1024]{1,0:T(8,128)(2,1)} %wup_ref.1) | copy-start | bytes 1572868
  41.2 6.2 %copy-start.2 = (bf16[1024,256]{1,0:T(8,128)(2,1)S(1)}, bf16[1024,256]{1,0:T(8,128)(2,1)}, u32[]{:S(2)}) copy-start(bf16[1024,256]{1,0:T(8,128)(2,1)} %wdown_ref.1) | copy-start | bytes 1572868
  41.2 6.2 %copy-start.3 = (bf16[256,768]{1,0:T(8,128)(2,1)S(1)}, bf16[256,768]{1,0:T(8,128)(2,1)}, u32[]{:S(2)}) copy-start(bf16[256,768]{1,0:T(8,128)(2,1)} %wqkv_ref.3) | copy-start | bytes 1179652
  41.2 6.2 %copy-start.4 = (f32[8,64,64]{2,1,0:T(8,128)S(1)}, f32[8,64,64]{2,1,0:T(8,128)}, u32[]{:S(2)}) copy-start(f32[8,64,64]{2,1,0:T(8,128)} %pos_ref.1) | copy-start | bytes 393220
  41.2 6.2 %copy-start.5 = (bf16[256,256]{1,0:T(8,128)(2,1)S(1)}, bf16[256,256]{1,0:T(8,128)(2,1)}, u32[]{:S(2)}) copy-start(bf16[256,256]{1,0:T(8,128)(2,1)} %wout_ref.3) | copy-start | bytes 393220
  41.2 6.2 %copy-start.6 = (f32[256]{0:T(256)S(1)}, f32[256]{0:T(256)}, u32[]{:S(2)}) copy-start(f32[256]{0:T(256)} %param.15) | copy-start | bytes 3076
  41.2 6.2 %copy-start.7 = (f32[256]{0:T(256)S(1)}, f32[256]{0:T(256)}, u32[]{:S(2)}) copy-start(f32[256]{0:T(256)} %param.11) | copy-start | bytes 3076
  41.2 34.1 %all-to-all-start.1 = ((bf16[64,64,256]{2,1,0:T(8,128)(2,1)}), bf16[64,64,256]{2,1,0:T(8,128)(2,1)}, u32[]{:S(2)}, u32[]{:S(2)}) async-start(bf16[64,64,256]{2,1,0:T(8,128)(2,1)} %bitcast.3), calls=%async_computation.1 | async-start | bytes 4194304 | tf_op jit(solution)/shard_map/all_to_all | solution.py:489
  75.3 33.5 %all-to-all-start.2 = ((bf16[64,64,256]{2,1,0:T(8,128)(2,1)}), bf16[64,64,256]{2,1,0:T(8,128)(2,1)}, u32[]{:S(2)}, u32[]{:S(2)}) async-start(bf16[64,64,256]{2,1,0:T(8,128)(2,1)} %bitcast.10), calls=%async_computation.2 | async-start | bytes 4194304 | tf_op jit(solution)/shard_map/all_to_all | solution.py:489
  102.1 2.1 %copy-start = (bf16[8,1,8,72,256]{4,3,2,1,0:T(8,128)(2,1)}, bf16[8,1,8,72,256]{4,3,2,1,0:T(8,128)(2,1)S(1)}, u32[]{:S(2)}) copy-start(bf16[8,1,8,72,256]{4,3,2,1,0:T(8,128)(2,1)S(1)} %get-tuple-element.18) | copy-start | bytes 7077892
  102.1 2.0 %collective-permute-start = (f32[512,256]{1,0:T(8,128)S(1)}, f32[512,256]{1,0:T(8,128)S(1)}, u32[]{:S(2)}, u32[]{:S(2)}) collective-permute-start(f32[512,256]{1,0:T(8,128)S(1)} %get-tuple-element.20), channel_id=1, source_target_pairs={{0,8},{8,0},{1,9},{9,1},{2,10},{10,2},{3,11},{11,3},{4,12},{12,4},... | collective-permute-start | bytes 1572872 | tf_op jit(solution)/shard_map/ppermute | solution.py:500
  149.1 18.0 %all-to-all-start.4 = ((bf16[128,8,256]{2,1,0:T(8,128)(2,1)}), bf16[128,8,256]{2,1,0:T(8,128)(2,1)S(1)}, u32[]{:S(2)}, u32[]{:S(2)}) async-start(bf16[128,8,256]{2,1,0:T(8,128)(2,1)} %broadcast_in_dim.2), calls=%async_computation.4 | async-start | bytes 1048576 | tf_op jit(solution)/shard_map/all_to_all | solution.py:507

commit v7 on v6

--- a/solution.py
+++ b/solution.py
@@ -375,7 +375,7 @@
     tokens = MEMBERS * BLOCK
     count = groups * MEMBERS
     row_width = LANES // width * MEMBERS
-    rows = data.shape[3] + 4 * channels // (GRID * CORES * GRID)
+    rows = data.shape[3]
     pieces = (4 * channels // CORES, channels)
     qkv, probs, context = (
         pltpu.with_memory_space_constraint(a, pltpu.HBM) for a in (qkv, probs, context)
@@ -441,6 +441,34 @@
     )(values)
 
 
+def join_kernel(grad_ref, own_ref, other_ref, out_ref):
+    positions = grad_ref.shape[1]
+    pair = (own_ref[...] + other_ref[...]).astype(jnp.bfloat16)
+    out_ref[:, :positions, :] = grad_ref[...]
+    out_ref[:, positions:, :] = pair.reshape(out_ref.shape[0], -1, out_ref.shape[2])
+
+
+def joined(grad, own, other):
+    peers, positions, channels = grad.shape
+    height = positions + own.shape[0] // peers
+    piece = pl.BlockSpec((own.shape[0] // 4, channels), lambda i: (i, 0))
+    return pl.pallas_call(
+        join_kernel,
+        grid=(4,),
+        in_specs=[
+            pl.BlockSpec((peers // 4, positions, channels), lambda i: (i, 0, 0)),
+            piece,
+            piece,
+        ],
+        out_specs=pl.BlockSpec((peers // 4, height, channels), lambda i: (i, 0, 0)),
+        out_shape=pltpu.VMEM((peers, height, channels), grad.dtype),
+        compiler_params=pltpu.CompilerParams(vmem_limit_bytes=16 * 1024 * 1024),
+        cost_estimate=pl.CostEstimate(
+            flops=own.size, bytes_accessed=4 * grad.size, transcendentals=0
+        ),
+    )(grad, own, other)
+
+
 def trim_kernel(source_ref, out_ref):
     rows, columns, channels = out_ref.shape
     positions = rows * columns // source_ref.shape[0]
@@ -497,10 +525,9 @@
     grad, own_pieces, other_pieces = backward(
         core.reshape(1), data, cot, qkv, probs, context, gain1, w_qkv, w_out, width
     )
-    pair = own_pieces + lax.ppermute(other_pieces, AXES, partner)
-    pair = pair.astype(jnp.bfloat16).reshape(GRID, 1, GRID, -1, channels)
-    grad = lax.dynamic_update_slice(grad, pair, (0, 0, 0, positions, 0))
-    grad, mixed = lax.optimization_barrier((grad.reshape(MEMBERS, -1, channels), mixed))
+    other_pieces = lax.ppermute(other_pieces, AXES, partner)
+    grad = joined(grad.reshape(sent), own_pieces, other_pieces)
+    grad, mixed = lax.optimization_barrier((grad, mixed))
     grad = exchange(grad)
     total = jnp.sum(grad[:, positions:].astype(jnp.float32), axis=0) * factor
     total = jnp.broadcast_to(total.astype(jnp.bfloat16)[None], (devices,) + total.shape)

time: 170 us -> 171 us (level)
  no operation moved by 1% of the time
where the time goes in v7:
time: 171 us; the launch traced here: 170 us
  Pallas kernels  53.9 us (32%)
  waiting for transfers between devices  41.9 us (25%)
  blocking collectives  40.3 us (24%)
  starting transfers between devices  28.8 us (17%)
  local copies, waits for them, and re-layouts  3.06 us (2%)
    all_to_all x1, blocking collectives, exchange(): lax.all_to_all(pieces, AXES, 0, 0, axis_index_groups=peers, tiled=True)  40.3 us
    all_to_all x3, waiting for transfers between devices, exchange(): lax.all_to_all(pieces, AXES, 0, 0, axis_index_groups=peers, tiled=True)  32.2 us
    all_to_all x3, starting transfers between devices, exchange(): lax.all_to_all(pieces, AXES, 0, 0, axis_index_groups=peers, tiled=True)  24.1 us
    pallas_call x1, Pallas kernels, forward(): pl.pallas_call(functools.partial(forward_kernel, width), grid=grid, in_sp...  23.5 us
    pallas_call x1, Pallas kernels, backward(): pl.pallas_call(functools.partial(backward_kernel, width), grid=grid, in_s...  20.6 us
    all_to_all x1, waiting for transfers between devices, local(): total = lax.all_to_all(total, AXES, 0, 0, tiled=True)  7.76 us
    pallas_call x2, Pallas kernels, placed(): pl.pallas_call(place_kernel, grid=(4,), in_specs=[block], out_specs=block...  7.6 us
    all_to_all x1, starting transfers between devices, local(): total = lax.all_to_all(total, AXES, 0, 0, tiled=True)  4.64 us
  transfers between devices with their start and end apart: 5, of which 5 were waited for; matrix products, arithmetic and copies ran while one was open for 0% of the time, Pallas kernels for 32%

profile of v7, /device:TPU:0, one launch (start us, length us, event | category | flops | bytes accessed | tf_op | source)
XLA Modules:
  0.0 169.8 jit_solution(10319770080316881124)
XLA Ops:
  0.6 11.8 %all-to-all-start = ((bf16[64,64,256]{2,1,0:T(8,128)(2,1)}), bf16[64,64,256]{2,1,0:T(8,128)(2,1)}, u32[]{:S(2)}, u32[]{:S(2)}) async-start(bf16[64,64,256]{2,1,0:T(8,128)(2,1)} %bitcast.22), calls=%async_computation | async-start | bytes 4194304 | tf_op jit(solution)/shard_map/all_to_all | solution.py:517
  12.4 3.8 %shard_map.120 = bf16[32,128,256]{2,1,0:T(8,128)(2,1)} custom-call(bf16[32,128,256]{2,1,0:T(8,128)(2,1)} %source_ref.1), custom_call_target="tpu_custom_call" | custom-call | bytes 4194304 | tf_op jit(solution)/shard_map/pallas_call | solution.py:432
  16.2 24.9 %all-to-all-done = bf16[64,64,256]{2,1,0:T(8,128)(2,1)} async-done(((bf16[64,64,256]{2,1,0:T(8,128)(2,1)}), bf16[64,64,256]{2,1,0:T(8,128)(2,1)}, u32[]{:S(2)}, u32[]{:S(2)}) %all-to-all-start) | async-done | bytes 2097184 | tf_op jit(solution)/shard_map/all_to_all | solution.py:517
  41.2 0.0 copy-start.1
  41.2 0.0 copy-start.2
  41.2 0.0 copy-start.3
  41.2 0.0 copy-start.4
  41.2 0.0 copy-start.5
  41.2 0.0 copy-start.6
  41.2 0.0 copy-start.7
  41.2 6.1 %all-to-all-start.1 = ((bf16[64,64,256]{2,1,0:T(8,128)(2,1)}), bf16[64,64,256]{2,1,0:T(8,128)(2,1)}, u32[]{:S(2)}, u32[]{:S(2)}) async-start(bf16[64,64,256]{2,1,0:T(8,128)(2,1)} %bitcast.3), calls=%async_computation.1 | async-start | bytes 4194304 | tf_op jit(solution)/shard_map/all_to_all | solution.py:517
  47.4 0.0 copy-done.1
  47.4 0.0 copy-done.2
  47.4 0.0 copy-done.3
  47.4 0.0 copy-done.4
  47.4 0.0 copy-done.5
  47.4 0.0 copy-done.6
  47.4 0.0 copy-done.7
  47.4 23.5 %shard_map.121 = (bf16[8,1,8,64,256]{4,3,2,1,0:T(8,128)(2,1)}, bf16[4096,768]{1,0:T(8,128)(2,1)}, bf16[8192,256]{1,0:T(8,128)(2,1)}, bf16[4096,256]{1,0:T(8,128)(2,1)}) custom-call(bf16[8,1,8,64,256]{4,3,2,1,0:T(8,128)(2,1)} %bitcast.2.data_ref, f32[1,256]{1,0:T(1,128)S(1)} %bitcast.20, bf16[256,768]{1,0:T(8,128)(2,1)S(1)} %copy-done.3, ...), custom_call_target="tpu_custom_call" | custom-call | flops 12884901888 | bytes 16777216 | tf_op jit(solution)/shard_map/pallas_call | solution.py:341
  71.0 4.4 %all-to-all-done.1 = bf16[64,64,256]{2,1,0:T(8,128)(2,1)} async-done(((bf16[64,64,256]{2,1,0:T(8,128)(2,1)}), bf16[64,64,256]{2,1,0:T(8,128)(2,1)}, u32[]{:S(2)}, u32[]{:S(2)}) %all-to-all-start.1) | async-done | bytes 2097184 | tf_op jit(solution)/shard_map/all_to_all | solution.py:517
  75.3 6.2 %all-to-all-start.2 = ((bf16[64,64,256]{2,1,0:T(8,128)(2,1)}), bf16[64,64,256]{2,1,0:T(8,128)(2,1)}, u32[]{:S(2)}, u32[]{:S(2)}) async-start(bf16[64,64,256]{2,1,0:T(8,128)(2,1)} %bitcast.8), calls=%async_computation.2 | async-start | bytes 4194304 | tf_op jit(solution)/shard_map/all_to_all | solution.py:517
  81.6 20.6 %shard_map.122 = (bf16[8,1,8,64,256]{4,3,2,1,0:T(8,128)(2,1)S(1)}, f32[512,256]{1,0:T(8,128)S(1)}, f32[512,256]{1,0:T(8,128)S(1)}) custom-call(s32[1]{0:T(128)} %bitcast.core_ref, bf16[8,1,8,64,256]{4,3,2,1,0:T(8,128)(2,1)} %bitcast.2.data_ref, bf16[8,1,8,64,256]{4,3,2,1,0:T(8,128)(2,1)} %bitcast.4.cot_ref, bf16[4096,768]{1,0:T(8,128)(2,1)} %get-tuple-element.15.qkv_ref, ...), custom_call_target="tpu_custom_call" | custom-call | flops 12884901888 | bytes 20971520 | tf_op jit(solution)/shard_map/pallas_call | solution.py:385
  102.2 0.1 collective-permute-start
  102.3 1.9 %collective-permute-done.other_ref = f32[512,256]{1,0:T(8,128)S(1)} collective-permute-done((f32[512,256]{1,0:T(8,128)S(1)}, f32[512,256]{1,0:T(8,128)S(1)}, u32[]{:S(2)}, u32[]{:S(2)}) %collective-permute-start) | collective-permute-done | bytes 524320 | tf_op jit(solution)/shard_map/ppermute | solution.py:528
  104.2 0.2 shard_map.123
  104.5 0.0 copy-start
  104.5 1.4 copy-done
  105.9 2.9 %all-to-all-done.2 = bf16[64,64,256]{2,1,0:T(8,128)(2,1)} async-done(((bf16[64,64,256]{2,1,0:T(8,128)(2,1)}), bf16[64,64,256]{2,1,0:T(8,128)(2,1)}, u32[]{:S(2)}, u32[]{:S(2)}) %all-to-all-start.2) | async-done | bytes 2097184 | tf_op jit(solution)/shard_map/all_to_all | solution.py:517
  108.8 40.3 %all_to_all.25.source_ref = bf16[64,72,256]{2,1,0:T(8,128)(2,1)S(1)} all-to-all(bf16[64,72,256]{2,1,0:T(8,128)(2,1)} %copy-done), channel_id=1, replica_groups={{0,1,2,3,4,5,6,7,16,17,18,19,20,21,22,23,32,33,34,35,36,37,38,39,48,49,..., dimensions={0} | all-to-all | bytes 4718592 | tf_op jit(solution)/shard_map/all_to_all | solution.py:517
  149.1 0.1 convert_reduce_fusion
  149.2 0.8 broadcast_in_dim.2
  150.0 4.6 %all-to-all-start.4 = ((bf16[128,8,256]{2,1,0:T(8,128)(2,1)}), bf16[128,8,256]{2,1,0:T(8,128)(2,1)S(1)}, u32[]{:S(2)}, u32[]{:S(2)}) async-start(bf16[128,8,256]{2,1,0:T(8,128)(2,1)} %broadcast_in_dim.2), calls=%async_computation.4 | async-start | bytes 1048576 | tf_op jit(solution)/shard_map/all_to_all | solution.py:534
  154.7 1.9 %shard_map.124 = bf16[32,128,256]{2,1,0:T(8,128)(2,1)} custom-call(bf16[64,72,256]{2,1,0:T(8,128)(2,1)S(1)} %all_to_all.25.source_ref), custom_call_target="tpu_custom_call" | custom-call | bytes 4718592 | tf_op jit(solution)/shard_map/pallas_call | solution.py:481
  156.5 3.8 %shard_map.125 = bf16[32,128,256]{2,1,0:T(8,128)(2,1)} custom-call(bf16[32,128,256]{2,1,0:T(8,128)(2,1)} %bitcast.9.source_ref), custom_call_target="tpu_custom_call" | custom-call | bytes 4194304 | tf_op jit(solution)/shard_map/pallas_call | solution.py:432
  160.3 7.8 %all-to-all-done.4 = bf16[128,8,256]{2,1,0:T(8,128)(2,1)S(1)} async-done(((bf16[128,8,256]{2,1,0:T(8,128)(2,1)}), bf16[128,8,256]{2,1,0:T(8,128)(2,1)S(1)}, u32[]{:S(2)}, u32[]{:S(2)}) %all-to-all-start.4) | async-done | bytes 524320 | tf_op jit(solution)/shard_map/all_to_all | solution.py:534
  168.1 0.1 convert_element_type.15
  168.1 0.8 slice_bitcast_fusion
  168.9 0.9 pad_maximum_fusion
  (1 shorter events, 0.0 us)
Async XLA Ops:
  0.6 40.6 %all-to-all-start = ((bf16[64,64,256]{2,1,0:T(8,128)(2,1)}), bf16[64,64,256]{2,1,0:T(8,128)(2,1)}, u32[]{:S(2)}, u32[]{:S(2)}) async-start(bf16[64,64,256]{2,1,0:T(8,128)(2,1)} %bitcast.22), calls=%async_computation | async-start | bytes 4194304 | tf_op jit(solution)/shard_map/all_to_all | solution.py:517
  41.2 6.2 %copy-start.1 = (bf16[256,1024]{1,0:T(8,128)(2,1)S(1)}, bf16[256,1024]{1,0:T(8,128)(2,1)}, u32[]{:S(2)}) copy-start(bf16[256,1024]{1,0:T(8,128)(2,1)} %wup_ref.1) | copy-start | bytes 1572868
  41.2 6.2 %copy-start.2 = (bf16[1024,256]{1,0:T(8,128)(2,1)S(1)}, bf16[1024,256]{1,0:T(8,128)(2,1)}, u32[]{:S(2)}) copy-start(bf16[1024,256]{1,0:T(8,128)(2,1)} %wdown_ref.1) | copy-start | bytes 1572868
  41.2 6.2 %copy-start.3 = (bf16[256,768]{1,0:T(8,128)(2,1)S(1)}, bf16[256,768]{1,0:T(8,128)(2,1)}, u32[]{:S(2)}) copy-start(bf16[256,768]{1,0:T(8,128)(2,1)} %wqkv_ref.3) | copy-start | bytes 1179652
  41.2 6.2 %copy-start.4 = (f32[8,64,64]{2,1,0:T(8,128)S(1)}, f32[8,64,64]{2,1,0:T(8,128)}, u32[]{:S(2)}) copy-start(f32[8,64,64]{2,1,0:T(8,128)} %pos_ref.1) | copy-start | bytes 393220
  41.2 6.2 %copy-start.5 = (bf16[256,256]{1,0:T(8,128)(2,1)S(1)}, bf16[256,256]{1,0:T(8,128)(2,1)}, u32[]{:S(2)}) copy-start(bf16[256,256]{1,0:T(8,128)(2,1)} %wout_ref.3) | copy-start | bytes 393220
  41.2 6.2 %copy-start.6 = (f32[256]{0:T(256)S(1)}, f32[256]{0:T(256)}, u32[]{:S(2)}) copy-start(f32[256]{0:T(256)} %param.15) | copy-start | bytes 3076
  41.2 6.2 %copy-start.7 = (f32[256]{0:T(256)S(1)}, f32[256]{0:T(256)}, u32[]{:S(2)}) copy-start(f32[256]{0:T(256)} %param.11) | copy-start | bytes 3076
  41.2 34.1 %all-to-all-start.1 = ((bf16[64,64,256]{2,1,0:T(8,128)(2,1)}), bf16[64,64,256]{2,1,0:T(8,128)(2,1)}, u32[]{:S(2)}, u32[]{:S(2)}) async-start(bf16[64,64,256]{2,1,0:T(8,128)(2,1)} %bitcast.3), calls=%async_computation.1 | async-start | bytes 4194304 | tf_op jit(solution)/shard_map/all_to_all | solution.py:517
  75.3 33.4 %all-to-all-start.2 = ((bf16[64,64,256]{2,1,0:T(8,128)(2,1)}), bf16[64,64,256]{2,1,0:T(8,128)(2,1)}, u32[]{:S(2)}, u32[]{:S(2)}) async-start(bf16[64,64,256]{2,1,0:T(8,128)(2,1)} %bitcast.8), calls=%async_computation.2 | async-start | bytes 4194304 | tf_op jit(solution)/shard_map/all_to_all | solution.py:517
  102.2 2.0 %collective-permute-start = (f32[512,256]{1,0:T(8,128)S(1)}, f32[512,256]{1,0:T(8,128)S(1)}, u32[]{:S(2)}, u32[]{:S(2)}) collective-permute-start(f32[512,256]{1,0:T(8,128)S(1)} %get-tuple-element.20), channel_id=1, source_target_pairs={{0,8},{8,0},{1,9},{9,1},{2,10},{10,2},{3,11},{11,3},{4,12},{12,4},... | collective-permute-start | bytes 1572872 | tf_op jit(solution)/shard_map/ppermute | solution.py:528
  104.5 1.4 copy-start
  150.0 18.0 %all-to-all-start.4 = ((bf16[128,8,256]{2,1,0:T(8,128)(2,1)}), bf16[128,8,256]{2,1,0:T(8,128)(2,1)S(1)}, u32[]{:S(2)}, u32[]{:S(2)}) async-start(bf16[128,8,256]{2,1,0:T(8,128)(2,1)} %broadcast_in_dim.2), calls=%async_computation.4 | async-start | bytes 1048576 | tf_op jit(solution)/shard_map/all_to_all | solution.py:534
